TPU v7x, 512 devices: a whole 4x4x16 slice. The times are simulated.
512 devices in a mesh: ctx: 64 (over z, x), head: 8 (over y, core).
Axes of the slice: x: 4, y: 4, z: 16, core: 2. Of those that a mesh axis runs over, the one named last changes fastest.
Arguments:
- queries: bfloat16 [8192, 128, 192], P('ctx', 'head')
- up_weight: bfloat16 [128, 128, 512], P('head'), may hold values from -0.5 to 0.5
- index_query: bfloat16 [8192, 64, 128], P(('ctx', 'head'))
- index_weight: float32 [8192, 64], P(('ctx', 'head')), may hold values from -3 to 3
- cache_entry: bfloat16 [8, 64, 64, 576], P(None, 'ctx'), may hold values from -6 to 6
- index_key: bfloat16 [8, 64, 64, 128], P(None, 'ctx'), may hold values from -6 to 6
- block_position: int32 [128], P('ctx'), may hold values from 384 to 511, as said below
- picked_blocks: int32 [128, 32], P('ctx'), may hold values from 0 to 511, as said below
Outputs:
- key_grad: float32 [8, 64, 64, 128], P(None, 'ctx')
- weight_grad: float32 [8192, 64], P(('ctx', 'head'))
Inputs may be any that keep to these rules, and one draw needn't show every extreme that they name: `block_position`: every block of the last 128 context blocks is named exactly once. `picked_blocks`: each row names 32 distinct blocks, none after the row's own block_position, and always that block itself; block 0 too, unless the own block lies on shard 0. Taking block b to lie on shard b modulo 512 / 8, a row names exactly 1 block on each of 32 distinct shards, so the 2 rows of one shard name at most 2 blocks on one shard, and shard 0 receives that many from every shard.
All inputs are finite; a program needn't handle non-finite values.
Results may differ from a plain program's by a relative error of at most 0.003.
Values may be sent and summed in bfloat16 or wider, within the bound.
A program may use at most 128 MiB of HBM per device.

v0:
```python
import jax
import jax.numpy as jnp
from jax import lax
from jax.sharding import PartitionSpec as P


def pick_layout(picked, owners):
    top_count = picked.shape[1]
    owner_of = picked % owners
    same_owner = owner_of[:, :, None] == owner_of[:, None, :]
    earlier = jnp.arange(top_count)[None, :] < jnp.arange(top_count)[:, None]
    owner_rank = jnp.sum((same_owner & earlier[None]).astype(jnp.int32), axis=2)
    return (owner_of, owner_rank)


def request_table(picked, owner_of, owner_rank, owners, per_owner):
    query_count = picked.shape[0]
    matched = (owner_of[:, :, None, None] == jnp.arange(owners)[None, None, :, None]) & (
        owner_rank[:, :, None, None] == jnp.arange(per_owner)[None, None, None, :]
    )
    block_ids = jnp.sum(jnp.where(matched, picked[:, :, None, None] + 1, 0), axis=1) - 1
    return jnp.transpose(block_ids, (1, 0, 2)).reshape(owners, query_count * per_owner)


def masked_softmax(values, allowed):
    shifted = jnp.where(allowed, values, -jnp.inf)
    row_max = jnp.max(shifted, axis=-1, keepdims=True)
    expo = jnp.exp(shifted - row_max)
    return expo / jnp.sum(expo, axis=-1, keepdims=True)


def local(
    queries,
    up_weight,
    index_query,
    index_weight,
    cache_entry,
    index_key,
    block_position,
    picked_blocks,
):
    owners = lax.axis_size("ctx")
    heads_axis = lax.axis_size("head")
    head_id = lax.axis_index("head")
    query_count, top_count = picked_blocks.shape
    block_len = cache_entry.shape[2]
    key_width = cache_entry.shape[3]
    index_width = index_key.shape[3]
    own_blocks = cache_entry.shape[0]
    per_owner = max(1, top_count // owners)
    slot_count = query_count * per_owner
    key_count = top_count * block_len
    owner_of, owner_rank = pick_layout(picked_blocks, owners)
    request_ids = request_table(picked_blocks, owner_of, owner_rank, owners, per_owner)
    wanted = lax.all_to_all(request_ids, "ctx", split_axis=0, concat_axis=0, tiled=True)
    present = wanted >= 0
    local_rows = jnp.where(present, wanted // owners, 0)
    own_entries = cache_entry[:, 0]
    own_keys = index_key[:, 0]
    entry_rows = jnp.where(
        present[:, :, None, None], own_entries[local_rows], jnp.zeros((), own_entries.dtype)
    )
    key_rows = jnp.where(
        present[:, :, None, None], own_keys[local_rows], jnp.zeros((), own_keys.dtype)
    )
    fetched, fetched_keys = (
        lax.all_to_all(entry_rows, "ctx", split_axis=0, concat_axis=0, tiled=True),
        lax.all_to_all(key_rows, "ctx", split_axis=0, concat_axis=0, tiled=True),
    )
    flat_entries = fetched.reshape(owners * slot_count, block_len, key_width)
    flat_keys = fetched_keys.reshape(owners * slot_count, block_len, index_width)
    slot_table = owner_of * slot_count + jnp.arange(query_count)[:, None] * per_owner + owner_rank
    local_heads = queries.shape[1]
    nope_width = up_weight.shape[1]
    query_latent = jnp.einsum(
        "thd,hdc->thc", queries[:, :, :nope_width], up_weight, preferred_element_type=jnp.float32
    ).astype(jnp.bfloat16)
    query_full = jnp.concatenate([query_latent, queries[:, :, nope_width:]], axis=2)
    query_full = query_full.reshape(query_count, block_len, local_heads, key_width)
    score_scale = queries.shape[2] ** (-0.5)
    group_size = min(local_heads, 8)

    def attend_block(pieces):
        query_block, slot_row, pick_row, position = pieces
        block_keys = flat_entries[slot_row].reshape(key_count, key_width)
        key_place = (pick_row[:, None] * block_len + jnp.arange(block_len)[None, :]).reshape(
            key_count
        )
        query_place = position * block_len + jnp.arange(block_len)
        allowed = key_place[None, :] <= query_place[:, None]
        grouped = query_block.reshape(
            block_len, local_heads // group_size, group_size, key_width
        ).transpose(1, 2, 0, 3)

        def head_group(running, query_group):
            logits = (
                jnp.einsum(
                    "gic,sc->gis", query_group, block_keys, preferred_element_type=jnp.float32
                )
                * score_scale
            )
            probability = masked_softmax(logits, allowed[None])
            return (running + jnp.sum(probability, axis=0), None)

        running, unused = lax.scan(
            head_group, jnp.zeros((block_len, key_count), jnp.float32), grouped
        )
        return running

    prob_sum = lax.map(attend_block, (query_full, slot_table, picked_blocks, block_position))
    my_target = lax.psum_scatter(
        prob_sum.reshape(query_count * block_len, key_count),
        "head",
        scatter_dimension=0,
        tiled=True,
    )
    my_target = my_target / (local_heads * heads_axis)
    my_rows = my_target.shape[0]
    my_blocks = max(1, my_rows // block_len)
    first_block = head_id * my_rows // block_len
    my_slots = lax.dynamic_slice_in_dim(slot_table, first_block, my_blocks, 0)
    my_picks = lax.dynamic_slice_in_dim(picked_blocks, first_block, my_blocks, 0)
    my_places = lax.dynamic_slice_in_dim(block_position, first_block, my_blocks, 0)
    my_owner = lax.dynamic_slice_in_dim(owner_of, first_block, my_blocks, 0)
    my_rank = lax.dynamic_slice_in_dim(owner_rank, first_block, my_blocks, 0)
    my_keys = flat_keys[my_slots].reshape(my_blocks, key_count, index_width)
    index_heads = index_query.shape[1]
    row_group = min(my_rows, 8, block_len)
    group_count = my_rows // row_group
    grouped_query = index_query.reshape(group_count, row_group, index_heads, index_width)
    grouped_weight = index_weight.reshape(group_count, row_group, index_heads)
    grouped_target = my_target.reshape(group_count, row_group, key_count)
    index_scale = index_width ** (-0.5)

    def index_group(grad_keys, pieces):
        query_group, weight_group, target_group, group_id = pieces
        first_row = head_id * my_rows + group_id * row_group
        local_block = first_row // block_len - first_block
        keys_group = lax.dynamic_index_in_dim(my_keys, local_block, 0, keepdims=False)
        pick_row = lax.dynamic_index_in_dim(my_picks, local_block, 0, keepdims=False)
        position = lax.dynamic_index_in_dim(my_places, local_block, 0, keepdims=False)
        key_place = (pick_row[:, None] * block_len + jnp.arange(block_len)[None, :]).reshape(
            key_count
        )
        query_place = position * block_len + first_row % block_len + jnp.arange(row_group)
        allowed = key_place[None, :] <= query_place[:, None]
        raw_dot = jnp.einsum(
            "ijd,sd->ijs", query_group, keys_group, preferred_element_type=jnp.float32
        )
        activated = jnp.maximum(raw_dot, 0.0) * index_scale
        index_score = jnp.sum(weight_group[:, :, None] * activated, axis=1)
        index_soft = masked_softmax(index_score, allowed)
        score_grad = jnp.where(allowed, index_soft - target_group, 0.0)
        weight_part = jnp.sum(score_grad[:, None, :] * activated, axis=2)
        coefficient = jnp.where(
            raw_dot > 0, score_grad[:, None, :] * weight_group[:, :, None] * index_scale, 0.0
        ).astype(jnp.bfloat16)
        key_part = jnp.einsum(
            "ijs,ijd->sd", coefficient, query_group, preferred_element_type=jnp.float32
        )
        grad_keys = grad_keys.at[local_block].add(key_part)
        return (grad_keys, weight_part)

    zero_keys = jnp.zeros((my_blocks, key_count, index_width), jnp.float32)
    grad_keys, weight_parts = lax.scan(
        index_group,
        zero_keys,
        (grouped_query, grouped_weight, grouped_target, jnp.arange(group_count)),
    )
    weight_grad = weight_parts.reshape(my_rows, index_heads)
    return_slot = (
        my_owner * (my_blocks * per_owner) + jnp.arange(my_blocks)[:, None] * per_owner + my_rank
    )
    outgoing = jnp.zeros((owners * my_blocks * per_owner, block_len, index_width), jnp.float32)
    outgoing = outgoing.at[return_slot.reshape(-1)].set(
        grad_keys.reshape(my_blocks * top_count, block_len, index_width)
    )
    outgoing = outgoing.reshape(owners, my_blocks * per_owner, block_len, index_width)
    arrived = lax.all_to_all(outgoing, "ctx", split_axis=0, concat_axis=0, tiled=True)
    their_ids = lax.dynamic_slice_in_dim(
        wanted, first_block * per_owner, my_blocks * per_owner, 1
    ).reshape(-1)
    local_ids = jnp.where(their_ids >= 0, their_ids // owners, -1)
    one_hot = (local_ids[:, None] == jnp.arange(own_blocks)[None, :]).astype(jnp.float32)
    summed = jnp.einsum(
        "nr,nf->rf",
        one_hot,
        arrived.reshape(owners * my_blocks * per_owner, block_len * index_width),
        precision=lax.Precision.HIGHEST,
    )
    owner_total = lax.psum(summed, "head")
    key_grad = owner_total.reshape(own_blocks, 1, block_len, index_width)
    return (key_grad, weight_grad)


def solution(mesh):
    return jax.shard_map(
        local,
        mesh=mesh,
        in_specs=(
            P("ctx", "head", None),
            P("head", None, None),
            P(("ctx", "head"), None, None),
            P(("ctx", "head"), None),
            P(None, "ctx", None, None),
            P(None, "ctx", None, None),
            P("ctx"),
            P("ctx", None),
        ),
        out_specs=(P(None, "ctx", None, None), P(("ctx", "head"), None)),
        check_vma=False,
    )
```

profile of v0, /device:TPU:1, one launch (start us, length us, event | category | flops | bytes accessed | tf_op | source)
XLA Modules:
  0.0 882.1 jit_solution(11494966983540921087)
XLA Ops:
  8.4 32.4 %all_to_all.27 = s32[64,1,2]{2,1,0:T(1,128)S(1)} all-to-all(s32[64,1,2]{2,1,0:T(1,128)S(1)} %copy.64), channel_id=1, replica_groups=mesh['ctx'=64,'head'=8] {'ctx'}, dimensions={0} | all-to-all | bytes 1024 | tf_op jit(solution)/shard_map/all_to_all | solution.py:55
  41.7 8.4 gather_fusion.3
  50.1 10.0 %broadcast_select_fusion = bf16[64,2,64,576]{3,2,1,0:T(8,128)(2,1)} fusion(bf16[64,2,64,576]{3,2,1,0:T(8,128)(2,1)} %bitcast.177, pred[64,2]{1,0:T(8,128)(4,1)S(1)} %copy.66), kind=kLoop, calls=%fused_computation.77 | loop fusion | flops 4718592 | bytes 18874496 | tf_op jit(solution)/shard_map/jit(_where)/select_n | solution.py:60
  78.9 436.5 %all-to-all-done.2 = bf16[64,2,64,576]{3,2,1,0:T(8,128)(2,1)} async-done(((bf16[64,2,64,576]{3,2,1,0:T(8,128)(2,1)}), bf16[64,2,64,576]{3,2,1,0:T(8,128)(2,1)}, u32[]{:S(2)}, u32[]{:S(2)}) %all-to-all-start.2) | async-done | bytes 9437216 | tf_op jit(solution)/shard_map/all_to_all | solution.py:67
  515.4 15.7 %all-to-all-start.1 = ((bf16[64,2,64,128]{3,2,1,0:T(8,128)(2,1)}), bf16[64,2,64,128]{3,2,1,0:T(8,128)(2,1)}, u32[]{:S(2)}, u32[]{:S(2)}) async-start(bf16[64,2,64,128]{3,2,1,0:T(8,128)(2,1)} %broadcast_select_fusion.1), calls=%async_computation.1 | async-start | bytes 4194304 | tf_op jit(solution)/shard_map/all_to_all | solution.py:68
  531.4 80.5 %while.38 = (s32[]{:T(128)}, f32[2,64,2048]{2,1,0:T(8,128)}, bf16[2,64,16,576]{3,2,1,0:T(8,128)(2,1)}, s32[2,32]{1,0:T(2,128)S(1)}, bf16[128,64,576]{2,1,0:T(8,1...) while((s32[]{:T(128)}, f32[2,64,2048]{2,1,0:T(8,128)}, ...), condition=%wide.region_8.9_spmd, body=%wide.region_2.8_spmd.sunk | while | flops 2424580864 | bytes 32151756 | solution.py:110
  531.5 6.4 gather_fusion
  545.4 25.5 %while.40 = (s32[]{:T(128)}, f32[64,2048]{1,0:T(8,128)S(1)}, bf16[2,8,64,576]{3,2,1,0:T(8,128)(2,1)S(1)}, bf16[2048,576]{0,1:T(8,128)(2,1)}, s32[64]{0:T(128)S(1)}, /*index=5*/s32[2048]{0:T(1024)S(1)}, s32[]{:T(128)}, s32[]{:T(128)}) while((s32[]{:T(128)}, f32[64,2048]{1,0:T(8,128)S(1)}, bf16[2,8,64,576]{3,2,1,0:T(8,128)(2,1)S(1)}, ...), condition=%wide.region_7.7_spmd.clone, body=%wide.region_3.6_spmd.clone.sunk | while | flops 2424577536 | bytes 16916840 | solution.py:105
  545.5 6.4 fusion.102
  552.0 6.0 divide_reduce_fusion.2
  558.3 6.4 fusion.102
  564.7 6.0 divide_reduce_fusion.2
  571.7 6.4 gather_fusion
  585.6 25.5 %while.40 = (s32[]{:T(128)}, f32[64,2048]{1,0:T(8,128)S(1)}, bf16[2,8,64,576]{3,2,1,0:T(8,128)(2,1)S(1)}, bf16[2048,576]{0,1:T(8,128)(2,1)}, s32[64]{0:T(128)S(1)}, /*index=5*/s32[2048]{0:T(1024)S(1)}, s32[]{:T(128)}, s32[]{:T(128)}) while((s32[]{:T(128)}, f32[64,2048]{1,0:T(8,128)S(1)}, bf16[2,8,64,576]{3,2,1,0:T(8,128)(2,1)S(1)}, ...), condition=%wide.region_7.7_spmd.clone, body=%wide.region_3.6_spmd.clone.sunk | while | flops 2424577536 | bytes 16916840 | solution.py:105
  585.7 6.4 fusion.102
  592.2 6.0 divide_reduce_fusion.2
  598.5 6.4 fusion.102
  604.9 6.0 divide_reduce_fusion.2
  613.4 12.3 %all-to-all-done.1 = bf16[64,2,64,128]{3,2,1,0:T(8,128)(2,1)} async-done(((bf16[64,2,64,128]{3,2,1,0:T(8,128)(2,1)}), bf16[64,2,64,128]{3,2,1,0:T(8,128)(2,1)}, u32[]{:S(2)}, u32[]{:S(2)}) %all-to-all-start.1) | async-done | bytes 2097184 | tf_op jit(solution)/shard_map/all_to_all | solution.py:68
  628.0 23.7 %reduce-scatter.2.cloned.1.call-done = f32[16,2048]{1,0:T(8,128)} async-done(((f32[128,2048]{1,0:T(8,128)}), f32[16,2048]{1,0:T(8,128)}) %reduce-scatter.2.cloned.1.call-update) | async-done | bytes 131088 | tf_op jit(solution)/shard_map/reduce_scatter | solution.py:111
  652.6 28.6 %while.39 = (s32[]{:T(128)}, f32[1,2048,128]{2,1,0:T(8,128)}, f32[2,8,64]{2,1,0:T(8,128)S(1)}, s32[2]{0:T(128)S(1)}, s32[]{:T(128)}, /*index=5*/s32[]{:T(128)}, ...) while((s32[]{:T(128)}, f32[1,2048,128]{2,1,0:T(8,128)}, ...), condition=%wide.region_16.17_spmd.clone, body=%wide.region_10.16_spmd.clone.sunk | while | flops 557664320 | bytes 16393370 | solution.py:165
  688.2 14.6 %all-to-all-start.3 = ((f32[64,1,64,128]{3,2,1,0:T(8,128)}), f32[64,1,64,128]{3,2,1,0:T(8,128)}, u32[]{:S(2)}, u32[]{:S(2)}) async-start(f32[64,1,64,128]{3,2,1,0:T(8,128)} %bitcast.181), calls=%async_computation.4 | async-start | bytes 4194304 | tf_op jit(solution)/shard_map/all_to_all | solution.py:179
  704.4 90.4 %all-to-all-done.3 = f32[64,1,64,128]{3,2,1,0:T(8,128)} async-done(((f32[64,1,64,128]{3,2,1,0:T(8,128)}), f32[64,1,64,128]{3,2,1,0:T(8,128)}, u32[]{:S(2)}, u32[]{:S(2)}) %all-to-all-start.3) | async-done | bytes 2097184 | tf_op jit(solution)/shard_map/all_to_all | solution.py:179
  799.0 74.6 %all-reduce.2.cloned.1.call-done = f32[8,1,64,128]{3,2,1,0:T(8,128)} async-done(((f32[8,1,64,128]{3,2,1,0:T(8,128)}), f32[8,1,64,128]{3,2,1,0:T(8,128)}) %all-reduce.2.cloned.1.call-update) | async-done | bytes 262160 | tf_op jit(solution)/shard_map/psum | solution.py:191
  (137 shorter events, 83.3 us)
Async XLA Ops:
  7.2 58.8 %copy-start = (bf16[16,128,512]{2,1,0:T(8,128)(2,1)S(1)}, bf16[16,128,512]{2,1,0:T(8,128)(2,1)}, u32[]{:S(2)}) copy-start(bf16[16,128,512]{2,1,0:T(8,128)(2,1)} %param.17) | copy-start | bytes 6291460
  8.0 65.5 %copy-start.8 = (s32[2,32]{1,0:T(2,128)}, s32[2,32]{1,0:T(2,128)S(1)}, u32[]{:S(2)}) copy-start(s32[2,32]{1,0:T(2,128)S(1)} %get-tuple-element.431) | copy-start | bytes 772
  8.2 65.3 %copy-start.10 = (s32[2,32]{1,0:T(2,128)}, s32[2,32]{1,0:T(2,128)S(1)}, u32[]{:S(2)}) copy-start(s32[2,32]{1,0:T(2,128)S(1)} %convert_reduce_fusion) | copy-start | bytes 772
  40.8 0.6 copy-start.5
  60.1 5.9 copy-start.4
  60.1 455.3 %all-to-all-start.2 = ((bf16[64,2,64,576]{3,2,1,0:T(8,128)(2,1)}), bf16[64,2,64,576]{3,2,1,0:T(8,128)(2,1)}, u32[]{:S(2)}, u32[]{:S(2)}) async-start(bf16[64,2,64,576]{3,2,1,0:T(8,128)(2,1)} %broadcast_select_fusion), calls=%async_computation.2 | async-start | bytes 20971520 | tf_op jit(solution)/shard_map/all_to_all | solution.py:67
  65.9 1.0 slice-start
  66.9 6.6 copy-start.2
  75.7 455.7 %copy-start.12 = (s32[2,32]{1,0:T(2,128)S(1)}, s32[2,32]{1,0:T(2,128)}, u32[]{:S(2)}) copy-start(s32[2,32]{1,0:T(2,128)} %param.23) | copy-start | bytes 772
  75.7 455.7 %copy-start.14 = (s32[2]{0:T(128)S(1)}, s32[2]{0:T(128)}, u32[]{:S(2)}) copy-start(s32[2]{0:T(128)} %param.22) | copy-start | bytes 28
  515.4 110.3 %all-to-all-start.1 = ((bf16[64,2,64,128]{3,2,1,0:T(8,128)(2,1)}), bf16[64,2,64,128]{3,2,1,0:T(8,128)(2,1)}, u32[]{:S(2)}, u32[]{:S(2)}) async-start(bf16[64,2,64,128]{3,2,1,0:T(8,128)(2,1)} %broadcast_select_fusion.1), calls=%async_computation.1 | async-start | bytes 4194304 | tf_op jit(solution)/shard_map/all_to_all | solution.py:68
  531.1 120.5 %reduce-scatter.2.cloned.1.call-start = ((), (), s32[]{:S(2)}) async-start(), calls=%async_computation.5 | async-start | bytes 1179648 | tf_op jit(solution)/shard_map/reduce_scatter | solution.py:111
  531.4 82.0 %copy-start.9 = (s32[2,32]{1,0:T(2,128)S(1)}, s32[2,32]{1,0:T(2,128)}, u32[]{:S(2)}) copy-start(s32[2,32]{1,0:T(2,128)} %copy-done.8) | copy-start | bytes 772
  531.4 82.0 %copy-start.11 = (s32[2,32]{1,0:T(2,128)S(1)}, s32[2,32]{1,0:T(2,128)}, u32[]{:S(2)}) copy-start(s32[2,32]{1,0:T(2,128)} %copy-done.10) | copy-start | bytes 772
  531.4 121.2 %copy-start.3 = (bf16[16,64,128]{2,1,0:T(8,128)(2,1)S(1)}, bf16[16,64,128]{2,1,0:T(8,128)(2,1)}, u32[]{:S(2)}) copy-start(bf16[16,64,128]{2,1,0:T(8,128)(2,1)} %param.18) | copy-start | bytes 786436
  531.4 121.2 %copy-start.7 = (f32[16,64]{1,0:T(8,128)S(1)}, f32[16,64]{1,0:T(8,128)}, u32[]{:S(2)}) copy-start(f32[16,64]{1,0:T(8,128)} %param.19) | copy-start | bytes 12292
  681.2 7.0 copy-start.13
  682.8 20.2 %copy-start.6 = (s32[64,1,2]{2,1,0:T(1,128)S(1)}, s32[64,1,2]{2,1,0:T(1,128)}, u32[]{:S(2)}) copy-start(s32[64,1,2]{2,1,0:T(1,128)} %copy-done.5) | copy-start | bytes 1540
  682.8 192.4 %copy-start.1 = (bf16[16,128,512]{2,1,0:T(8,128)(2,1)S(1)}, bf16[16,128,512]{2,1,0:T(8,128)(2,1)}, u32[]{:S(2)}) copy-start(bf16[16,128,512]{2,1,0:T(8,128)(2,1)} %param.17) | copy-start | bytes 6291460
  688.2 106.6 %all-to-all-start.3 = ((f32[64,1,64,128]{3,2,1,0:T(8,128)}), f32[64,1,64,128]{3,2,1,0:T(8,128)}, u32[]{:S(2)}, u32[]{:S(2)}) async-start(f32[64,1,64,128]{3,2,1,0:T(8,128)} %bitcast.181), calls=%async_computation.4 | async-start | bytes 4194304 | tf_op jit(solution)/shard_map/all_to_all | solution.py:179
  702.8 170.8 %all-reduce.2.cloned.1.call-start = ((), (), s32[]{:S(2)}) async-start(), calls=%async_computation.6 | async-start | bytes 524288 | tf_op jit(solution)/shard_map/psum | solution.py:191
Sparse Core Ops, SparseCore 0:
  612.0 39.6 reduce-scatter.1
  799.1 74.4 all-reduce.1
where the time goes:
time: 884 us; the launch traced here: 882 us
  waiting for transfers between devices  637 us (72%)
  matrix products  65.9 us (7%)
  local copies, waits for them, and re-layouts  59.5 us (7%)
  starting transfers between devices  36.7 us (4%)
  blocking collectives  32.4 us (4%)
  other arithmetic  32.1 us (4%)
  between operations  15.1 us (2%)
    all_to_all x1, waiting for transfers between devices, local(): lax.all_to_all(entry_rows, 'ctx', split_axis=0, concat_axis=0, tiled=True)  436 us
    all_to_all x1, waiting for transfers between devices, local(): lax.all_to_all(outgoing, 'ctx', split_axis=0, concat_axis=0, tiled=True)  90.4 us
    psum x1, waiting for transfers between devices, local(): owner_total = lax.psum(summed, 'head')  74.6 us
    all_to_all x1, blocking collectives, local(): lax.all_to_all(request_ids, 'ctx', split_axis=0, concat_axis=0, tiled=True)  32.4 us
    div x4, matrix products, masked_softmax(): return expo / jnp.sum(expo, axis=-1, keepdims=True)  25.7 us
    sub x4, matrix products, masked_softmax(): expo = jnp.exp(shifted - row_max)  23.8 us
    reduce_scatter x1, waiting for transfers between devices, local(): lax.psum_scatter(prob_sum.reshape(query_count * block_len, key_count), 'h...  23.7 us
  transfers between devices with their start and end apart: 5, of which 5 were waited for; matrix products, arithmetic and copies ran while one was open for 11% of the time, Pallas kernels for 0%

commit v1 on v0

v1 whole, which is shorter than its diff:
```python
import functools

import jax
import jax.numpy as jnp
from jax import lax
from jax.experimental import pallas as pl
from jax.experimental.pallas import tpu as pltpu
from jax.sharding import PartitionSpec as P

MESH = pl.DeviceIdType.MESH
X = 4
CORES = 2
LANES = 128


def fetch_kernel(
    zs, ys, tab_ref, own_ref, keys_ref,
    tabs_v, tabs_s, zbuf, xsend, xrecv,
    z_send, z_recv, x_send, x_recv, t_send, t_recv, y_send, y_recv, local_sem,
):
    ctx = lax.axis_index("ctx")
    head = lax.axis_index("head")
    z, x = ctx // X, ctx % X
    y, c = head // CORES, head % CORES
    own_blocks, rows, half = own_ref.shape
    z_up = (lax.rem(z + 1, zs) * X + x, head)
    z_down = (lax.rem(z + zs - 1, zs) * X + x, head)
    step = 1 - 2 * c
    y_a = lax.rem(y + step + ys, ys)
    y_b = lax.rem(y - step + ys, ys)
    x_peers = []
    for dx in range(X):
        for dc in range(CORES):
            if dx or dc:
                tx, tc = lax.rem(x + dx, X), lax.rem(c + dc, CORES)
                x_peers.append((dx, dc, tx, tc, (z * X + tx, y * CORES + tc)))

    barrier = pltpu.get_barrier_semaphore()
    peers = [z_up, z_down, (ctx, y_a * CORES + c), (ctx, y_b * CORES + c)] + [p[4] for p in x_peers]
    for peer in peers:
        pl.semaphore_signal(barrier, inc=1, device_id=peer, device_id_type=MESH)
    zbuf[z] = own_ref[...]
    tabs_v[x] = tab_ref[...]
    pl.semaphore_wait(barrier, len(peers))

    def send(src, dst, s_sem, r_sem, device):
        copy = pltpu.make_async_remote_copy(
            src_ref=src, dst_ref=dst, send_sem=s_sem, recv_sem=r_sem, device_id=device, device_id_type=MESH
        )
        return copy

    steps = zs // 2
    part = own_blocks // 2
    sent = []

    def z_piece(direction, k, i):
        owner = lax.rem(z + (zs - k if direction == 0 else k), zs)
        piece = zbuf.at[owner, pl.ds(i * part, part)]
        return send(
            piece, piece, z_send.at[direction, k, i], z_recv.at[direction, k, i],
            z_up if direction == 0 else z_down,
        )

    def z_arrived(direction, k, i):
        owner = lax.rem(z + (zs - k - 1 if direction == 0 else k + 1), zs)
        piece = zbuf.at[owner, pl.ds(i * part, part)]
        send(piece, piece, z_send.at[direction, k, i], z_recv.at[direction, k, i], z_up).wait_recv()

    tab_copies = []
    for k in range(steps):
        for i in range(2):
            for direction in range(2):
                if k == steps - 1 and i != direction:
                    continue
                if k > 0:
                    z_arrived(direction, k - 1, i)
                copy = z_piece(direction, k, i)
                copy.start()
                sent.append(copy)
        if k == 0:
            for dx in range(1, X):
                tx = lax.rem(x + dx, X)
                copy = send(tabs_v.at[x], tabs_v.at[x], t_send.at[dx - 1], t_recv.at[dx - 1], (z * X + tx, head))
                copy.start()
                tab_copies.append(copy)
    for dx in range(1, X):
        fx = lax.rem(x + X - dx, X)
        send(tabs_v.at[fx], tabs_v.at[fx], t_send.at[dx - 1], t_recv.at[dx - 1], z_up).wait_recv()
    to_scalar = pltpu.make_async_copy(tabs_v, tabs_s, local_sem)
    to_scalar.start()
    to_scalar.wait()
    z_arrived(0, steps - 2, 1)
    z_arrived(1, steps - 2, 0)
    z_arrived(0, steps - 1, 0)
    z_arrived(1, steps - 1, 1)

    def choose(tx, tc, dst):
        def body(owner, carry):
            pick = tabs_s[tx, tc, owner * X + x]
            dst[owner] = zbuf[owner, pick]
            return carry

        lax.fori_loop(0, zs, body, 0)

    x_copies = []
    for n, (dx, dc, tx, tc, device) in enumerate(x_peers):
        choose(tx, tc, xsend.at[n])
        copy = send(xsend.at[n], xrecv.at[x, c], x_send.at[n], x_recv.at[n], device)
        copy.start()
        x_copies.append(copy)
    choose(x, c, xrecv.at[x, c])
    for n, (dx, dc, tx, tc, device) in enumerate(x_peers):
        fx, fc = lax.rem(x + X - dx, X), lax.rem(c + dc, CORES)
        send(xsend.at[n], xrecv.at[fx, fc], x_send.at[n], x_recv.at[n], device).wait_recv()

    picks = keys_ref.shape[0]
    chunks = y_send.shape[1]
    chunk = picks // chunks

    def place(m, carry):
        owner = tabs_s[x, CORES + c, m]
        for fc in range(CORES):
            keys_ref[m, pl.ds(pl.multiple_of(y * rows, rows), rows), fc * half : (fc + 1) * half] = xrecv[
                lax.rem(owner, X), fc, lax.div(owner, X)
            ]
        return carry

    def quarter(owner, j):
        return keys_ref.at[pl.ds(j * chunk, chunk), pl.ds(pl.multiple_of(owner * rows, rows), rows)]

    y_far = lax.rem(y + 2, ys)
    y_copies = []

    def y_send_quarter(kind, owner, j, device):
        ref = quarter(owner, j)
        copy = send(ref, ref, y_send.at[kind, j], y_recv.at[kind, j], device)
        copy.start()
        y_copies.append(copy)

    def y_arrived(kind, owner, j):
        ref = quarter(owner, j)
        send(ref, ref, y_send.at[kind, j], y_recv.at[kind, j], (ctx, y_a * CORES + c)).wait_recv()

    for j in range(chunks):
        lax.fori_loop(j * chunk, (j + 1) * chunk, place, 0)
        y_send_quarter(0, y, j, (ctx, y_a * CORES + c))
        y_send_quarter(1, y, j, (ctx, y_b * CORES + c))
    for j in range(chunks):
        y_arrived(0, y_b, j)
        y_send_quarter(2, y_b, j, (ctx, y_a * CORES + c))
    for j in range(chunks):
        y_arrived(1, y_a, j)
        y_arrived(2, y_far, j)
    for copy in sent + tab_copies + x_copies + y_copies:
        copy.wait_send()


def fetch(table, own, zs, ys, picks, block_len):
    own_blocks, rows, half = own.shape
    steps = zs // 2
    peers = X * CORES - 1
    chunks = 4
    return pl.pallas_call(
        functools.partial(fetch_kernel, zs, ys),
        out_shape=jax.ShapeDtypeStruct((picks, block_len, half * CORES), own.dtype),
        in_specs=[pl.BlockSpec(memory_space=pltpu.VMEM)] * 2,
        out_specs=pl.BlockSpec(memory_space=pltpu.VMEM),
        scratch_shapes=[
            pltpu.VMEM((X, 8, LANES), jnp.int32),
            pltpu.SMEM((X, 8, LANES), jnp.int32),
            pltpu.VMEM((zs, own_blocks, rows, half), own.dtype),
            pltpu.VMEM((peers, zs, rows, half), own.dtype),
            pltpu.VMEM((X, CORES, zs, rows, half), own.dtype),
            pltpu.SemaphoreType.DMA((2, steps, 2)),
            pltpu.SemaphoreType.DMA((2, steps, 2)),
            pltpu.SemaphoreType.DMA((peers,)),
            pltpu.SemaphoreType.DMA((peers,)),
            pltpu.SemaphoreType.DMA((X - 1,)),
            pltpu.SemaphoreType.DMA((X - 1,)),
            pltpu.SemaphoreType.DMA((3, chunks)),
            pltpu.SemaphoreType.DMA((3, chunks)),
            pltpu.SemaphoreType.DMA,
        ],
        compiler_params=pltpu.CompilerParams(
            collective_id=0, has_side_effects=True, vmem_limit_bytes=40 * 2**20
        ),
        name="fetch_keys",
    )(table, own)


def attend_kernel(width, scale, q_ref, k_ref, bias_ref, out_ref, logits):
    group, tokens, unused = q_ref.shape
    step = pl.program_id(0)
    keys = k_ref[:, :width]
    queries = q_ref[...].reshape(group * tokens, width)
    logits[...] = lax.dot_general(
        queries, keys, (((1,), (1,)), ((), ())), preferred_element_type=jnp.float32
    )

    @pl.when(step == 0)
    def first():
        out_ref[...] = jnp.zeros_like(out_ref)

    def tile(i, carry):
        at = pl.multiple_of(i * 8, 8)
        bias = bias_ref[pl.ds(at, 8), :]
        total = out_ref[pl.ds(at, 8), :]
        for g in range(group):
            value = logits[pl.ds(pl.multiple_of(g * tokens + i * 8, 8), 8), :] * scale + bias
            expo = jnp.exp2(value - jnp.max(value, axis=1, keepdims=True))
            total = total + expo * (1.0 / jnp.sum(expo, axis=1, keepdims=True))
        out_ref[pl.ds(at, 8), :] = total
        return carry

    lax.fori_loop(0, tokens // 8, tile, 0)


def attend(query, keys, bias, width, scale):
    heads, tokens, unused = query.shape
    key_count, key_width = keys.shape
    group = 4
    return pl.pallas_call(
        functools.partial(attend_kernel, width, scale),
        grid=(heads // group,),
        out_shape=jax.ShapeDtypeStruct((tokens, key_count), jnp.float32),
        in_specs=[
            pl.BlockSpec((group, tokens, width), lambda i: (i, 0, 0)),
            pl.BlockSpec((key_count, key_width), lambda i: (0, 0)),
            pl.BlockSpec((tokens, key_count), lambda i: (0, 0)),
        ],
        out_specs=pl.BlockSpec((tokens, key_count), lambda i: (0, 0)),
        scratch_shapes=[pltpu.VMEM((group * tokens, key_count), jnp.float32)],
        compiler_params=pltpu.CompilerParams(vmem_limit_bytes=40 * 2**20),
        name="attend",
    )(query, keys, bias)


def masked_softmax(values, allowed):
    shifted = jnp.where(allowed, values, -jnp.inf)
    row_max = jnp.max(shifted, axis=-1, keepdims=True)
    expo = jnp.exp(shifted - row_max)
    return expo / jnp.sum(expo, axis=-1, keepdims=True)


def local(
    queries,
    up_weight,
    index_query,
    index_weight,
    cache_entry,
    index_key,
    block_position,
    picked_blocks,
):
    owners = lax.axis_size("ctx")
    head_devices = lax.axis_size("head")
    zs, ys = owners // X, head_devices // CORES
    ctx = lax.axis_index("ctx")
    head = lax.axis_index("head")
    y, c = head // CORES, head % CORES
    query_count, picks = picked_blocks.shape
    own_blocks, unused, block_len, entry_width = cache_entry.shape
    index_width = index_key.shape[3]
    key_count = picks * block_len
    rows = block_len // ys
    local_heads = queries.shape[1]
    nope = up_weight.shape[1]
    latent = up_weight.shape[2]
    pad_width = -(-entry_width // LANES) * LANES
    full_width = pad_width + index_width
    half = full_width // CORES

    owner_of = picked_blocks % owners
    matched = owner_of[:, :, None] == jnp.arange(owners)[None, None, :]
    request = jnp.sum(jnp.where(matched, picked_blocks[:, :, None] // owners + 1, 0), axis=1)
    table = jnp.zeros((8, LANES), jnp.int32)
    table = table.at[:query_count, :owners].set(jnp.maximum(request - 1, 0))
    table = table.at[query_count : 2 * query_count, :picks].set(owner_of)

    own = jnp.concatenate(
        [
            lax.dynamic_slice_in_dim(cache_entry[:, 0], y * rows, rows, 1),
            jnp.zeros((own_blocks, rows, pad_width - entry_width), cache_entry.dtype),
            lax.dynamic_slice_in_dim(index_key[:, 0], y * rows, rows, 1),
        ],
        axis=2,
    )
    own = lax.dynamic_slice_in_dim(own, c * half, half, 2)

    swap = [(i, i ^ 1) for i in range(head_devices)]
    to_row = [((i % CORES) * ys + i // CORES, i) for i in range(head_devices)]
    my_index_query = lax.ppermute(index_query, "head", to_row)
    my_index_weight = lax.ppermute(index_weight, "head", to_row)
    lat = jnp.einsum(
        "thd,hdc->htc", queries[:, :, :nope], up_weight, preferred_element_type=jnp.float32
    ).astype(jnp.bfloat16)
    rope = jnp.transpose(queries[:, :, nope:], (1, 0, 2))
    query_full = jnp.concatenate(
        [lat, rope, jnp.zeros(rope.shape[:2] + (pad_width - entry_width,), rope.dtype)], axis=2
    )
    mine = lax.dynamic_slice_in_dim(query_full, c * block_len, block_len, 1)
    other = lax.dynamic_slice_in_dim(query_full, (1 - c) * block_len, block_len, 1)
    query_row = jnp.concatenate([mine, lax.ppermute(other, "head", swap)], axis=0)

    keys = fetch(table, own, zs, ys, picks, block_len).reshape(key_count, full_width)

    my_picks = lax.dynamic_index_in_dim(picked_blocks, c, 0, keepdims=False)
    my_owner = lax.dynamic_index_in_dim(owner_of, c, 0, keepdims=False)
    my_position = lax.dynamic_index_in_dim(block_position, c, 0, keepdims=False)
    key_place = (my_picks[:, None] * block_len + jnp.arange(block_len)[None, :]).reshape(key_count)
    query_place = my_position * block_len + jnp.arange(block_len)
    allowed = key_place[None, :] <= query_place[:, None]
    bias = jnp.where(allowed, 0.0, -jnp.inf).astype(jnp.float32)
    scale = queries.shape[2] ** (-0.5) * 1.4426950408889634
    prob_sum = attend(query_row, keys, bias, pad_width, scale)

    y_groups = [[k * CORES + j for k in range(ys)] for j in range(CORES)]
    core_groups = [[k * CORES + j for j in range(CORES)] for k in range(ys)]
    target = lax.psum_scatter(
        prob_sum, "head", scatter_dimension=0, axis_index_groups=y_groups, tiled=True
    ) / (local_heads * head_devices)

    index_keys = keys[:, pad_width:]
    my_allowed = lax.dynamic_slice_in_dim(allowed, y * rows, rows, 0)
    index_scale = index_width ** (-0.5)
    raw = jnp.einsum("ijd,sd->ijs", my_index_query, index_keys, preferred_element_type=jnp.float32)
    act = jnp.maximum(raw, 0.0) * index_scale
    score = jnp.sum(my_index_weight[:, :, None] * act, axis=1)
    soft = masked_softmax(score, my_allowed)
    score_grad = jnp.where(my_allowed, soft - target, 0.0)
    weight_part = jnp.sum(score_grad[:, None, :] * act, axis=2)
    coefficient = jnp.where(
        raw > 0, score_grad[:, None, :] * my_index_weight[:, :, None] * index_scale, 0.0
    ).astype(jnp.bfloat16)
    key_part = jnp.einsum(
        "ijs,ijd->sd", coefficient, my_index_query, preferred_element_type=jnp.float32
    )
    weight_grad = lax.ppermute(weight_part, "head", [(b, a) for a, b in to_row])

    quarter = lax.psum_scatter(
        key_part.reshape(picks, ys, rows * index_width),
        "head", scatter_dimension=1, axis_index_groups=y_groups, tiled=True,
    ).reshape(picks, rows * index_width)
    one_hot = (my_owner[None, :] == jnp.arange(owners)[:, None]).astype(jnp.float32)
    outgoing = jnp.einsum("om,mf->of", one_hot, quarter, precision=lax.Precision.HIGHEST)
    arrived = lax.all_to_all(outgoing, "ctx", split_axis=0, concat_axis=0, tiled=True)
    all_requests = lax.all_gather(request, "ctx")
    theirs = lax.dynamic_index_in_dim(all_requests, c, 1, keepdims=False)
    theirs = lax.dynamic_index_in_dim(theirs, ctx, 1, keepdims=False) - 1
    block_hot = (theirs[None, :] == jnp.arange(own_blocks)[:, None]).astype(jnp.float32)
    summed = jnp.einsum("rn,nf->rf", block_hot, arrived, precision=lax.Precision.HIGHEST)
    summed = lax.psum(summed, "head", axis_index_groups=core_groups)
    gathered = lax.all_gather(summed, "head", axis_index_groups=y_groups)
    key_grad = jnp.transpose(
        gathered.reshape(ys, own_blocks, rows, index_width), (1, 0, 2, 3)
    ).reshape(own_blocks, 1, block_len, index_width)
    return (key_grad, weight_grad)


def solution(mesh):
    return jax.shard_map(
        local,
        mesh=mesh,
        in_specs=(
            P("ctx", "head", None),
            P("head", None, None),
            P(("ctx", "head"), None, None),
            P(("ctx", "head"), None),
            P(None, "ctx", None, None),
            P(None, "ctx", None, None),
            P("ctx"),
            P("ctx", None),
        ),
        out_specs=(P(None, "ctx", None, None), P(("ctx", "head"), None)),
        check_vma=False,
    )
```

time: 884 us -> 377 us (0.43)
  waiting for transfers between devices: 637 us -> 77.1 us
  Pallas kernels: 0 us -> 101 us
  blocking collectives: 32.4 us -> 89.7 us
  matrix products: 65.9 us -> 17.4 us
  local copies, waits for them, and re-layouts: 59.5 us -> 11.4 us
  other arithmetic: 32.1 us -> 12.3 us
  starting transfers between devices: 36.7 us -> 51.4 us
    all_to_all x2 -> x0, waiting for transfers between devices: 449 us -> none  [the longest x1 436 us: local(): lax.all_to_all(entry_rows, 'ctx', split_axis=0, concat_axis=0, tiled=True)]
    pallas_call x0 -> x2, Pallas kernels: none -> 101 us  [the longest x1 77.7 us: fetch(): pl.pallas_call(functools.partial(fetch_kernel, zs, ys), out_shape=jax.Sha...]
    all_to_all x1, waiting for transfers between devices: 90.4 us -> 0.01 us  [local(): lax.all_to_all(outgoing, 'ctx', split_axis=0, concat_axis=0, tiled=True)]
    all_gather x0 -> x2, blocking collectives: none -> 89.7 us  [the longest x1 80.1 us: local(): all_requests = lax.all_gather(request, 'ctx')]
    psum x1, waiting for transfers between devices: 74.6 us -> 28.8 us  [local(): summed = lax.psum(summed, 'head', axis_index_groups=core_groups)]
    ppermute x0 -> x4, starting transfers between devices: none -> 36 us  [the longest x1 22.2 us: local(): weight_grad = lax.ppermute(weight_part, 'head', [(b, a) for a, b in to_row])]
    all_to_all x1 -> x0, blocking collectives: 32.4 us -> none  [local(): lax.all_to_all(request_ids, 'ctx', split_axis=0, concat_axis=0, tiled=True)]
    div x4 -> x0, matrix products: 25.7 us -> none  [masked_softmax(): return expo / jnp.sum(expo, axis=-1, keepdims=True)]
  transfers between devices with their start and end apart: 5 -> 8, of which waited for: 5 -> 4; matrix products, arithmetic and copies ran while one was open for 11% -> 7% of each run, Pallas kernels for 0% -> 27%
where the time goes in v1:
time: 377 us; the launch traced here: 375 us
  Pallas kernels  101 us (27%)
  blocking collectives  89.7 us (24%)
  waiting for transfers between devices  77.1 us (20%)
  starting transfers between devices  51.4 us (14%)
  matrix products  17.4 us (5%)
  between operations  14.7 us (4%)
  other arithmetic  12.3 us (3%)
  local copies, waits for them, and re-layouts  11.4 us (3%)
    all_gather x1, blocking collectives, local(): all_requests = lax.all_gather(request, 'ctx')  80.1 us
    pallas_call x1, Pallas kernels, fetch(): pl.pallas_call(functools.partial(fetch_kernel, zs, ys), out_shape=jax.Sha...  77.7 us
    reduce_scatter x1, waiting for transfers between devices, local(): lax.psum_scatter(key_part.reshape(picks, ys, rows * index_width), 'head',...  31.5 us
    psum x1, waiting for transfers between devices, local(): summed = lax.psum(summed, 'head', axis_index_groups=core_groups)  28.8 us
    pallas_call x1, Pallas kernels, attend(): pl.pallas_call(functools.partial(attend_kernel, width, scale), grid=(head...  23.2 us
    ppermute x1, starting transfers between devices, local(): weight_grad = lax.ppermute(weight_part, 'head', [(b, a) for a, b in to_row])  22.2 us
    reduce_scatter x1, waiting for transfers between devices, local(): lax.psum_scatter(prob_sum, 'head', scatter_dimension=0, axis_index_groups...  16 us
    all_to_all x1, starting transfers between devices, local(): lax.all_to_all(outgoing, 'ctx', split_axis=0, concat_axis=0, tiled=True)  15.3 us
  transfers between devices with their start and end apart: 8, of which 4 were waited for; matrix products, arithmetic and copies ran while one was open for 7% of the time, Pallas kernels for 27%

profile of v1, /device:TPU:1, one launch (start us, length us, event | category | flops | bytes accessed | tf_op | source)
XLA Modules:
  0.0 374.8 jit_solution(3035319211583252181)
XLA Ops:
  7.2 4.7 %collective-permute-start.1 = (f32[16,64]{1,0:T(8,128)}, f32[16,64]{1,0:T(8,128)S(1)}, u32[]{:S(2)}, u32[]{:S(2)}) collective-permute-start(f32[16,64]{1,0:T(8,128)} %param.15), channel_id=1, source_target_pairs={{0,0},{4,1},{1,2},{5,3},{2,4},{6,5},{3,6},{7,7},{8,8},{12,9},{9,10... | collective-permute-start | bytes 12296 | tf_op jit(solution)/shard_map/ppermute | solution.py:293
  12.0 3.5 collective-permute-start
  16.8 3.2 convolution_convert_fusion
  20.0 2.2 maximum_maximum_fusion
  22.2 1.3 constant_dynamic-slice_fusion.1
  23.6 5.6 %collective-permute-start.2 = (bf16[16,64,640]{2,1,0:T(8,128)(2,1)}, bf16[16,64,640]{2,1,0:T(8,128)(2,1)}, u32[]{:S(2)}, u32[]{:S(2)}) collective-permute-start(bf16[16,64,640]{2,1,0:T(8,128)(2,1)} %get-tuple-element.29), channel_id=1, source_target_pairs={{0,1},{1,0},{2,3},{3,2},{4,5},{5,4},{6,7},{7,6},{8,9},{9,8},{10,11... | collective-permute-start | bytes 3932168 | tf_op jit(solution)/shard_map/ppermute | solution.py:303
  32.9 77.7 %fetch_keys.1 = bf16[32,64,768]{2,1,0:T(8,128)(2,1)S(1)} custom-call(s32[8,128]{1,0:T(8,128)S(1)} %scatter.9.tab_ref, bf16[8,16,384]{2,1,0:T(8,128)(2,1)S(1)} %fusion.11.own_ref), custom_call_target="tpu_custom_call" | custom-call | tf_op jit(solution)/shard_map/fetch_keys/pallas_call | solution.py:163
  110.8 2.6 pad_maximum_fusion.q_ref
  113.4 23.2 %attend.1 = f32[64,2048]{1,0:T(8,128)} custom-call(bf16[32,64,640]{2,1,0:T(8,128)(2,1)S(1)} %pad_maximum_fusion.q_ref, bf16[2048,768]{1,0:T(8,128)(2,1)S(1)} %bitcast.48, f32[64,2048]{1,0:T(8,128)S(1)} %broadcast_select_fusion.bias_ref), custom_call_target="tpu_custom_call" | custom-call | tf_op jit(solution)/shard_map/attend/pallas_call | solution.py:222
  136.8 5.6 %fusion = (f32[16,2048]{1,0:T(8,128)S(1)}, f32[2048,16,64]{0,2,1:T(8,128)}) fusion(f32[16,64]{1,0:T(8,128)S(1)} %broadcast_multiply_fusion.1, bf16[16,64,128]{2,1,0:T(8,128)(2,1)} %collective-permute-done, bf16[2048,768]{1,0:T(8,128)(2,1)} %bitcast.49), kind=kOutput, calls=%fused_computation.2 | convolution fusion | flops 543129600 | bytes 9310208 | tf_op jit(solution)/shard_map/ijd,sd->ijs/dot_general | solution.py:326
  142.8 16.0 %reduce-scatter.3.cloned.1.call-done = f32[16,2048]{1,0:T(8,128)} async-done(((f32[64,2048]{1,0:T(8,128)}), f32[16,2048]{1,0:T(8,128)}) %reduce-scatter.3.cloned.1.call-update) | async-done | bytes 131088 | tf_op jit(solution)/shard_map/reduce_scatter | solution.py:319
  159.8 6.2 %fusion.3 = f32[2048,128]{1,0:T(8,128)} fusion(bf16[16,64,128]{2,1,0:T(8,128)(2,1)} %collective-permute-done, f32[2048,16,64]{0,2,1:T(8,128)} %get-tuple-element.33, f32[16,64]{1,0:T(8,128)S(1)} %collective-permute-done.1, f32[16,2048]{1,0:T(8,128)S(1)} %get-tuple-element.27), kind=kOutput, calls=%fused_computation.8 | convolution fusion | flops 547356672 | bytes 9834496 | tf_op jit(solution)/shard_map/ijs,ijd->sd/dot_general | solution.py:335
  166.0 1.6 reshape.149
  167.6 1.7 copy.23
  169.3 31.5 %reduce-scatter.5.cloned.1.call-done = f32[32,1,2048]{2,0,1:T(8,128)} async-done(((f32[32,4,2048]{2,0,1:T(8,128)}), f32[32,1,2048]{2,0,1:T(8,128)}) %reduce-scatter.5.cloned.1.call-update) | async-done | bytes 262160 | tf_op jit(solution)/shard_map/reduce_scatter | solution.py:340
  200.8 1.3 convolution_bitcast_fusion
  202.1 1.4 copy.24
  203.5 15.3 %all-to-all-start = ((f32[64,1,2048]{2,1,0:T(1,128)}), f32[64,1,2048]{2,1,0:T(1,128)S(1)}, u32[]{:S(2)}, u32[]{:S(2)}) async-start(f32[64,1,2048]{2,1,0:T(1,128)} %copy.24), calls=%async_computation.2 | async-start | bytes 1048576 | tf_op jit(solution)/shard_map/all_to_all | solution.py:346
  218.9 80.1 %all-gather.1 = s32[64,2,64]{2,1,0:T(2,128)S(1)} all-gather(s32[1,2,64]{2,1,0:T(2,128)S(1)} %bitcast.53), channel_id=2, replica_groups=mesh['ctx'=64,'head'=8] {'ctx'}, dimensions={0}, use_global_device_ids=true | all-gather | bytes 33280 | tf_op jit(solution)/shard_map/all_gather | solution.py:347
  299.0 1.3 fusion.13
  301.4 4.3 %fusion.1 = f32[16,64]{1,0:T(8,128)S(1)} fusion(f32[2048,16,64]{0,2,1:T(8,128)} %get-tuple-element.33, f32[16,2048]{1,0:T(8,128)S(1)} %get-tuple-element.26), kind=kLoop, calls=%fused_computation.3 | loop fusion | flops 6290432 | bytes 8523776 | tf_op jit(solution)/shard_map/reduce_sum | solution.py:331
  305.7 22.2 %collective-permute-start.3 = (f32[16,64]{1,0:T(8,128)S(1)}, f32[16,64]{1,0:T(8,128)S(1)}, u32[]{:S(2)}, u32[]{:S(2)}) collective-permute-start(f32[16,64]{1,0:T(8,128)S(1)} %fusion.1), channel_id=1, source_target_pairs={{0,0},{1,4},{2,1},{3,5},{4,2},{5,6},{6,3},{7,7},{8,8},{9,12},{10,9... | collective-permute-start | bytes 12296 | tf_op jit(solution)/shard_map/ppermute | solution.py:338
  328.6 28.8 %all-reduce.3.cloned.1.call-done = f32[1,8,2048]{2,1,0:T(8,128)} async-done(((f32[1,8,2048]{2,1,0:T(8,128)}), f32[1,8,2048]{2,1,0:T(8,128)}) %all-reduce.3.cloned.1.call-update) | async-done | bytes 65552 | tf_op jit(solution)/shard_map/psum | solution.py:352
  357.4 9.6 %all_gather.15 = f32[4,8,2048]{2,1,0:T(8,128)S(1)} all-gather(f32[1,8,2048]{2,1,0:T(8,128)} %all-reduce.3.cloned.1.call-done), channel_id=1, replica_groups={{0,2,4,6},{1,3,5,7},{8,10,12,14},{9,11,13,15},{16,18,20,22},{17,19,21,2..., dimensions={0}, use_global_device_ids=true | all-gather | bytes 327680 | tf_op jit(solution)/shard_map/all_gather | solution.py:353
  (47 shorter events, 9.3 us)
Async XLA Ops:
  7.2 9.6 %copy-start = (bf16[16,128,512]{2,1,0:T(8,128)(2,1)S(1)}, bf16[16,128,512]{2,1,0:T(8,128)(2,1)}, u32[]{:S(2)}) copy-start(bf16[16,128,512]{2,1,0:T(8,128)(2,1)} %param.13) | copy-start | bytes 6291460
  7.2 151.6 %reduce-scatter.3.cloned.1.call-start = ((), (), s32[]{:S(2)}) async-start(), calls=%async_computation.3 | async-start | bytes 655360 | tf_op jit(solution)/shard_map/reduce_scatter | solution.py:319
  7.2 129.6 %collective-permute-start.1 = (f32[16,64]{1,0:T(8,128)}, f32[16,64]{1,0:T(8,128)S(1)}, u32[]{:S(2)}, u32[]{:S(2)}) collective-permute-start(f32[16,64]{1,0:T(8,128)} %param.15), channel_id=1, source_target_pairs={{0,0},{4,1},{1,2},{5,3},{2,4},{6,5},{3,6},{7,7},{8,8},{12,9},{9,10... | collective-permute-start | bytes 12296 | tf_op jit(solution)/shard_map/ppermute | solution.py:293
  12.0 124.9 %collective-permute-start = (bf16[16,64,128]{2,1,0:T(8,128)(2,1)}, bf16[16,64,128]{2,1,0:T(8,128)(2,1)}, u32[]{:S(2)}, u32[]{:S(2)}) collective-permute-start(bf16[16,64,128]{2,1,0:T(8,128)(2,1)} %param.14), channel_id=1, source_target_pairs={{0,0},{4,1},{1,2},{5,3},{2,4},{6,5},{3,6},{7,7},{8,8},{12,9},{9,10... | collective-permute-start | bytes 786440 | tf_op jit(solution)/shard_map/ppermute | solution.py:292
  20.0 9.2 %copy-start.2 = (s32[2,32]{1,0:T(2,128)S(1)}, s32[2,32]{1,0:T(2,128)}, u32[]{:S(2)}) copy-start(s32[2,32]{1,0:T(2,128)} %param.19) | copy-start | bytes 772
  20.0 9.2 %copy-start.3 = (s32[2]{0:T(128)S(1)}, s32[2]{0:T(128)}, u32[]{:S(2)}) copy-start(s32[2]{0:T(128)} %param.18) | copy-start | bytes 28
  23.6 87.2 %collective-permute-start.2 = (bf16[16,64,640]{2,1,0:T(8,128)(2,1)}, bf16[16,64,640]{2,1,0:T(8,128)(2,1)}, u32[]{:S(2)}, u32[]{:S(2)}) collective-permute-start(bf16[16,64,640]{2,1,0:T(8,128)(2,1)} %get-tuple-element.29), channel_id=1, source_target_pairs={{0,1},{1,0},{2,3},{3,2},{4,5},{5,4},{6,7},{7,6},{8,9},{9,8},{10,11... | collective-permute-start | bytes 3932168 | tf_op jit(solution)/shard_map/ppermute | solution.py:303
  110.6 2.7 copy-start.1
  136.6 64.2 %reduce-scatter.5.cloned.1.call-start = ((), (), s32[]{:S(2)}) async-start(), calls=%async_computation.4 | async-start | bytes 1310720 | tf_op jit(solution)/shard_map/reduce_scatter | solution.py:340
  203.5 96.8 %all-to-all-start = ((f32[64,1,2048]{2,1,0:T(1,128)}), f32[64,1,2048]{2,1,0:T(1,128)S(1)}, u32[]{:S(2)}, u32[]{:S(2)}) async-start(f32[64,1,2048]{2,1,0:T(1,128)} %copy.24), calls=%async_computation.2 | async-start | bytes 1048576 | tf_op jit(solution)/shard_map/all_to_all | solution.py:346
  218.8 138.5 %all-reduce.3.cloned.1.call-start = ((), (), s32[]{:S(2)}) async-start(), calls=%async_computation.5 | async-start | bytes 131072 | tf_op jit(solution)/shard_map/psum | solution.py:352
  305.7 22.9 %collective-permute-start.3 = (f32[16,64]{1,0:T(8,128)S(1)}, f32[16,64]{1,0:T(8,128)S(1)}, u32[]{:S(2)}, u32[]{:S(2)}) collective-permute-start(f32[16,64]{1,0:T(8,128)S(1)} %fusion.1), channel_id=1, source_target_pairs={{0,0},{1,4},{2,1},{3,5},{4,2},{5,6},{6,3},{7,7},{8,8},{9,12},{10,9... | collective-permute-start | bytes 12296 | tf_op jit(solution)/shard_map/ppermute | solution.py:338
Sparse Core Ops, SparseCore 0:
  136.7 22.0 reduce-scatter.2
  169.4 31.3 reduce-scatter.4
  301.5 55.8 all-reduce.2

commit v2 on v1

--- a/solution.py
+++ b/solution.py
@@ -14,7 +14,7 @@
 
 
 def fetch_kernel(
-    zs, ys, tab_ref, own_ref, keys_ref,
+    zs, ys, tab_ref, own_ref, keys_ref, tabs_ref,
     tabs_v, tabs_s, zbuf, xsend, xrecv,
     z_send, z_recv, x_send, x_recv, t_send, t_recv, y_send, y_recv, local_sem,
 ):
@@ -89,6 +89,7 @@
     to_scalar = pltpu.make_async_copy(tabs_v, tabs_s, local_sem)
     to_scalar.start()
     to_scalar.wait()
+    tabs_ref[...] = tabs_v[...]
     z_arrived(0, steps - 2, 1)
     z_arrived(1, steps - 2, 0)
     z_arrived(0, steps - 1, 0)
@@ -162,9 +163,12 @@
     chunks = 4
     return pl.pallas_call(
         functools.partial(fetch_kernel, zs, ys),
-        out_shape=jax.ShapeDtypeStruct((picks, block_len, half * CORES), own.dtype),
+        out_shape=(
+            jax.ShapeDtypeStruct((picks, block_len, half * CORES), own.dtype),
+            jax.ShapeDtypeStruct((X, 8, LANES), jnp.int32),
+        ),
         in_specs=[pl.BlockSpec(memory_space=pltpu.VMEM)] * 2,
-        out_specs=pl.BlockSpec(memory_space=pltpu.VMEM),
+        out_specs=[pl.BlockSpec(memory_space=pltpu.VMEM)] * 2,
         scratch_shapes=[
             pltpu.VMEM((X, 8, LANES), jnp.int32),
             pltpu.SMEM((X, 8, LANES), jnp.int32),
@@ -233,6 +237,218 @@
         compiler_params=pltpu.CompilerParams(vmem_limit_bytes=40 * 2**20),
         name="attend",
     )(query, keys, bias)
+
+
+def remote(src, dst, s_sem, r_sem, device):
+    return pltpu.make_async_remote_copy(
+        src_ref=src, dst_ref=dst, send_sem=s_sem, recv_sem=r_sem, device_id=device, device_id_type=MESH
+    )
+
+
+def enter(peers):
+    barrier = pltpu.get_barrier_semaphore()
+    for peer in peers:
+        pl.semaphore_signal(barrier, inc=1, device_id=peer, device_id_type=MESH)
+    pl.semaphore_wait(barrier, len(peers))
+
+
+def y_sides(ys):
+    head = lax.axis_index("head")
+    y, c = head // CORES, head % CORES
+    step = 1 - 2 * c
+    return y, c, lax.rem(y + step + ys, ys), lax.rem(y - step + ys, ys), lax.rem(y + 2, ys)
+
+
+def target_kernel(ys, prob_ref, out_ref, arrived, middle, s_sem, r_sem):
+    ctx = lax.axis_index("ctx")
+    y, c, y_a, y_b, y_far = y_sides(ys)
+    rows = out_ref.shape[0]
+    to_a, to_b = (ctx, y_a * CORES + c), (ctx, y_b * CORES + c)
+    enter([to_a, to_b])
+
+    def quarter(k):
+        return prob_ref.at[pl.ds(pl.multiple_of(k * rows, rows), rows)]
+
+    far = remote(quarter(y_far), arrived.at[0], s_sem.at[0], r_sem.at[0], to_a)
+    near = remote(quarter(y_b), arrived.at[1], s_sem.at[1], r_sem.at[1], to_b)
+    far.start()
+    near.start()
+    far.wait_recv()
+    middle[...] = quarter(y_a)[...] + arrived[0]
+    last = remote(middle, arrived.at[2], s_sem.at[2], r_sem.at[2], to_a)
+    last.start()
+    near.wait_recv()
+    last.wait_recv()
+    out_ref[...] = quarter(y)[...] + arrived[1] + arrived[2]
+    for copy in (far, near, last):
+        copy.wait_send()
+
+
+def sum_target(prob_sum, ys):
+    tokens, key_count = prob_sum.shape
+    rows = tokens // ys
+    return pl.pallas_call(
+        functools.partial(target_kernel, ys),
+        out_shape=jax.ShapeDtypeStruct((rows, key_count), jnp.float32),
+        in_specs=[pl.BlockSpec(memory_space=pltpu.VMEM)],
+        out_specs=pl.BlockSpec(memory_space=pltpu.VMEM),
+        scratch_shapes=[
+            pltpu.VMEM((3, rows, key_count), jnp.float32),
+            pltpu.VMEM((rows, key_count), jnp.float32),
+            pltpu.SemaphoreType.DMA((3,)),
+            pltpu.SemaphoreType.DMA((3,)),
+        ],
+        compiler_params=pltpu.CompilerParams(
+            collective_id=1, has_side_effects=True, vmem_limit_bytes=40 * 2**20
+        ),
+        name="sum_target",
+    )(prob_sum)
+
+
+def return_kernel(
+    zs, ys, tabs_ref, part_ref, out_ref,
+    y_out, y_in, quarter, x_out, x_in, z_out, z_in, mine, theirs,
+    ys_sem, yr_sem, xs_sem, xr_sem, zs_sem, zr_sem, cs_sem, cr_sem, os_sem, or_sem,
+):
+    ctx = lax.axis_index("ctx")
+    z, x = ctx // X, ctx % X
+    y, c, y_a, y_b, y_far = y_sides(ys)
+    head = y * CORES + c
+    picks, block_len, width = part_ref.shape
+    own_blocks = out_ref.shape[0]
+    rows = block_len // ys
+    slots = X * rows
+    to_a, to_b, to_far = (ctx, y_a * CORES + c), (ctx, y_b * CORES + c), (ctx, y_far * CORES + c)
+    to_core = (ctx, y * CORES + 1 - c)
+    x_peers = [(lax.rem(x + d, X), (z * X + lax.rem(x + d, X), head)) for d in range(1, X)]
+    z_peers = [(lax.rem(z + d, zs), (lax.rem(z + d, zs) * X + x, head)) for d in range(1, zs)]
+    enter([to_a, to_b, to_far, to_core] + [p[1] for p in x_peers] + [p[1] for p in z_peers])
+
+    def span(k):
+        return pl.ds(pl.multiple_of(k * rows, rows), rows)
+
+    y_out[0] = part_ref[:, span(y_far), :].astype(y_out.dtype)
+    far = remote(y_out.at[0], y_in.at[0], ys_sem.at[0], yr_sem.at[0], to_a)
+    far.start()
+    y_out[1] = part_ref[:, span(y_b), :].astype(y_out.dtype)
+    near = remote(y_out.at[1], y_in.at[1], ys_sem.at[1], yr_sem.at[1], to_b)
+    near.start()
+    far.wait_recv()
+    y_out[2] = (part_ref[:, span(y_a), :] + y_in[0].astype(jnp.float32)).astype(y_out.dtype)
+    last = remote(y_out.at[2], y_in.at[2], ys_sem.at[2], yr_sem.at[2], to_a)
+    last.start()
+    near.wait_recv()
+    last.wait_recv()
+    quarter[...] = (
+        part_ref[:, span(y), :] + y_in[1].astype(jnp.float32) + y_in[2].astype(jnp.float32)
+    )
+
+    def choose(tx, dst):
+        def body(owner, carry):
+            place = tabs_ref[x, 3 * CORES + c, owner * X + tx]
+            value = quarter[jnp.maximum(place - 1, 0)]
+            dst[owner] = jnp.where(place > 0, value, 0.0).astype(dst.dtype)
+            return carry
+
+        lax.fori_loop(0, zs, body, 0)
+
+    x_copies = []
+    for n, (tx, device) in enumerate(x_peers):
+        choose(tx, x_out.at[n])
+        copy = remote(x_out.at[n], x_in.at[x], xs_sem.at[n], xr_sem.at[n], device)
+        copy.start()
+        x_copies.append(copy)
+    choose(x, x_in.at[x])
+    for n in range(X - 1):
+        fx = lax.rem(x + X - n - 1, X)
+        remote(x_out.at[n], x_in.at[fx], xs_sem.at[n], xr_sem.at[n], to_a).wait_recv()
+
+    line = lax.broadcasted_iota(jnp.int32, (rows, width), 0)
+
+    def gather(owner, dst):
+        ids = jnp.zeros((rows, width), jnp.float32)
+        for fx in range(X):
+            dst[fx * rows : (fx + 1) * rows] = x_in[fx, owner]
+            block = tabs_ref[fx, 2 * CORES + c, owner * X + x]
+            ids = jnp.where(line == fx, block.astype(jnp.float32), ids)
+        dst[slots : slots + rows] = ids.astype(dst.dtype)
+
+    z_copies = []
+    order = sorted(range(1, zs), key=lambda d: -min(d, zs - d))
+    for d in order:
+        tz, device = z_peers[d - 1]
+        gather(tz, z_out.at[d - 1])
+        copy = remote(z_out.at[d - 1], z_in.at[z], zs_sem.at[d - 1], zr_sem.at[d - 1], device)
+        copy.start()
+        z_copies.append(copy)
+    gather(z, z_in.at[z])
+    for d in order:
+        fz = lax.rem(z + zs - d, zs)
+        remote(z_out.at[d - 1], z_in.at[fz], zs_sem.at[d - 1], zr_sem.at[d - 1], to_a).wait_recv()
+
+    def add(fz, totals):
+        ids = z_in[fz, slots : slots + rows].astype(jnp.float32)
+        totals = list(totals)
+        for fx in range(X):
+            value = z_in[fz, fx * rows : (fx + 1) * rows].astype(jnp.float32)
+            block = jnp.broadcast_to(ids[fx : fx + 1], value.shape)
+            for r in range(own_blocks):
+                totals[r] = totals[r] + jnp.where(block == r + 1.0, value, 0.0)
+        return tuple(totals)
+
+    totals = lax.fori_loop(
+        0, zs, add, tuple(jnp.zeros((rows, width), jnp.float32) for r in range(own_blocks))
+    )
+    for r in range(own_blocks):
+        mine[r] = totals[r]
+    core = remote(mine, theirs, cs_sem, cr_sem, to_core)
+    core.start()
+    core.wait_recv()
+    out_ref[:, span(y), :] = mine[...] + theirs[...]
+    o_copies = []
+    for n, device in enumerate((to_a, to_b, to_far)):
+        ref = out_ref.at[:, span(y), :]
+        copy = remote(ref, ref, os_sem.at[n], or_sem.at[n], device)
+        copy.start()
+        o_copies.append(copy)
+    for n, fy in enumerate((y_b, y_a, y_far)):
+        ref = out_ref.at[:, span(fy), :]
+        remote(ref, ref, os_sem.at[n], or_sem.at[n], to_a).wait_recv()
+    for copy in [far, near, last, core] + x_copies + z_copies + o_copies:
+        copy.wait_send()
+
+
+def give_back(tables, key_part, zs, ys, own_blocks):
+    picks, block_len, width = key_part.shape
+    rows = block_len // ys
+    half = jnp.bfloat16
+    dma = pltpu.SemaphoreType.DMA
+    return pl.pallas_call(
+        functools.partial(return_kernel, zs, ys),
+        out_shape=jax.ShapeDtypeStruct((own_blocks, block_len, width), jnp.float32),
+        in_specs=[
+            pl.BlockSpec(memory_space=pltpu.SMEM),
+            pl.BlockSpec(memory_space=pltpu.VMEM),
+        ],
+        out_specs=pl.BlockSpec(memory_space=pltpu.VMEM),
+        scratch_shapes=[
+            pltpu.VMEM((3, picks, rows, width), half),
+            pltpu.VMEM((3, picks, rows, width), half),
+            pltpu.VMEM((picks, rows, width), jnp.float32),
+            pltpu.VMEM((X - 1, zs, rows, width), half),
+            pltpu.VMEM((X, zs, rows, width), half),
+            pltpu.VMEM((zs - 1, (X + 1) * rows, width), half),
+            pltpu.VMEM((zs, (X + 1) * rows, width), half),
+            pltpu.VMEM((own_blocks, rows, width), jnp.float32),
+            pltpu.VMEM((own_blocks, rows, width), jnp.float32),
+            dma((3,)), dma((3,)), dma((X - 1,)), dma((X - 1,)), dma((zs - 1,)), dma((zs - 1,)),
+            dma, dma, dma((3,)), dma((3,)),
+        ],
+        compiler_params=pltpu.CompilerParams(
+            collective_id=2, has_side_effects=True, vmem_limit_bytes=40 * 2**20
+        ),
+        name="give_back",
+    )(tables, key_part)
 
 
 def masked_softmax(values, allowed):
@@ -276,6 +492,9 @@
     table = jnp.zeros((8, LANES), jnp.int32)
     table = table.at[:query_count, :owners].set(jnp.maximum(request - 1, 0))
     table = table.at[query_count : 2 * query_count, :picks].set(owner_of)
+    table = table.at[2 * query_count : 3 * query_count, :owners].set(request)
+    place = jnp.sum(jnp.where(matched, jnp.arange(1, picks + 1)[None, :, None], 0), axis=1)
+    table = table.at[3 * query_count : 4 * query_count, :owners].set(place)
 
     own = jnp.concatenate(
         [
@@ -302,10 +521,10 @@
     other = lax.dynamic_slice_in_dim(query_full, (1 - c) * block_len, block_len, 1)
     query_row = jnp.concatenate([mine, lax.ppermute(other, "head", swap)], axis=0)
 
-    keys = fetch(table, own, zs, ys, picks, block_len).reshape(key_count, full_width)
+    keys, tables = fetch(table, own, zs, ys, picks, block_len)
+    keys = keys.reshape(key_count, full_width)
 
     my_picks = lax.dynamic_index_in_dim(picked_blocks, c, 0, keepdims=False)
-    my_owner = lax.dynamic_index_in_dim(owner_of, c, 0, keepdims=False)
     my_position = lax.dynamic_index_in_dim(block_position, c, 0, keepdims=False)
     key_place = (my_picks[:, None] * block_len + jnp.arange(block_len)[None, :]).reshape(key_count)
     query_place = my_position * block_len + jnp.arange(block_len)
@@ -314,11 +533,7 @@
     scale = queries.shape[2] ** (-0.5) * 1.4426950408889634
     prob_sum = attend(query_row, keys, bias, pad_width, scale)
 
-    y_groups = [[k * CORES + j for k in range(ys)] for j in range(CORES)]
-    core_groups = [[k * CORES + j for j in range(CORES)] for k in range(ys)]
-    target = lax.psum_scatter(
-        prob_sum, "head", scatter_dimension=0, axis_index_groups=y_groups, tiled=True
-    ) / (local_heads * head_devices)
+    target = sum_target(prob_sum, ys) / (local_heads * head_devices)
 
     index_keys = keys[:, pad_width:]
     my_allowed = lax.dynamic_slice_in_dim(allowed, y * rows, rows, 0)
@@ -337,22 +552,8 @@
     )
     weight_grad = lax.ppermute(weight_part, "head", [(b, a) for a, b in to_row])
 
-    quarter = lax.psum_scatter(
-        key_part.reshape(picks, ys, rows * index_width),
-        "head", scatter_dimension=1, axis_index_groups=y_groups, tiled=True,
-    ).reshape(picks, rows * index_width)
-    one_hot = (my_owner[None, :] == jnp.arange(owners)[:, None]).astype(jnp.float32)
-    outgoing = jnp.einsum("om,mf->of", one_hot, quarter, precision=lax.Precision.HIGHEST)
-    arrived = lax.all_to_all(outgoing, "ctx", split_axis=0, concat_axis=0, tiled=True)
-    all_requests = lax.all_gather(request, "ctx")
-    theirs = lax.dynamic_index_in_dim(all_requests, c, 1, keepdims=False)
-    theirs = lax.dynamic_index_in_dim(theirs, ctx, 1, keepdims=False) - 1
-    block_hot = (theirs[None, :] == jnp.arange(own_blocks)[:, None]).astype(jnp.float32)
-    summed = jnp.einsum("rn,nf->rf", block_hot, arrived, precision=lax.Precision.HIGHEST)
-    summed = lax.psum(summed, "head", axis_index_groups=core_groups)
-    gathered = lax.all_gather(summed, "head", axis_index_groups=y_groups)
-    key_grad = jnp.transpose(
-        gathered.reshape(ys, own_blocks, rows, index_width), (1, 0, 2, 3)
+    key_grad = give_back(
+        tables, key_part.reshape(picks, block_len, index_width), zs, ys, own_blocks
     ).reshape(own_blocks, 1, block_len, index_width)
     return (key_grad, weight_grad)
 

time: 377 us -> 195 us (0.52)
  blocking collectives: 89.7 us -> 0 us
  waiting for transfers between devices: 77.1 us -> 0.01 us
  Pallas kernels: 101 us -> 153 us
  starting transfers between devices: 51.4 us -> 19 us
  between operations: 14.7 us -> 1.63 us
  matrix products: 17.4 us -> 6.25 us
  other arithmetic: 12.3 us -> 5.78 us
    all_gather x2 -> x0, blocking collectives: 89.7 us -> none  [the longest x1 80.1 us: local(): all_requests = lax.all_gather(request, 'ctx')]
    pallas_call x1 -> x3, Pallas kernels: 77.7 us -> 131 us  [the longest x1 79.4 us: fetch(): pl.pallas_call(functools.partial(fetch_kernel, zs, ys), out_shape=(jax.Sh...]
    reduce_scatter x2 -> x0, waiting for transfers between devices: 47.5 us -> none  [the longest x1 31.5 us: local(): lax.psum_scatter(key_part.reshape(picks, ys, rows * index_width), 'head',...]
    psum x1 -> x0, waiting for transfers between devices: 28.8 us -> none  [local(): summed = lax.psum(summed, 'head', axis_index_groups=core_groups)]
    ppermute x1, starting transfers between devices: 22.2 us -> 6.41 us  [local(): weight_grad = lax.ppermute(weight_part, 'head', [(b, a) for a, b in to_row])]
    all_to_all x1 -> x0, starting transfers between devices: 15.3 us -> none  [local(): lax.all_to_all(outgoing, 'ctx', split_axis=0, concat_axis=0, tiled=True)]
    dot_general x1, matrix products: 6.23 us -> 1.81 us  [local(): jnp.einsum('ijs,ijd->sd', coefficient, my_index_query, preferred_element_...]
    dot_general x1, matrix products: 5.62 us -> 1.28 us  [local(): jnp.einsum('ijd,sd->ijs', my_index_query, index_keys, preferred_element_t...]
  transfers between devices with their start and end apart: 8 -> 4, of which waited for: 4 -> 0; matrix products, arithmetic and copies ran while one was open for 7% -> 4% of each run, Pallas kernels for 27% -> 63%
where the time goes in v2:
time: 195 us; the launch traced here: 194 us
  Pallas kernels  153 us (78%)
  starting transfers between devices  19 us (10%)
  local copies, waits for them, and re-layouts  8.41 us (4%)
  matrix products  6.25 us (3%)
  other arithmetic  5.78 us (3%)
    pallas_call x1, Pallas kernels, fetch(): pl.pallas_call(functools.partial(fetch_kernel, zs, ys), out_shape=(jax.Sh...  79.4 us
    pallas_call x1, Pallas kernels, give_back(): pl.pallas_call(functools.partial(return_kernel, zs, ys), out_shape=jax.Sh...  43.3 us
    pallas_call x1, Pallas kernels, attend(): pl.pallas_call(functools.partial(attend_kernel, width, scale), grid=(head...  22.4 us
    ppermute x1, starting transfers between devices, local(): lax.ppermute(other, 'head', swap)  8.77 us
    pallas_call x1, Pallas kernels, sum_target(): pl.pallas_call(functools.partial(target_kernel, ys), out_shape=jax.ShapeD...  8.11 us
    ppermute x1, starting transfers between devices, local(): weight_grad = lax.ppermute(weight_part, 'head', [(b, a) for a, b in to_row])  6.41 us
  transfers between devices with their start and end apart: 4, of which 0 were waited for; matrix products, arithmetic and copies ran while one was open for 4% of the time, Pallas kernels for 63%

profile of v2, /device:TPU:1, one launch (start us, length us, event | category | flops | bytes accessed | tf_op | source)
XLA Modules:
  0.0 194.3 jit_solution(8272987839539112812)
XLA Ops:
  0.7 1.6 copy-done
  2.2 3.2 %convolution_convert_fusion = bf16[16,128,512]{2,1,0:T(8,128)(2,1)} fusion(bf16[16,128,512]{2,1,0:T(8,128)(2,1)S(1)} %copy-done, bf16[128,16,192]{0,2,1:T(8,128)(2,1)} %param.16), kind=kOutput, calls=%fused_computation.8 | convolution fusion | flops 269484032 | bytes 4718592 | tf_op jit(solution)/shard_map/thd,hdc->htc/dot_general | solution.py:513
  5.8 2.3 %maximum_maximum_fusion = bf16[16,128,640]{2,1,0:T(8,128)(2,1)S(1)} fusion(bf16[16,128,64]{2,1,0:T(8,128)(2,1)S(1)} %bitcast.37, bf16[16,128,512]{2,1,0:T(8,128)(2,1)} %convolution_convert_fusion, bf16[640]{0:T(1024)(128)(2,1)S(1)} %pad.22.clone), kind=kLoop, calls=%fused_computation.6 | loop fusion | flops 7864320 | bytes 4982016 | tf_op jit(solution)/shard_map/concatenate | solution.py:517
  8.0 1.8 constant_dynamic-slice_fusion.1
  9.8 8.8 %collective-permute-start.2 = (bf16[16,64,640]{2,1,0:T(8,128)(2,1)}, bf16[16,64,640]{2,1,0:T(8,128)(2,1)}, u32[]{:S(2)}, u32[]{:S(2)}) collective-permute-start(bf16[16,64,640]{2,1,0:T(8,128)(2,1)} %get-tuple-element.63), channel_id=1, source_target_pairs={{0,1},{1,0},{2,3},{3,2},{4,5},{5,4},{6,7},{7,6},{8,9},{9,8},{10,11... | collective-permute-start | bytes 3932168 | tf_op jit(solution)/shard_map/ppermute | solution.py:522
  18.6 1.9 collective-permute-start
  20.5 1.9 collective-permute-start.1
  22.7 0.6 dynamic_slice.36
  24.2 0.9 dynamic-slice_bitcast_fusion
  25.1 0.8 dynamic-slice_bitcast_fusion.1
  26.2 0.3 scatter.15
  26.5 0.3 scatter.16
  26.8 0.3 scatter.19.tab_ref
  27.1 79.4 %fetch_keys.1 = (bf16[32,64,768]{2,1,0:T(8,128)(2,1)S(1)}, s32[4,8,128]{2,1,0:T(8,128)S(1)}) custom-call(s32[8,128]{1,0:T(8,128)S(1)} %scatter.19.tab_ref, bf16[8,16,384]{2,1,0:T(8,128)(2,1)S(1)} %fusion.7.own_ref), custom_call_target="tpu_custom_call" | custom-call | tf_op jit(solution)/shard_map/fetch_keys/pallas_call | solution.py:164
  106.6 1.3 fusion
  108.3 1.6 pad_maximum_fusion.q_ref
  109.9 22.4 %attend.1.prob_ref = f32[64,2048]{1,0:T(8,128)S(1)} custom-call(bf16[32,64,640]{2,1,0:T(8,128)(2,1)S(1)} %pad_maximum_fusion.q_ref, bf16[2048,768]{1,0:T(8,128)(2,1)S(1)} %bitcast.34, f32[64,2048]{1,0:T(8,128)S(1)} %broadcast_select_fusion.bias_ref), custom_call_target="tpu_custom_call" | custom-call | tf_op jit(solution)/shard_map/attend/pallas_call | solution.py:226
  132.3 8.1 %sum_target.1 = f32[16,2048]{1,0:T(8,128)S(1)} custom-call(f32[64,2048]{1,0:T(8,128)S(1)} %attend.1.prob_ref), custom_call_target="tpu_custom_call" | custom-call | tf_op jit(solution)/shard_map/sum_target/pallas_call | solution.py:290
  140.5 1.0 fusion.1
  141.5 6.4 %collective-permute-start.3 = (f32[16,64]{1,0:T(8,128)S(1)}, f32[16,64]{1,0:T(8,128)S(1)}, u32[]{:S(2)}, u32[]{:S(2)}) collective-permute-start(f32[16,64]{1,0:T(8,128)S(1)} %fusion.1), channel_id=1, source_target_pairs={{0,0},{1,4},{2,1},{3,5},{4,2},{5,6},{6,3},{7,7},{8,8},{9,12},{10,9... | collective-permute-start | bytes 12296 | tf_op jit(solution)/shard_map/ppermute | solution.py:553
  147.9 1.8 fusion.2
  149.7 43.3 %give_back.1 = f32[8,64,128]{2,1,0:T(8,128)S(1)} custom-call(s32[4,8,128]{2,1,0:T(8,128)S(1)} %get-tuple-element.52.tabs_ref, f32[32,64,128]{2,1,0:T(8,128)S(1)} %bitcast.35), custom_call_target="tpu_custom_call" | custom-call | tf_op jit(solution)/shard_map/give_back/pallas_call | solution.py:426
  193.0 0.7 copy.23
  193.7 0.6 copy.24
  (35 shorter events, 1.5 us)
Async XLA Ops:
  0.6 1.6 copy-start
  0.6 4.7 %slice-start = ((bf16[128,16,192]{0,2,1:T(8,128)(2,1)}), bf16[128,16,64]{0,2,1:T(8,128)(2,1)S(1)}, s32[]{:S(2)}) async-start(bf16[128,16,192]{0,2,1:T(8,128)(2,1)} %param.16), calls=%async_computation | async-start | bytes 524288 | tf_op jit(solution)/shard_map/slice | solution.py:516
  5.8 14.7 %copy-start.3 = (f32[16,64]{1,0:T(8,128)S(1)}, f32[16,64]{1,0:T(8,128)}, u32[]{:S(2)}) copy-start(f32[16,64]{1,0:T(8,128)} %param.19) | copy-start | bytes 12292
  5.8 16.7 %copy-start.2 = (s32[2,32]{1,0:T(2,128)S(1)}, s32[2,32]{1,0:T(2,128)}, u32[]{:S(2)}) copy-start(s32[2,32]{1,0:T(2,128)} %param.23) | copy-start | bytes 772
  5.8 16.9 %copy-start.4 = (s32[2]{0:T(128)S(1)}, s32[2]{0:T(128)}, u32[]{:S(2)}) copy-start(s32[2]{0:T(128)} %param.22) | copy-start | bytes 28
  9.8 98.5 %collective-permute-start.2 = (bf16[16,64,640]{2,1,0:T(8,128)(2,1)}, bf16[16,64,640]{2,1,0:T(8,128)(2,1)}, u32[]{:S(2)}, u32[]{:S(2)}) collective-permute-start(bf16[16,64,640]{2,1,0:T(8,128)(2,1)} %get-tuple-element.63), channel_id=1, source_target_pairs={{0,1},{1,0},{2,3},{3,2},{4,5},{5,4},{6,7},{7,6},{8,9},{9,8},{10,11... | collective-permute-start | bytes 3932168 | tf_op jit(solution)/shard_map/ppermute | solution.py:522
  18.6 88.0 %collective-permute-start = (bf16[16,64,128]{2,1,0:T(8,128)(2,1)}, bf16[16,64,128]{2,1,0:T(8,128)(2,1)S(1)}, u32[]{:S(2)}, u32[]{:S(2)}) collective-permute-start(bf16[16,64,128]{2,1,0:T(8,128)(2,1)} %param.18), channel_id=1, source_target_pairs={{0,0},{4,1},{1,2},{5,3},{2,4},{6,5},{3,6},{7,7},{8,8},{12,9},{9,10... | collective-permute-start | bytes 786440 | tf_op jit(solution)/shard_map/ppermute | solution.py:511
  20.5 86.0 %collective-permute-start.1 = (f32[16,64]{1,0:T(8,128)S(1)}, f32[16,64]{1,0:T(8,128)S(1)}, u32[]{:S(2)}, u32[]{:S(2)}) collective-permute-start(f32[16,64]{1,0:T(8,128)S(1)} %copy-done.3), channel_id=1, source_target_pairs={{0,0},{4,1},{1,2},{5,3},{2,4},{6,5},{3,6},{7,7},{8,8},{12,9},{9,10... | collective-permute-start | bytes 12296 | tf_op jit(solution)/shard_map/ppermute | solution.py:512
  106.6 1.7 copy-start.1
  141.5 51.5 %collective-permute-start.3 = (f32[16,64]{1,0:T(8,128)S(1)}, f32[16,64]{1,0:T(8,128)S(1)}, u32[]{:S(2)}, u32[]{:S(2)}) collective-permute-start(f32[16,64]{1,0:T(8,128)S(1)} %fusion.1), channel_id=1, source_target_pairs={{0,0},{1,4},{2,1},{3,5},{4,2},{5,6},{6,3},{7,7},{8,8},{9,12},{10,9... | collective-permute-start | bytes 12296 | tf_op jit(solution)/shard_map/ppermute | solution.py:553

commit v3 on v2

v3 whole, which is shorter than its diff:
```python
import functools

import jax
import jax.numpy as jnp
from jax import lax
from jax.experimental import pallas as pl
from jax.experimental.pallas import tpu as pltpu
from jax.sharding import PartitionSpec as P

MESH = pl.DeviceIdType.MESH
X = 4
CORES = 2
LANES = 128


def remote(src, dst, s_sem, r_sem, device):
    return pltpu.make_async_remote_copy(
        src_ref=src, dst_ref=dst, send_sem=s_sem, recv_sem=r_sem, device_id=device, device_id_type=MESH
    )


def enter(peers):
    barrier = pltpu.get_barrier_semaphore()
    for peer in peers:
        pl.semaphore_signal(barrier, inc=1, device_id=peer, device_id_type=MESH)
    pl.semaphore_wait(barrier, len(peers))


def y_sides(ys):
    head = lax.axis_index("head")
    y, c = head // CORES, head % CORES
    step = 1 - 2 * c
    return y, c, lax.rem(y + step + ys, ys), lax.rem(y - step + ys, ys), lax.rem(y + 2, ys)


def attend_kernel(
    zs, ys, scale, heads_total,
    tab_ref, own_ref, q_ref, up_ref, bias_ref,
    target_ref, index_keys_ref, tabs_ref,
    tabs_v, tabs_s, z_low, z_high, x_out, x_in, x_all, keys, query, query_out,
    logits_a, logits_b, expo, top, total, part, middle, t_in,
    zs_sem, zr_sem, xs_sem, xr_sem, ts_sem, tr_sem, ys_sem, yr_sem, qs_sem, qr_sem, ps_sem, pr_sem, local_sem,
):
    ctx = lax.axis_index("ctx")
    z, x = ctx // X, ctx % X
    y, c, y_a, y_b, y_far = y_sides(ys)
    head = y * CORES + c
    own_blocks, rows, half = own_ref.shape
    picks, block_len, full = keys.shape
    local_heads, unused, nope = up_ref.shape[0], up_ref.shape[2], up_ref.shape[1]
    latent = up_ref.shape[2]
    width = query.shape[2]
    steps = zs // 2
    halves = 2
    part_blocks = own_blocks // halves
    z_up = (lax.rem(z + 1, zs) * X + x, head)
    z_down = (lax.rem(z + zs - 1, zs) * X + x, head)
    to_a, to_b = (ctx, y_a * CORES + c), (ctx, y_b * CORES + c)
    to_core = (ctx, y * CORES + 1 - c)
    x_peers = []
    for dx in range(X):
        for dc in range(CORES):
            if dx or dc:
                tx, tc = lax.rem(x + dx, X), lax.rem(c + dc, CORES)
                x_peers.append((dx, dc, tx, tc, (z * X + tx, y * CORES + tc)))
    tabs_v[x] = tab_ref[...]
    enter([z_up, z_down, to_a, to_b] + [p[4] for p in x_peers])
    pending = []

    def start(copy):
        copy.start()
        pending.append(copy)

    def piece(direction, k, i):
        span = pl.ds(i * part_blocks, part_blocks)
        if k == 0:
            return own_ref.at[span]
        if direction == 0 or k == steps:
            return z_low[k - 1].at[span]
        return z_high[k - 1].at[span]

    def z_copy(direction, k, i):
        return remote(
            piece(direction, k - 1, i), piece(direction, k, i),
            zs_sem.at[direction, k - 1, i], zr_sem.at[direction, k - 1, i],
            z_up if direction == 0 else z_down,
        )

    def z_lanes(k):
        return [(d, i) for i in range(halves) for d in range(2) if k < steps or (i == d)]

    for d, i in z_lanes(1):
        start(z_copy(d, 1, i))
    for dx in range(1, X):
        tx = lax.rem(x + dx, X)
        start(remote(tabs_v.at[x], tabs_v.at[x], ts_sem.at[dx - 1], tr_sem.at[dx - 1], (z * X + tx, head)))
    for dx in range(1, X):
        fx = lax.rem(x + X - dx, X)
        remote(tabs_v.at[fx], tabs_v.at[fx], ts_sem.at[dx - 1], tr_sem.at[dx - 1], z_up).wait_recv()
    to_scalar = pltpu.make_async_copy(tabs_v, tabs_s, local_sem)
    to_scalar.start()
    to_scalar.wait()
    tabs_ref[...] = tabs_v[...]

    def sources(k):
        if k == 0:
            return [(own_ref, 0)]
        if k == steps:
            return [(z_low[k - 1], zs - k)]
        return [(z_low[k - 1], zs - k), (z_high[k - 1], k)]

    def x_step(k):
        found = [(ref, rel, lax.rem(z + rel, zs) * X + x) for ref, rel in sources(k)]
        for n, (dx, dc, tx, tc, device) in enumerate(x_peers):
            for i, (ref, rel, shard) in enumerate(found):
                x_out[k, n, i] = ref[tabs_s[tx, tc, shard]]
            span = pl.ds(0, len(found))
            start(remote(x_out.at[k, n, span], x_in.at[k, n, span], xs_sem.at[k, n], xr_sem.at[k, n], device))
        for ref, rel, shard in found:
            x_all[rel * X + x, c] = ref[tabs_s[x, c, shard]]

    def x_finish(k):
        for n, (dx, dc, tx, tc, device) in enumerate(x_peers):
            fx, fc = lax.rem(x + X - dx, X), lax.rem(c + dc, CORES)
            span = pl.ds(0, len(sources(k)))
            remote(x_out.at[k, n, span], x_in.at[k, n, span], xs_sem.at[k, n], xr_sem.at[k, n], device).wait_recv()
            for i, (unused_ref, rel) in enumerate(sources(k)):
                x_all[rel * X + fx, fc] = x_in[k, n, i]

    chunks = ys_sem.shape[1]
    chunk = picks // chunks

    def y_copy(kind, owner, j, device):
        ref = keys.at[pl.ds(j * chunk, chunk), pl.ds(pl.multiple_of(owner * rows, rows), rows)]
        return remote(ref, ref, ys_sem.at[kind, j], yr_sem.at[kind, j], device)

    def y_start(j):
        def place(m, carry):
            slot = tabs_s[x, CORES + c, m]
            for fc in range(CORES):
                keys[m, pl.ds(pl.multiple_of(y * rows, rows), rows), fc * half : (fc + 1) * half] = x_all[slot, fc]
            return carry

        lax.fori_loop(j * chunk, (j + 1) * chunk, place, 0)
        start(y_copy(0, y, j, to_a))
        start(y_copy(1, y, j, to_b))

    def y_forward(j):
        y_copy(0, y_b, j, to_a).wait_recv()
        y_copy(2, y_b, j, to_a).start()

    def make_query(h):
        for mine, ref in ((True, query), (False, query_out)):
            at = pl.ds(pl.multiple_of((c if mine else 1 - c) * block_len, block_len), block_len)
            ref[h, :, :latent] = jnp.dot(
                q_ref[h, at, :nope], up_ref[h], preferred_element_type=jnp.float32
            ).astype(query.dtype)
            ref[h, :, latent:] = q_ref[h, at, nope:]

    swap = remote(query_out, query.at[pl.ds(local_heads, local_heads)], qs_sem, qr_sem, to_core)
    first = steps + 1 - chunks
    per_step = local_heads // steps
    x_step(0)
    for k in range(1, steps + 1):
        for h in range((k - 1) * per_step, k * per_step):
            make_query(h)
        if k == steps:
            start(swap)
        for d, i in z_lanes(k):
            z_copy(d, k, i).wait_recv()
            if (d, i) in z_lanes(k + 1) and k < steps:
                start(z_copy(d, k + 1, i))
        x_step(k)
        x_finish(k - 1)
        if k - 1 >= first:
            y_start(k - 1 - first)
        if k - 2 >= first:
            y_forward(k - 2 - first)
    x_finish(steps)
    y_start(chunks - 1)
    y_forward(chunks - 2)
    swap.wait_recv()

    group = logits_a.shape[0] // block_len
    groups = query.shape[0] // group
    pieces = chunk * block_len // LANES

    def dot(j, g, dst):
        block = query[pl.ds(g * group, group)].reshape(group * block_len, width)
        these = keys[pl.ds(j * chunk, chunk)].reshape(chunk * block_len, full)[:, :width]
        dst[...] = lax.dot_general(
            block, these, (((1,), (1,)), ((), ())), preferred_element_type=jnp.float32
        )

    def soften(j, g, src):
        for i in range(block_len // 8):
            bias = bias_ref[j, i * 8 : (i + 1) * 8, :]
            for h in range(group):
                value = src[h * block_len + i * 8 : h * block_len + i * 8 + 8, :] * scale + bias
                cuts = [value[:, n * LANES : (n + 1) * LANES] for n in range(pieces)]
                high = functools.reduce(jnp.maximum, cuts)
                high = jnp.maximum(high, -1e30)
                raised = [jnp.exp2(cut - high) for cut in cuts]
                at = pl.ds(pl.multiple_of((g * group + h) * block_len + i * 8, 8), 8)
                for n in range(pieces):
                    expo[j, at, n * LANES : (n + 1) * LANES] = raised[n]
                top[j, at, :] = high
                total[j, at, :] = functools.reduce(jnp.add, raised)

    def attend_chunk(j, carry):
        @pl.when(j == 1)
        def forward_last():
            y_forward(chunks - 1)

        y_copy(1, y_a, j, to_a).wait_recv()
        y_copy(2, y_far, j, to_a).wait_recv()
        dot(j, 0, logits_a)

        def pair(p, inner):
            dot(j, 2 * p + 1, logits_b)
            soften(j, 2 * p, logits_a)
            dot(j, lax.rem(2 * p + 2, groups), logits_a)
            soften(j, 2 * p + 1, logits_b)
            return inner

        lax.fori_loop(0, groups // 2, pair, 0)
        return carry

    lax.fori_loop(0, chunks, attend_chunk, 0)
    index_keys_ref[...] = keys[:, :, width:]

    def sum_heads(at):
        def one(h, sums):
            here = pl.ds(pl.multiple_of(h * block_len + at, 8), 8)
            highs = [top[j, here, :] for j in range(chunks)]
            high = jnp.max(functools.reduce(jnp.maximum, highs), axis=1, keepdims=True)
            factors = [jnp.exp2(value - high) for value in highs]
            mass = functools.reduce(
                jnp.add, [total[j, here, :] * factors[j] for j in range(chunks)]
            )
            share = 1.0 / jnp.sum(mass, axis=1, keepdims=True)
            sums = list(sums)
            for j in range(chunks):
                factor = factors[j] * share
                for n in range(pieces):
                    sums[j * pieces + n] += expo[j, here, n * LANES : (n + 1) * LANES] * factor
            return tuple(sums)

        zero = jnp.zeros((8, LANES), jnp.float32)
        return lax.fori_loop(0, query.shape[0], one, (zero,) * (chunks * pieces), unroll=4)

    def quarter(owner, dst):
        for i in range(rows // 8):
            sums = sum_heads(pl.multiple_of(owner * rows + i * 8, 8))
            for n, value in enumerate(sums):
                dst[i * 8 : (i + 1) * 8, n * LANES : (n + 1) * LANES] = value

    quarter(y_far, part.at[0])
    far = remote(part.at[0], t_in.at[0], ps_sem.at[0], pr_sem.at[0], to_a)
    start(far)
    quarter(y_b, part.at[1])
    near = remote(part.at[1], t_in.at[1], ps_sem.at[1], pr_sem.at[1], to_b)
    start(near)
    quarter(y_a, middle)
    far.wait_recv()
    part[2] = middle[...] + t_in[0]
    last = remote(part.at[2], t_in.at[2], ps_sem.at[2], pr_sem.at[2], to_a)
    start(last)
    quarter(y, middle)
    near.wait_recv()
    last.wait_recv()
    target_ref[...] = (middle[...] + t_in[1] + t_in[2]) * (1.0 / heads_total)
    for j in range(chunks):
        y_copy(2, y_b, j, to_a).wait_send()
    for copy in pending:
        copy.wait_send()


def attend(table, own, query, up_weight, bias, zs, ys, picks, block_len, heads_total, scale):
    own_blocks, rows, half = own.shape
    local_heads, unused, q_width = query.shape
    nope, latent = up_weight.shape[1:]
    width = latent + q_width - nope
    full = half * CORES
    heads = local_heads * CORES
    steps = zs // 2
    peers = X * CORES - 1
    chunks = bias.shape[0]
    chunk_keys = bias.shape[2]
    group = 8
    keep = own.dtype
    single = jnp.float32
    dma = pltpu.SemaphoreType.DMA
    return pl.pallas_call(
        functools.partial(attend_kernel, zs, ys, scale, heads_total),
        out_shape=(
            jax.ShapeDtypeStruct((rows, picks * block_len), single),
            jax.ShapeDtypeStruct((picks, block_len, full - width), keep),
            jax.ShapeDtypeStruct((X, 8, LANES), jnp.int32),
        ),
        in_specs=[pl.BlockSpec(memory_space=pltpu.VMEM)] * 5,
        out_specs=[pl.BlockSpec(memory_space=pltpu.VMEM)] * 3,
        scratch_shapes=[
            pltpu.VMEM((X, 8, LANES), jnp.int32),
            pltpu.SMEM((X, 8, LANES), jnp.int32),
            [pltpu.VMEM((own_blocks, rows, half), keep) for k in range(steps)],
            [pltpu.VMEM((own_blocks, rows, half), keep) for k in range(steps - 1)],
            pltpu.VMEM((steps + 1, peers, 2, rows, half), keep),
            pltpu.VMEM((steps + 1, peers, 2, rows, half), keep),
            pltpu.VMEM((zs * X, CORES, rows, half), keep),
            pltpu.VMEM((picks, block_len, full), keep),
            pltpu.VMEM((heads, block_len, width), keep),
            pltpu.VMEM((local_heads, block_len, width), keep),
            pltpu.VMEM((group * block_len, chunk_keys), single),
            pltpu.VMEM((group * block_len, chunk_keys), single),
            pltpu.VMEM((chunks, heads * block_len, chunk_keys), single),
            pltpu.VMEM((chunks, heads * block_len, LANES), single),
            pltpu.VMEM((chunks, heads * block_len, LANES), single),
            pltpu.VMEM((3, rows, picks * block_len), single),
            pltpu.VMEM((rows, picks * block_len), single),
            pltpu.VMEM((3, rows, picks * block_len), single),
            dma((2, steps, 2)), dma((2, steps, 2)),
            dma((steps + 1, peers)), dma((steps + 1, peers)),
            dma((X - 1,)), dma((X - 1,)),
            dma((3, chunks)), dma((3, chunks)),
            dma, dma, dma((3,)), dma((3,)), dma,
        ],
        compiler_params=pltpu.CompilerParams(
            collective_id=0, has_side_effects=True, vmem_limit_bytes=56 * 2**20
        ),
        name="attend",
    )(table, own, query, up_weight, bias)


def return_kernel(
    zs, ys, tabs_ref, part_ref, out_ref,
    y_out, y_in, quarter, x_out, x_in, z_out, z_in, mine, theirs,
    ys_sem, yr_sem, xs_sem, xr_sem, zs_sem, zr_sem, cs_sem, cr_sem, os_sem, or_sem,
):
    ctx = lax.axis_index("ctx")
    z, x = ctx // X, ctx % X
    y, c, y_a, y_b, y_far = y_sides(ys)
    head = y * CORES + c
    picks, block_len, width = part_ref.shape
    own_blocks = out_ref.shape[0]
    rows = block_len // ys
    slots = X * rows
    to_a, to_b, to_far = (ctx, y_a * CORES + c), (ctx, y_b * CORES + c), (ctx, y_far * CORES + c)
    to_core = (ctx, y * CORES + 1 - c)
    x_peers = [(lax.rem(x + d, X), (z * X + lax.rem(x + d, X), head)) for d in range(1, X)]
    z_peers = [(lax.rem(z + d, zs), (lax.rem(z + d, zs) * X + x, head)) for d in range(1, zs)]
    enter([to_a, to_b, to_far, to_core] + [p[1] for p in x_peers] + [p[1] for p in z_peers])

    def span(k):
        return pl.ds(pl.multiple_of(k * rows, rows), rows)

    y_out[0] = part_ref[:, span(y_far), :].astype(y_out.dtype)
    far = remote(y_out.at[0], y_in.at[0], ys_sem.at[0], yr_sem.at[0], to_a)
    far.start()
    y_out[1] = part_ref[:, span(y_b), :].astype(y_out.dtype)
    near = remote(y_out.at[1], y_in.at[1], ys_sem.at[1], yr_sem.at[1], to_b)
    near.start()
    far.wait_recv()
    y_out[2] = (part_ref[:, span(y_a), :] + y_in[0].astype(jnp.float32)).astype(y_out.dtype)
    last = remote(y_out.at[2], y_in.at[2], ys_sem.at[2], yr_sem.at[2], to_a)
    last.start()
    near.wait_recv()
    last.wait_recv()
    quarter[...] = (
        part_ref[:, span(y), :] + y_in[1].astype(jnp.float32) + y_in[2].astype(jnp.float32)
    )

    def choose(tx, dst):
        def body(owner, carry):
            place = tabs_ref[x, 3 * CORES + c, owner * X + tx]
            value = quarter[jnp.maximum(place - 1, 0)]
            dst[owner] = jnp.where(place > 0, value, 0.0).astype(dst.dtype)
            return carry

        lax.fori_loop(0, zs, body, 0)

    x_copies = []
    for n, (tx, device) in enumerate(x_peers):
        choose(tx, x_out.at[n])
        copy = remote(x_out.at[n], x_in.at[x], xs_sem.at[n], xr_sem.at[n], device)
        copy.start()
        x_copies.append(copy)
    choose(x, x_in.at[x])
    for n in range(X - 1):
        fx = lax.rem(x + X - n - 1, X)
        remote(x_out.at[n], x_in.at[fx], xs_sem.at[n], xr_sem.at[n], to_a).wait_recv()

    line = lax.broadcasted_iota(jnp.int32, (rows, width), 0)

    def gather(owner, dst):
        ids = jnp.zeros((rows, width), jnp.float32)
        for fx in range(X):
            dst[fx * rows : (fx + 1) * rows] = x_in[fx, owner]
            block = tabs_ref[fx, 2 * CORES + c, owner * X + x]
            ids = jnp.where(line == fx, block.astype(jnp.float32), ids)
        dst[slots : slots + rows] = ids.astype(dst.dtype)

    z_copies = []
    order = sorted(range(1, zs), key=lambda d: -min(d, zs - d))
    for d in order:
        tz, device = z_peers[d - 1]
        gather(tz, z_out.at[d - 1])
        copy = remote(z_out.at[d - 1], z_in.at[z], zs_sem.at[d - 1], zr_sem.at[d - 1], device)
        copy.start()
        z_copies.append(copy)
    gather(z, z_in.at[z])
    for d in order:
        fz = lax.rem(z + zs - d, zs)
        remote(z_out.at[d - 1], z_in.at[fz], zs_sem.at[d - 1], zr_sem.at[d - 1], to_a).wait_recv()

    def add(fz, totals):
        ids = z_in[fz, slots : slots + rows].astype(jnp.float32)
        totals = list(totals)
        for fx in range(X):
            value = z_in[fz, fx * rows : (fx + 1) * rows].astype(jnp.float32)
            block = jnp.broadcast_to(ids[fx : fx + 1], value.shape)
            for r in range(own_blocks):
                totals[r] = totals[r] + jnp.where(block == r + 1.0, value, 0.0)
        return tuple(totals)

    totals = lax.fori_loop(
        0, zs, add, tuple(jnp.zeros((rows, width), jnp.float32) for r in range(own_blocks))
    )
    for r in range(own_blocks):
        mine[r] = totals[r]
    core = remote(mine, theirs, cs_sem, cr_sem, to_core)
    core.start()
    core.wait_recv()
    out_ref[:, span(y), :] = mine[...] + theirs[...]
    o_copies = []
    for n, device in enumerate((to_a, to_b, to_far)):
        ref = out_ref.at[:, span(y), :]
        copy = remote(ref, ref, os_sem.at[n], or_sem.at[n], device)
        copy.start()
        o_copies.append(copy)
    for n, fy in enumerate((y_b, y_a, y_far)):
        ref = out_ref.at[:, span(fy), :]
        remote(ref, ref, os_sem.at[n], or_sem.at[n], to_a).wait_recv()
    for copy in [far, near, last, core] + x_copies + z_copies + o_copies:
        copy.wait_send()


def give_back(tables, key_part, zs, ys, own_blocks):
    picks, block_len, width = key_part.shape
    rows = block_len // ys
    half = jnp.bfloat16
    dma = pltpu.SemaphoreType.DMA
    return pl.pallas_call(
        functools.partial(return_kernel, zs, ys),
        out_shape=jax.ShapeDtypeStruct((own_blocks, block_len, width), jnp.float32),
        in_specs=[
            pl.BlockSpec(memory_space=pltpu.SMEM),
            pl.BlockSpec(memory_space=pltpu.VMEM),
        ],
        out_specs=pl.BlockSpec(memory_space=pltpu.VMEM),
        scratch_shapes=[
            pltpu.VMEM((3, picks, rows, width), half),
            pltpu.VMEM((3, picks, rows, width), half),
            pltpu.VMEM((picks, rows, width), jnp.float32),
            pltpu.VMEM((X - 1, zs, rows, width), half),
            pltpu.VMEM((X, zs, rows, width), half),
            pltpu.VMEM((zs - 1, (X + 1) * rows, width), half),
            pltpu.VMEM((zs, (X + 1) * rows, width), half),
            pltpu.VMEM((own_blocks, rows, width), jnp.float32),
            pltpu.VMEM((own_blocks, rows, width), jnp.float32),
            dma((3,)), dma((3,)), dma((X - 1,)), dma((X - 1,)), dma((zs - 1,)), dma((zs - 1,)),
            dma, dma, dma((3,)), dma((3,)),
        ],
        compiler_params=pltpu.CompilerParams(
            collective_id=2, has_side_effects=True, vmem_limit_bytes=40 * 2**20
        ),
        name="give_back",
    )(tables, key_part)


def masked_softmax(values, allowed):
    shifted = jnp.where(allowed, values, -jnp.inf)
    row_max = jnp.max(shifted, axis=-1, keepdims=True)
    expo = jnp.exp(shifted - row_max)
    return expo / jnp.sum(expo, axis=-1, keepdims=True)


def local(
    queries,
    up_weight,
    index_query,
    index_weight,
    cache_entry,
    index_key,
    block_position,
    picked_blocks,
):
    owners = lax.axis_size("ctx")
    head_devices = lax.axis_size("head")
    zs, ys = owners // X, head_devices // CORES
    ctx = lax.axis_index("ctx")
    head = lax.axis_index("head")
    y, c = head // CORES, head % CORES
    query_count, picks = picked_blocks.shape
    own_blocks, unused, block_len, entry_width = cache_entry.shape
    index_width = index_key.shape[3]
    key_count = picks * block_len
    rows = block_len // ys
    local_heads = queries.shape[1]
    pad_width = -(-entry_width // LANES) * LANES
    full_width = pad_width + index_width
    half = full_width // CORES

    shard_of = picked_blocks % owners
    behind = (shard_of // X - ctx // X + zs) % zs
    distance = jnp.minimum(behind, zs - behind) * picks + jnp.arange(picks)[None, :]
    rank = jnp.sum((distance[:, None, :] < distance[:, :, None]).astype(jnp.int32), axis=2)
    ordered = rank[:, :, None] == jnp.arange(picks)[None, None, :]
    blocks = jnp.sum(jnp.where(ordered, picked_blocks[:, :, None], 0), axis=1)
    owner_of = blocks % owners
    slot = (owner_of // X - ctx // X + zs) % zs * X + owner_of % X

    matched = owner_of[:, :, None] == jnp.arange(owners)[None, None, :]
    request = jnp.sum(jnp.where(matched, blocks[:, :, None] // owners + 1, 0), axis=1)
    place = jnp.sum(jnp.where(matched, jnp.arange(1, picks + 1)[None, :, None], 0), axis=1)
    wide = [(0, 0), (0, LANES - owners)]
    table = jnp.concatenate(
        [
            jnp.pad(jnp.maximum(request - 1, 0), wide),
            jnp.pad(slot, [(0, 0), (0, LANES - picks)]),
            jnp.pad(request, wide),
            jnp.pad(place, wide),
        ],
        axis=0,
    )

    own = jnp.concatenate(
        [
            lax.dynamic_slice_in_dim(cache_entry[:, 0], y * rows, rows, 1),
            jnp.zeros((own_blocks, rows, pad_width - entry_width), cache_entry.dtype),
            lax.dynamic_slice_in_dim(index_key[:, 0], y * rows, rows, 1),
        ],
        axis=2,
    )
    own = lax.dynamic_slice_in_dim(own, c * half, half, 2)

    to_row = [((i % CORES) * ys + i // CORES, i) for i in range(head_devices)]
    my_index_query = lax.ppermute(index_query, "head", to_row)
    my_index_weight = lax.ppermute(index_weight, "head", to_row)
    heads_first = jnp.pad(
        jnp.transpose(queries, (1, 0, 2)), [(0, 0), (0, 0), (0, pad_width - entry_width)]
    )

    my_picks = lax.dynamic_index_in_dim(blocks, c, 0, keepdims=False)
    my_position = lax.dynamic_index_in_dim(block_position, c, 0, keepdims=False)
    key_place = (my_picks[:, None] * block_len + jnp.arange(block_len)[None, :]).reshape(key_count)
    query_place = my_position * block_len + jnp.arange(block_len)
    allowed = key_place[None, :] <= query_place[:, None]
    chunks = 4
    chunk_place = key_place.reshape(chunks, 1, key_count // chunks)
    bias = jnp.where(chunk_place <= query_place[None, :, None], 0.0, -jnp.inf).astype(jnp.float32)
    scale = queries.shape[2] ** (-0.5) * 1.4426950408889634
    target, index_keys, tables = attend(
        table, own, heads_first, up_weight, bias,
        zs, ys, picks, block_len, local_heads * head_devices, scale,
    )
    index_keys = index_keys.reshape(key_count, index_width)
    my_allowed = lax.dynamic_slice_in_dim(allowed, y * rows, rows, 0)
    index_scale = index_width ** (-0.5)
    raw = jnp.einsum("ijd,sd->ijs", my_index_query, index_keys, preferred_element_type=jnp.float32)
    act = jnp.maximum(raw, 0.0) * index_scale
    score = jnp.sum(my_index_weight[:, :, None] * act, axis=1)
    soft = masked_softmax(score, my_allowed)
    score_grad = jnp.where(my_allowed, soft - target, 0.0)
    weight_part = jnp.sum(score_grad[:, None, :] * act, axis=2)
    coefficient = jnp.where(
        raw > 0, score_grad[:, None, :] * my_index_weight[:, :, None] * index_scale, 0.0
    ).astype(jnp.bfloat16)
    key_part = jnp.einsum(
        "ijs,ijd->sd", coefficient, my_index_query, preferred_element_type=jnp.float32
    )
    weight_grad = lax.ppermute(weight_part, "head", [(b, a) for a, b in to_row])

    key_grad = give_back(
        tables, key_part.reshape(picks, block_len, index_width), zs, ys, own_blocks
    ).reshape(own_blocks, 1, block_len, index_width)
    return (key_grad, weight_grad)


def solution(mesh):
    return jax.shard_map(
        local,
        mesh=mesh,
        in_specs=(
            P("ctx", "head", None),
            P("head", None, None),
            P(("ctx", "head"), None, None),
            P(("ctx", "head"), None),
            P(None, "ctx", None, None),
            P(None, "ctx", None, None),
            P("ctx"),
            P("ctx", None),
        ),
        out_specs=(P(None, "ctx", None, None), P(("ctx", "head"), None)),
        check_vma=False,
    )
```

time: 195 us -> 163 us (0.84)
  Pallas kernels: 153 us -> 134 us
  starting transfers between devices: 19 us -> 11.4 us
  matrix products: 6.25 us -> 4.12 us
    pallas_call x3 -> x1, Pallas kernels: 110 us -> 88 us  [attend(): pl.pallas_call(functools.partial(attend_kernel, zs, ys, scale, heads_tota...]
    ppermute x1 -> x0, starting transfers between devices: 8.77 us -> none  [local(): lax.ppermute(other, 'head', swap)]
    ppermute x1, starting transfers between devices: 6.41 us -> 3.15 us  [local(): weight_grad = lax.ppermute(weight_part, 'head', [(b, a) for a, b in to_row])]
    concatenate x2 -> x1, other arithmetic: 3.85 us -> 0.6 us  [local(): jnp.concatenate([jnp.pad(jnp.maximum(request - 1, 0), wide), jnp.pad(slot...]
    dot_general x1 -> x0, matrix products: 3.15 us -> none  [local(): jnp.einsum('thd,hdc->htc', queries[:, :, :nope], up_weight, preferred_ele...]
    ppermute x1, starting transfers between devices: 1.92 us -> 4.73 us  [local(): my_index_weight = lax.ppermute(index_weight, 'head', to_row)]
    pallas_call x1, Pallas kernels: 43.3 us -> 45.7 us  [give_back(): pl.pallas_call(functools.partial(return_kernel, zs, ys), out_shape=jax.Sh...]
  transfers between devices with their start and end apart: 4 -> 3, of which waited for: 0 -> 0; matrix products, arithmetic and copies ran while one was open for 4% -> 7% of each run, Pallas kernels for 63% -> 82%
where the time goes in v3:
time: 163 us
  Pallas kernels  134 us (82%)
  starting transfers between devices  11.4 us (7%)
  local copies, waits for them, and re-layouts  6.51 us (4%)
  other arithmetic  5.62 us (3%)
  matrix products  4.12 us (3%)
    pallas_call x1, Pallas kernels, attend(): pl.pallas_call(functools.partial(attend_kernel, zs, ys, scale, heads_tota...  88 us
    pallas_call x1, Pallas kernels, give_back(): pl.pallas_call(functools.partial(return_kernel, zs, ys), out_shape=jax.Sh...  45.7 us
    ppermute x1, starting transfers between devices, local(): my_index_weight = lax.ppermute(index_weight, 'head', to_row)  4.73 us
    ppermute x1, starting transfers between devices, local(): my_index_query = lax.ppermute(index_query, 'head', to_row)  3.48 us
  transfers between devices with their start and end apart: 3, of which 0 were waited for; matrix products, arithmetic and copies ran while one was open for 7% of the time, Pallas kernels for 82%

profile of v3, /device:TPU:1, one launch (start us, length us, event | category | flops | bytes accessed | tf_op | source)
XLA Modules:
  0.0 162.8 jit_solution(4898969631254791607)
XLA Ops:
  0.6 4.7 %collective-permute-start.1 = (f32[16,64]{1,0:T(8,128)}, f32[16,64]{1,0:T(8,128)S(1)}, u32[]{:S(2)}, u32[]{:S(2)}) collective-permute-start(f32[16,64]{1,0:T(8,128)} %param.11), channel_id=1, source_target_pairs={{0,0},{4,1},{1,2},{5,3},{2,4},{6,5},{3,6},{7,7},{8,8},{12,9},{9,10... | collective-permute-start | bytes 12296 | tf_op jit(solution)/shard_map/ppermute | solution.py:549
  5.4 3.5 %collective-permute-start = (bf16[16,64,128]{2,1,0:T(8,128)(2,1)}, bf16[16,64,128]{2,1,0:T(8,128)(2,1)S(1)}, u32[]{:S(2)}, u32[]{:S(2)}) collective-permute-start(bf16[16,64,128]{2,1,0:T(8,128)(2,1)} %param.10), channel_id=1, source_target_pairs={{0,0},{4,1},{1,2},{5,3},{2,4},{6,5},{3,6},{7,7},{8,8},{12,9},{9,10... | collective-permute-start | bytes 786440 | tf_op jit(solution)/shard_map/ppermute | solution.py:548
  8.9 0.7 fusion.8
  9.7 0.2 convert_reduce_fusion
  9.8 0.8 select_reduce_fusion.2
  10.7 1.2 dynamic_slice.30
  12.6 0.1 select_reduce_fusion.1
  13.1 0.8 dynamic-slice_bitcast_fusion.1
  14.0 0.9 compare_select_fusion.bias_ref
  14.9 0.7 fusion.6.own_ref
  15.6 0.6 pad_add_fusion.tab_ref
  16.3 1.4 copy.12
  17.8 1.2 pad.22.q_ref
  19.0 88.0 %attend.1 = (f32[16,2048]{1,0:T(8,128)}, bf16[32,64,128]{2,1,0:T(8,128)(2,1)}, s32[4,8,128]{2,1,0:T(8,128)}) custom-call(s32[8,128]{1,0:T(8,128)} %pad_add_fusion.tab_ref, bf16[8,16,384]{2,1,0:T(8,128)(2,1)} %fusion.6.own_ref, bf16[16,128,256]{2,1,0:T(8,128)(2,1)} %pad.22.q_ref, bf16[16,128,512]{2,1,0:T(8,128)(2,1)} %up_ref.1, ...), custom_call_target="tpu_custom_call" | custom-call | tf_op jit(solution)/shard_map/attend/pallas_call | solution.py:294
  107.0 2.3 %fusion = (f32[16,2048]{1,0:T(8,128)S(1)}, f32[2048,16,64]{0,2,1:T(8,128)S(1)}) fusion(f32[16,64]{1,0:T(8,128)S(1)} %broadcast_multiply_fusion.1, bf16[2048,128,1]{1,0,2:T(8,128)(2,1)} %bitcast.33, bf16[16,64,128]{2,1,0:T(8,128)(2,1)S(1)} %collective-permute-done), kind=kOutput, calls=%fused_computation.2 | convolution fusion | flops 543129600 | bytes 9310208 | tf_op jit(solution)/shard_map/ijd,sd->ijs/dot_general | solution.py:570
  109.4 0.2 fusion.4
  109.6 0.2 fusion.3
  109.8 0.1 broadcast_multiply_fusion
  109.9 1.0 fusion.1
  110.9 3.1 %collective-permute-start.2 = (f32[16,64]{1,0:T(8,128)S(1)}, f32[16,64]{1,0:T(8,128)S(1)}, u32[]{:S(2)}, u32[]{:S(2)}) collective-permute-start(f32[16,64]{1,0:T(8,128)S(1)} %fusion.1), channel_id=1, source_target_pairs={{0,0},{1,4},{2,1},{3,5},{4,2},{5,6},{6,3},{7,7},{8,8},{9,12},{10,9... | collective-permute-start | bytes 12296 | tf_op jit(solution)/shard_map/ppermute | solution.py:582
  114.1 1.8 %fusion.2 = f32[2048,128,1]{1,0,2:T(8,128)S(1)} fusion(bf16[16,64,128]{2,1,0:T(8,128)(2,1)S(1)} %collective-permute-done, f32[2048,16,64]{0,2,1:T(8,128)S(1)} %get-tuple-element.22, f32[16,64]{1,0:T(8,128)S(1)} %collective-permute-done.1, f32[16,2048]{1,0:T(8,128)S(1)} %get-tuple-element.15), kind=kOutput, calls=%fused_computation.5 | convolution fusion | flops 547356672 | bytes 9834496 | tf_op jit(solution)/shard_map/ijs,ijd->sd/dot_general | solution.py:579
  115.9 45.7 %give_back.1 = f32[8,64,128]{2,1,0:T(8,128)S(1)} custom-call(s32[4,8,128]{2,1,0:T(8,128)S(1)} %copy-done.1, f32[32,64,128]{2,1,0:T(8,128)S(1)} %bitcast.30), custom_call_target="tpu_custom_call" | custom-call | tf_op jit(solution)/shard_map/give_back/pallas_call | solution.py:453
  161.5 0.7 copy.16
  162.2 0.6 copy.17
  (27 shorter events, 0.7 us)
Async XLA Ops:
  0.6 13.2 %copy-start = (bf16[8,1,64,576]{3,2,1,0:T(8,128)(2,1)S(1)}, bf16[8,1,64,576]{3,2,1,0:T(8,128)(2,1)}, u32[]{:S(2)}) copy-start(bf16[8,1,64,576]{3,2,1,0:T(8,128)(2,1)} %param.12) | copy-start | bytes 1769476
  0.6 106.4 %collective-permute-start.1 = (f32[16,64]{1,0:T(8,128)}, f32[16,64]{1,0:T(8,128)S(1)}, u32[]{:S(2)}, u32[]{:S(2)}) collective-permute-start(f32[16,64]{1,0:T(8,128)} %param.11), channel_id=1, source_target_pairs={{0,0},{4,1},{1,2},{5,3},{2,4},{6,5},{3,6},{7,7},{8,8},{12,9},{9,10... | collective-permute-start | bytes 12296 | tf_op jit(solution)/shard_map/ppermute | solution.py:549
  5.4 101.7 %collective-permute-start = (bf16[16,64,128]{2,1,0:T(8,128)(2,1)}, bf16[16,64,128]{2,1,0:T(8,128)(2,1)S(1)}, u32[]{:S(2)}, u32[]{:S(2)}) collective-permute-start(bf16[16,64,128]{2,1,0:T(8,128)(2,1)} %param.10), channel_id=1, source_target_pairs={{0,0},{4,1},{1,2},{5,3},{2,4},{6,5},{3,6},{7,7},{8,8},{12,9},{9,10... | collective-permute-start | bytes 786440 | tf_op jit(solution)/shard_map/ppermute | solution.py:548
  107.0 2.8 %copy-start.2 = (f32[16,2048]{1,0:T(8,128)S(1)}, f32[16,2048]{1,0:T(8,128)}, u32[]{:S(2)}) copy-start(f32[16,2048]{1,0:T(8,128)} %get-tuple-element.7) | copy-start | bytes 393220
  110.9 50.6 %collective-permute-start.2 = (f32[16,64]{1,0:T(8,128)S(1)}, f32[16,64]{1,0:T(8,128)S(1)}, u32[]{:S(2)}, u32[]{:S(2)}) collective-permute-start(f32[16,64]{1,0:T(8,128)S(1)} %fusion.1), channel_id=1, source_target_pairs={{0,0},{1,4},{2,1},{3,5},{4,2},{5,6},{6,3},{7,7},{8,8},{9,12},{10,9... | collective-permute-start | bytes 12296 | tf_op jit(solution)/shard_map/ppermute | solution.py:582
  114.1 1.8 %copy-start.1 = (s32[4,8,128]{2,1,0:T(8,128)S(1)}, s32[4,8,128]{2,1,0:T(8,128)}, u32[]{:S(2)}) copy-start(s32[4,8,128]{2,1,0:T(8,128)} %get-tuple-element.5.tabs_ref) | copy-start | bytes 49156

commit v4 on v3

--- a/solution.py
+++ b/solution.py
@@ -11,6 +11,18 @@
 X = 4
 CORES = 2
 LANES = 128
+JUMP = 1
+
+
+def z_plan(steps):
+    jump = min(JUMP, steps)
+    plan = []
+    for hop in range(1, max(jump, steps - jump + 2)):
+        plan.append(
+            ([(hop, hop - 1)] if hop < jump else [])
+            + ([(jump + hop - 1, jump + hop - 2 if hop > 1 else 0)] if jump + hop - 1 <= steps else [])
+        )
+    return plan
 
 
 def remote(src, dst, s_sem, r_sem, device):
@@ -19,11 +31,11 @@
     )
 
 
-def enter(peers):
+def enter(peers, more=0):
     barrier = pltpu.get_barrier_semaphore()
     for peer in peers:
         pl.semaphore_signal(barrier, inc=1, device_id=peer, device_id_type=MESH)
-    pl.semaphore_wait(barrier, len(peers))
+    pl.semaphore_wait(barrier, len(peers) + more)
 
 
 def y_sides(ys):
@@ -35,11 +47,11 @@
 
 def attend_kernel(
     zs, ys, scale, heads_total,
-    tab_ref, own_ref, q_ref, up_ref, bias_ref,
-    target_ref, index_keys_ref, tabs_ref,
-    tabs_v, tabs_s, z_low, z_high, x_out, x_in, x_all, keys, query, query_out,
-    logits_a, logits_b, expo, top, total, part, middle, t_in,
-    zs_sem, zr_sem, xs_sem, xr_sem, ts_sem, tr_sem, ys_sem, yr_sem, qs_sem, qr_sem, ps_sem, pr_sem, local_sem,
+    picked_ref, position_ref, cache_ref, index_ref, raw_ref, up_ref, iq_ref, iw_ref,
+    target_ref, index_keys_ref, tabs_ref, mask_ref, my_iq_ref, my_iw_ref,
+    tabs_v, tabs_s, slots_v, slots_s, own_ref, q_ref, bias_ref, z_low, z_high, x_out, x_in, x_all, keys, query, query_out,
+    logits_a, logits_b, expo, top, total, part, t_in,
+    zs_sem, zr_sem, xs_sem, xr_sem, ts_sem, tr_sem, ys_sem, yr_sem, is_sem, ir_sem, qs_sem, qr_sem, ps_sem, pr_sem, ms_sem, mr_sem, local_sem,
 ):
     ctx = lax.axis_index("ctx")
     z, x = ctx // X, ctx % X
@@ -53,9 +65,13 @@
     steps = zs // 2
     halves = 2
     part_blocks = own_blocks // halves
-    z_up = (lax.rem(z + 1, zs) * X + x, head)
-    z_down = (lax.rem(z + zs - 1, zs) * X + x, head)
-    to_a, to_b = (ctx, y_a * CORES + c), (ctx, y_b * CORES + c)
+    plan = z_plan(steps)
+    jumps = sorted({d - f for hop in plan for d, f in hop})
+
+    def z_device(shift):
+        return (lax.rem(z + shift + zs, zs) * X + x, head)
+
+    to_a, to_b, to_far = [(ctx, k * CORES + c) for k in (y_a, y_b, y_far)]
     to_core = (ctx, y * CORES + 1 - c)
     x_peers = []
     for dx in range(X):
@@ -63,8 +79,35 @@
             if dx or dc:
                 tx, tc = lax.rem(x + dx, X), lax.rem(c + dc, CORES)
                 x_peers.append((dx, dc, tx, tc, (z * X + tx, y * CORES + tc)))
-    tabs_v[x] = tab_ref[...]
-    enter([z_up, z_down, to_a, to_b] + [p[4] for p in x_peers])
+    row_to = lax.rem(head, ys) * CORES + head // ys
+    row_from = c * ys + y
+    moves = row_to != head
+
+    entry = cache_ref.shape[2]
+    mine_rows = pl.ds(pl.multiple_of(y * rows, rows), rows)
+
+    @pl.when(c == 0)
+    def low_half():
+        own_ref[...] = cache_ref[:, mine_rows, :half]
+
+    @pl.when(c == 1)
+    def high_half():
+        own_ref[:, :, : entry - half] = cache_ref[:, mine_rows, half:]
+        own_ref[:, :, entry - half : width - half] = jnp.zeros(
+            (own_blocks, rows, width - entry), own_ref.dtype
+        )
+        own_ref[:, :, width - half :] = index_ref[:, mine_rows, :]
+
+    z_peers = [z_device(sign * jump) for jump in jumps for sign in (1, -1)]
+    barrier = pltpu.get_barrier_semaphore()
+
+    @pl.when(moves)
+    def greet_movers():
+        for other in (row_to, row_from):
+            pl.semaphore_signal(barrier, inc=1, device_id=(ctx, other), device_id_type=MESH)
+
+    enter(z_peers + [to_a, to_b, to_far] + [p[4] for p in x_peers], 2 * moves.astype(jnp.int32))
+
     pending = []
 
     def start(copy):
@@ -79,35 +122,83 @@
             return z_low[k - 1].at[span]
         return z_high[k - 1].at[span]
 
-    def z_copy(direction, k, i):
+    def z_copy(direction, d, f, i):
         return remote(
-            piece(direction, k - 1, i), piece(direction, k, i),
-            zs_sem.at[direction, k - 1, i], zr_sem.at[direction, k - 1, i],
-            z_up if direction == 0 else z_down,
+            piece(direction, f, i), piece(direction, d, i),
+            zs_sem.at[direction, d - 1, i], zr_sem.at[direction, d - 1, i],
+            z_device(d - f if direction == 0 else f - d),
         )
 
-    def z_lanes(k):
-        return [(d, i) for i in range(halves) for d in range(2) if k < steps or (i == d)]
-
-    for d, i in z_lanes(1):
-        start(z_copy(d, 1, i))
+    def z_lanes(hop):
+        return [
+            (direction, d, f, i)
+            for i in range(halves)
+            for d, f in plan[hop]
+            for direction in range(2)
+            if d < steps or i == direction
+        ]
+
+    for lane in z_lanes(0):
+        start(z_copy(*lane))
+
+    shards = zs * X
+    lane_id = lax.broadcasted_iota(jnp.int32, (8, LANES), 1)
+    line_id = lax.broadcasted_iota(jnp.int32, (8, LANES), 0)
+
+    def ring(shard):
+        behind = lax.rem(lax.div(shard, X) - z + zs, zs)
+        return behind, jnp.minimum(behind, zs - behind)
+
+    lane_shard = jnp.minimum(lane_id, shards - 1)
+    lane_behind, lane_far = ring(lane_shard)
+    lane_key = lane_far * LANES + lane_shard
+    requests, places = [], []
+    for row in range(CORES):
+        request = jnp.zeros((8, LANES), jnp.int32)
+        place = jnp.zeros((8, LANES), jnp.int32)
+        for m in range(picks):
+            block = picked_ref[row, m]
+            shard = lax.rem(block, shards)
+            key = ring(shard)[1] * LANES + shard
+            request = jnp.where(lane_id == shard, lax.div(block, shards) + 1, request)
+            place = place + jnp.where(key < lane_key, 1, 0)
+        requests.append(request)
+        places.append(jnp.where(request > 0, place + 1, 0))
+    table = jnp.zeros((8, LANES), jnp.int32)
+    for row in range(CORES):
+        table = jnp.where(line_id == row, jnp.maximum(requests[row] - 1, 0), table)
+        table = jnp.where(line_id == 2 * CORES + row, requests[row], table)
+        table = jnp.where(line_id == 3 * CORES + row, places[row], table)
+    tabs_v[x] = table
     for dx in range(1, X):
         tx = lax.rem(x + dx, X)
         start(remote(tabs_v.at[x], tabs_v.at[x], ts_sem.at[dx - 1], tr_sem.at[dx - 1], (z * X + tx, head)))
     for dx in range(1, X):
         fx = lax.rem(x + X - dx, X)
-        remote(tabs_v.at[fx], tabs_v.at[fx], ts_sem.at[dx - 1], tr_sem.at[dx - 1], z_up).wait_recv()
+        remote(tabs_v.at[fx], tabs_v.at[fx], ts_sem.at[dx - 1], tr_sem.at[dx - 1], to_a).wait_recv()
+    my_place = jnp.where(c == 0, places[0], places[1])
+    lane_slot = lane_behind * X + lax.rem(lane_shard, X)
+    for i in range(picks // 8):
+        hit = my_place == line_id + (i * 8 + 1)
+        slot = jnp.sum(jnp.where(hit, lane_slot, 0), axis=1, keepdims=True)
+        slots_v[i * 8 : (i + 1) * 8, :] = jnp.broadcast_to(slot, (8, LANES))
+    slots_copy = pltpu.make_async_copy(slots_v, slots_s, local_sem)
+    slots_copy.start()
+    slots_copy.wait()
     to_scalar = pltpu.make_async_copy(tabs_v, tabs_s, local_sem)
     to_scalar.start()
     to_scalar.wait()
     tabs_ref[...] = tabs_v[...]
 
-    def sources(k):
-        if k == 0:
+    def sources(hop):
+        if hop == 0:
             return [(own_ref, 0)]
-        if k == steps:
-            return [(z_low[k - 1], zs - k)]
-        return [(z_low[k - 1], zs - k), (z_high[k - 1], k)]
+        found = []
+        for d, f in plan[hop - 1]:
+            found.append((z_low[d - 1], zs - d))
+            if d < steps:
+                found.append((z_high[d - 1], d))
+        return found
 
     def x_step(k):
         found = [(ref, rel, lax.rem(z + rel, zs) * X + x) for ref, rel in sources(k)]
@@ -131,12 +222,18 @@
     chunk = picks // chunks
 
     def y_copy(kind, owner, j, device):
-        ref = keys.at[pl.ds(j * chunk, chunk), pl.ds(pl.multiple_of(owner * rows, rows), rows)]
+        here = pl.ds(pl.multiple_of(owner * rows, rows), rows)
+        ref = keys.at[pl.ds(j * chunk, chunk), here, pl.ds(0, width)]
         return remote(ref, ref, ys_sem.at[kind, j], yr_sem.at[kind, j], device)
+
+    def index_copy(kind, owner, device):
+        here = pl.ds(pl.multiple_of(owner * rows, rows), rows)
+        ref = keys.at[:, here, pl.ds(width, full - width)]
+        return remote(ref, ref, is_sem.at[kind], ir_sem.at[kind], device)
 
     def y_start(j):
         def place(m, carry):
-            slot = tabs_s[x, CORES + c, m]
+            slot = slots_s[m, 0]
             for fc in range(CORES):
                 keys[m, pl.ds(pl.multiple_of(y * rows, rows), rows), fc * half : (fc + 1) * half] = x_all[slot, fc]
             return carry
@@ -147,7 +244,7 @@
 
     def y_forward(j):
         y_copy(0, y_b, j, to_a).wait_recv()
-        y_copy(2, y_b, j, to_a).start()
+        start(y_copy(2, y_b, j, to_a))
 
     def make_query(h):
         for mine, ref in ((True, query), (False, query_out)):
@@ -155,39 +252,86 @@
             ref[h, :, :latent] = jnp.dot(
                 q_ref[h, at, :nope], up_ref[h], preferred_element_type=jnp.float32
             ).astype(query.dtype)
-            ref[h, :, latent:] = q_ref[h, at, nope:]
+            entry_end = latent + q_ref.shape[2] - nope
+            ref[h, :, latent:entry_end] = q_ref[h, at, nope:]
+            ref[h, :, entry_end:] = jnp.zeros((block_len, width - entry_end), query.dtype)
+
+    def prepare():
+        @pl.when(moves)
+        def move():
+            remote(iq_ref, my_iq_ref, ms_sem.at[0], mr_sem.at[0], (ctx, row_to)).start()
+            remote(iw_ref, my_iw_ref, ms_sem.at[1], mr_sem.at[1], (ctx, row_to)).start()
+
+        @pl.when(jnp.logical_not(moves))
+        def stay():
+            my_iq_ref[...] = iq_ref[...]
+            my_iw_ref[...] = iw_ref[...]
+
+        q_ref[...] = jnp.swapaxes(raw_ref[...], 0, 1)
+        own_shard = lax.rem(position_ref[c], shards)
+        own_place = jnp.sum(jnp.where(lane_id == own_shard, my_place, 0), axis=1, keepdims=True) - 1
+        parts, unused, part_keys = bias_ref.shape
+        key_id = lax.broadcasted_iota(jnp.int32, (8, part_keys), 1)
+        token = lax.broadcasted_iota(jnp.int32, (8, part_keys), 0)
+        for j in range(parts):
+            pick_of = lax.div(key_id, block_len) + j * (part_keys // block_len)
+            inside = lax.rem(key_id, block_len)
+            for i in range(block_len // 8):
+                after = (pick_of == own_place) & (inside > token + i * 8)
+                bias_ref[j, i * 8 : (i + 1) * 8, :] = jnp.where(after, -jnp.inf, 0.0)
+            mask_ref[:, j * part_keys : (j + 1) * part_keys] = bias_ref[j, mine_rows, :]
 
     swap = remote(query_out, query.at[pl.ds(local_heads, local_heads)], qs_sem, qr_sem, to_core)
-    first = steps + 1 - chunks
-    per_step = local_heads // steps
+    hops = len(plan)
+    arrived = X
+    started = forwarded = 0
     x_step(0)
-    for k in range(1, steps + 1):
-        for h in range((k - 1) * per_step, k * per_step):
-            make_query(h)
-        if k == steps:
+    prepare()
+    made = 0
+    for hop in range(1, hops + 1):
+        while made * hops < local_heads * hop:
+            make_query(made)
+            made += 1
+        if hop == hops:
             start(swap)
-        for d, i in z_lanes(k):
-            z_copy(d, k, i).wait_recv()
-            if (d, i) in z_lanes(k + 1) and k < steps:
-                start(z_copy(d, k + 1, i))
-        x_step(k)
-        x_finish(k - 1)
-        if k - 1 >= first:
-            y_start(k - 1 - first)
-        if k - 2 >= first:
-            y_forward(k - 2 - first)
-    x_finish(steps)
-    y_start(chunks - 1)
-    y_forward(chunks - 2)
+        for direction, d, f, i in z_lanes(hop - 1):
+            z_copy(direction, d, f, i).wait_recv()
+            if hop < hops:
+                for lane in z_lanes(hop):
+                    if lane[0] == direction and lane[2] == d and lane[3] == i:
+                        start(z_copy(*lane))
+        x_step(hop)
+        x_finish(hop - 1)
+        before = started
+        ready = max(0, picks - (shards - arrived)) // chunk
+        arrived += X * len(sources(hop))
+        while started < ready:
+            y_start(started)
+            started += 1
+        while forwarded < before:
+            y_forward(forwarded)
+            forwarded += 1
+    x_finish(hops)
+    before = started
+    while started < chunks:
+        y_start(started)
+        started += 1
+    start(index_copy(0, y, to_a))
+    start(index_copy(1, y, to_b))
+    while forwarded < before:
+        y_forward(forwarded)
+        forwarded += 1
     swap.wait_recv()
 
     group = logits_a.shape[0] // block_len
     groups = query.shape[0] // group
-    pieces = chunk * block_len // LANES
+    parts = expo.shape[0]
+    per_part = picks // parts
+    pieces = per_part * block_len // LANES
 
     def dot(j, g, dst):
         block = query[pl.ds(g * group, group)].reshape(group * block_len, width)
-        these = keys[pl.ds(j * chunk, chunk)].reshape(chunk * block_len, full)[:, :width]
+        these = keys[pl.ds(j * per_part, per_part), :, :width].reshape(per_part * block_len, width)
         dst[...] = lax.dot_general(
             block, these, (((1,), (1,)), ((), ())), preferred_element_type=jnp.float32
         )
@@ -208,46 +352,45 @@
                 total[j, at, :] = functools.reduce(jnp.add, raised)
 
     def attend_chunk(j, carry):
-        @pl.when(j == 1)
-        def forward_last():
-            y_forward(chunks - 1)
-
-        y_copy(1, y_a, j, to_a).wait_recv()
-        y_copy(2, y_far, j, to_a).wait_recv()
+        for i in range(chunks // parts):
+            y_copy(1, y_a, j * (chunks // parts) + i, to_a).wait_recv()
+            y_copy(2, y_far, j * (chunks // parts) + i, to_a).wait_recv()
         dot(j, 0, logits_a)
 
-        def pair(p, inner):
+        for p in range(groups // 2):
             dot(j, 2 * p + 1, logits_b)
             soften(j, 2 * p, logits_a)
-            dot(j, lax.rem(2 * p + 2, groups), logits_a)
+            if p + 1 < groups // 2:
+                dot(j, 2 * p + 2, logits_a)
             soften(j, 2 * p + 1, logits_b)
-            return inner
-
-        lax.fori_loop(0, groups // 2, pair, 0)
         return carry
 
-    lax.fori_loop(0, chunks, attend_chunk, 0)
-    index_keys_ref[...] = keys[:, :, width:]
-
+    lax.fori_loop(0, 1, attend_chunk, 0)
+    while forwarded < chunks:
+        y_forward(forwarded)
+        forwarded += 1
+    lax.fori_loop(1, parts, attend_chunk, 0)
+    index_copy(0, y_b, to_a).wait_recv()
+    start(index_copy(2, y_b, to_a))
     def sum_heads(at):
         def one(h, sums):
             here = pl.ds(pl.multiple_of(h * block_len + at, 8), 8)
-            highs = [top[j, here, :] for j in range(chunks)]
+            highs = [top[j, here, :] for j in range(parts)]
             high = jnp.max(functools.reduce(jnp.maximum, highs), axis=1, keepdims=True)
             factors = [jnp.exp2(value - high) for value in highs]
             mass = functools.reduce(
-                jnp.add, [total[j, here, :] * factors[j] for j in range(chunks)]
+                jnp.add, [total[j, here, :] * factors[j] for j in range(parts)]
             )
             share = 1.0 / jnp.sum(mass, axis=1, keepdims=True)
             sums = list(sums)
-            for j in range(chunks):
+            for j in range(parts):
                 factor = factors[j] * share
                 for n in range(pieces):
                     sums[j * pieces + n] += expo[j, here, n * LANES : (n + 1) * LANES] * factor
             return tuple(sums)
 
         zero = jnp.zeros((8, LANES), jnp.float32)
-        return lax.fori_loop(0, query.shape[0], one, (zero,) * (chunks * pieces), unroll=4)
+        return lax.fori_loop(0, query.shape[0], one, (zero,) * (parts * pieces), unroll=4)
 
     def quarter(owner, dst):
         for i in range(rows // 8):
@@ -255,40 +398,46 @@
             for n, value in enumerate(sums):
                 dst[i * 8 : (i + 1) * 8, n * LANES : (n + 1) * LANES] = value
 
-    quarter(y_far, part.at[0])
-    far = remote(part.at[0], t_in.at[0], ps_sem.at[0], pr_sem.at[0], to_a)
-    start(far)
-    quarter(y_b, part.at[1])
-    near = remote(part.at[1], t_in.at[1], ps_sem.at[1], pr_sem.at[1], to_b)
-    start(near)
-    quarter(y_a, middle)
-    far.wait_recv()
-    part[2] = middle[...] + t_in[0]
-    last = remote(part.at[2], t_in.at[2], ps_sem.at[2], pr_sem.at[2], to_a)
-    start(last)
-    quarter(y, middle)
-    near.wait_recv()
-    last.wait_recv()
-    target_ref[...] = (middle[...] + t_in[1] + t_in[2]) * (1.0 / heads_total)
-    for j in range(chunks):
-        y_copy(2, y_b, j, to_a).wait_send()
+    for n, (owner, device) in enumerate(((y_far, to_far), (y_a, to_a), (y_b, to_b))):
+        quarter(owner, part.at[n])
+        start(remote(part.at[n], t_in.at[n], ps_sem.at[n], pr_sem.at[n], device))
+    quarter(y, target_ref)
+    index_copy(1, y_a, to_a).wait_recv()
+    index_copy(2, y_far, to_a).wait_recv()
+    index_keys_ref[...] = keys[:, :, width:]
+    for n in range(ys - 1):
+        remote(part.at[n], t_in.at[n], ps_sem.at[n], pr_sem.at[n], to_a).wait_recv()
+    target_ref[...] = (target_ref[...] + t_in[0] + t_in[1] + t_in[2]) * (1.0 / heads_total)
+    @pl.when(moves)
+    def moved():
+        for n, (src, dst) in enumerate(((iq_ref, my_iq_ref), (iw_ref, my_iw_ref))):
+            copy = remote(src, dst, ms_sem.at[n], mr_sem.at[n], (ctx, row_to))
+            copy.wait_send()
+            copy.wait_recv()
+
     for copy in pending:
         copy.wait_send()
 
 
-def attend(table, own, query, up_weight, bias, zs, ys, picks, block_len, heads_total, scale):
-    own_blocks, rows, half = own.shape
-    local_heads, unused, q_width = query.shape
+def attend(picked, position, cache, index_key, queries, up_weight, index_query, index_weight, zs, ys, heads_total):
+    own_blocks, block_len, entry = cache.shape
+    query_rows, picks = picked.shape
+    rows = block_len // ys
+    tokens, local_heads, q_width = queries.shape
+    scale = q_width ** (-0.5) * 1.4426950408889634
     nope, latent = up_weight.shape[1:]
-    width = latent + q_width - nope
-    full = half * CORES
+    width = -(-entry // LANES) * LANES
+    full = width + index_key.shape[2]
+    half = full // CORES
+    parts = 4
+    part_keys = picks * block_len // parts
     heads = local_heads * CORES
     steps = zs // 2
+    hops = len(z_plan(steps))
     peers = X * CORES - 1
-    chunks = bias.shape[0]
-    chunk_keys = bias.shape[2]
+    chunks = 8
     group = 8
-    keep = own.dtype
+    keep = cache.dtype
     single = jnp.float32
     dma = pltpu.SemaphoreType.DMA
     return pl.pallas_call(
@@ -297,39 +446,46 @@
             jax.ShapeDtypeStruct((rows, picks * block_len), single),
             jax.ShapeDtypeStruct((picks, block_len, full - width), keep),
             jax.ShapeDtypeStruct((X, 8, LANES), jnp.int32),
+            jax.ShapeDtypeStruct((rows, picks * block_len), single),
+            jax.ShapeDtypeStruct(index_query.shape, index_query.dtype),
+            jax.ShapeDtypeStruct(index_weight.shape, index_weight.dtype),
         ),
-        in_specs=[pl.BlockSpec(memory_space=pltpu.VMEM)] * 5,
-        out_specs=[pl.BlockSpec(memory_space=pltpu.VMEM)] * 3,
+        in_specs=[pl.BlockSpec(memory_space=pltpu.SMEM)] * 2 + [pl.BlockSpec(memory_space=pltpu.VMEM)] * 6,
+        out_specs=[pl.BlockSpec(memory_space=pltpu.VMEM)] * 6,
         scratch_shapes=[
             pltpu.VMEM((X, 8, LANES), jnp.int32),
             pltpu.SMEM((X, 8, LANES), jnp.int32),
+            pltpu.VMEM((picks, LANES), jnp.int32),
+            pltpu.SMEM((picks, LANES), jnp.int32),
+            pltpu.VMEM((own_blocks, rows, half), keep),
+            pltpu.VMEM((local_heads, tokens, q_width), keep),
+            pltpu.VMEM((parts, block_len, part_keys), single),
             [pltpu.VMEM((own_blocks, rows, half), keep) for k in range(steps)],
             [pltpu.VMEM((own_blocks, rows, half), keep) for k in range(steps - 1)],
-            pltpu.VMEM((steps + 1, peers, 2, rows, half), keep),
-            pltpu.VMEM((steps + 1, peers, 2, rows, half), keep),
+            pltpu.VMEM((hops + 1, peers, 4, rows, half), keep),
+            pltpu.VMEM((hops + 1, peers, 4, rows, half), keep),
             pltpu.VMEM((zs * X, CORES, rows, half), keep),
             pltpu.VMEM((picks, block_len, full), keep),
             pltpu.VMEM((heads, block_len, width), keep),
             pltpu.VMEM((local_heads, block_len, width), keep),
-            pltpu.VMEM((group * block_len, chunk_keys), single),
-            pltpu.VMEM((group * block_len, chunk_keys), single),
-            pltpu.VMEM((chunks, heads * block_len, chunk_keys), single),
-            pltpu.VMEM((chunks, heads * block_len, LANES), single),
-            pltpu.VMEM((chunks, heads * block_len, LANES), single),
+            pltpu.VMEM((group * block_len, part_keys), single),
+            pltpu.VMEM((group * block_len, part_keys), single),
+            pltpu.VMEM((parts, heads * block_len, part_keys), single),
+            pltpu.VMEM((parts, heads * block_len, LANES), single),
+            pltpu.VMEM((parts, heads * block_len, LANES), single),
             pltpu.VMEM((3, rows, picks * block_len), single),
-            pltpu.VMEM((rows, picks * block_len), single),
             pltpu.VMEM((3, rows, picks * block_len), single),
             dma((2, steps, 2)), dma((2, steps, 2)),
-            dma((steps + 1, peers)), dma((steps + 1, peers)),
+            dma((hops + 1, peers)), dma((hops + 1, peers)),
             dma((X - 1,)), dma((X - 1,)),
-            dma((3, chunks)), dma((3, chunks)),
-            dma, dma, dma((3,)), dma((3,)), dma,
+            dma((3, chunks)), dma((3, chunks)), dma((3,)), dma((3,)),
+            dma, dma, dma((3,)), dma((3,)), dma((2,)), dma((2,)), dma,
         ],
         compiler_params=pltpu.CompilerParams(
             collective_id=0, has_side_effects=True, vmem_limit_bytes=56 * 2**20
         ),
         name="attend",
-    )(table, own, query, up_weight, bias)
+    )(picked, position, cache, index_key, queries, up_weight, index_query, index_weight)
 
 
 def return_kernel(
@@ -354,20 +510,19 @@
     def span(k):
         return pl.ds(pl.multiple_of(k * rows, rows), rows)
 
-    y_out[0] = part_ref[:, span(y_far), :].astype(y_out.dtype)
-    far = remote(y_out.at[0], y_in.at[0], ys_sem.at[0], yr_sem.at[0], to_a)
-    far.start()
-    y_out[1] = part_ref[:, span(y_b), :].astype(y_out.dtype)
-    near = remote(y_out.at[1], y_in.at[1], ys_sem.at[1], yr_sem.at[1], to_b)
-    near.start()
-    far.wait_recv()
-    y_out[2] = (part_ref[:, span(y_a), :] + y_in[0].astype(jnp.float32)).astype(y_out.dtype)
-    last = remote(y_out.at[2], y_in.at[2], ys_sem.at[2], yr_sem.at[2], to_a)
-    last.start()
-    near.wait_recv()
-    last.wait_recv()
+    y_copies = []
+    for n, (owner, device) in enumerate(((y_far, to_far), (y_a, to_a), (y_b, to_b))):
+        y_out[n] = part_ref[:, span(owner), :].astype(y_out.dtype)
+        copy = remote(y_out.at[n], y_in.at[n], ys_sem.at[n], yr_sem.at[n], device)
+        copy.start()
+        y_copies.append(copy)
+    for n in range(ys - 1):
+        remote(y_out.at[n], y_in.at[n], ys_sem.at[n], yr_sem.at[n], to_a).wait_recv()
     quarter[...] = (
-        part_ref[:, span(y), :] + y_in[1].astype(jnp.float32) + y_in[2].astype(jnp.float32)
+        part_ref[:, span(y), :]
+        + y_in[0].astype(jnp.float32)
+        + y_in[1].astype(jnp.float32)
+        + y_in[2].astype(jnp.float32)
     )
 
     def choose(tx, dst):
@@ -441,7 +596,7 @@
     for n, fy in enumerate((y_b, y_a, y_far)):
         ref = out_ref.at[:, span(fy), :]
         remote(ref, ref, os_sem.at[n], or_sem.at[n], to_a).wait_recv()
-    for copy in [far, near, last, core] + x_copies + z_copies + o_copies:
+    for copy in y_copies + [core] + x_copies + z_copies + o_copies:
         copy.wait_send()
 
 
@@ -498,74 +653,19 @@
     owners = lax.axis_size("ctx")
     head_devices = lax.axis_size("head")
     zs, ys = owners // X, head_devices // CORES
-    ctx = lax.axis_index("ctx")
-    head = lax.axis_index("head")
-    y, c = head // CORES, head % CORES
-    query_count, picks = picked_blocks.shape
+    picks = picked_blocks.shape[1]
     own_blocks, unused, block_len, entry_width = cache_entry.shape
     index_width = index_key.shape[3]
     key_count = picks * block_len
     rows = block_len // ys
     local_heads = queries.shape[1]
-    pad_width = -(-entry_width // LANES) * LANES
-    full_width = pad_width + index_width
-    half = full_width // CORES
-
-    shard_of = picked_blocks % owners
-    behind = (shard_of // X - ctx // X + zs) % zs
-    distance = jnp.minimum(behind, zs - behind) * picks + jnp.arange(picks)[None, :]
-    rank = jnp.sum((distance[:, None, :] < distance[:, :, None]).astype(jnp.int32), axis=2)
-    ordered = rank[:, :, None] == jnp.arange(picks)[None, None, :]
-    blocks = jnp.sum(jnp.where(ordered, picked_blocks[:, :, None], 0), axis=1)
-    owner_of = blocks % owners
-    slot = (owner_of // X - ctx // X + zs) % zs * X + owner_of % X
-
-    matched = owner_of[:, :, None] == jnp.arange(owners)[None, None, :]
-    request = jnp.sum(jnp.where(matched, blocks[:, :, None] // owners + 1, 0), axis=1)
-    place = jnp.sum(jnp.where(matched, jnp.arange(1, picks + 1)[None, :, None], 0), axis=1)
-    wide = [(0, 0), (0, LANES - owners)]
-    table = jnp.concatenate(
-        [
-            jnp.pad(jnp.maximum(request - 1, 0), wide),
-            jnp.pad(slot, [(0, 0), (0, LANES - picks)]),
-            jnp.pad(request, wide),
-            jnp.pad(place, wide),
-        ],
-        axis=0,
+    target, index_keys, tables, mask, my_index_query, my_index_weight = attend(
+        picked_blocks, block_position, cache_entry[:, 0], index_key[:, 0], queries, up_weight,
+        index_query, index_weight, zs, ys, local_heads * head_devices,
     )
-
-    own = jnp.concatenate(
-        [
-            lax.dynamic_slice_in_dim(cache_entry[:, 0], y * rows, rows, 1),
-            jnp.zeros((own_blocks, rows, pad_width - entry_width), cache_entry.dtype),
-            lax.dynamic_slice_in_dim(index_key[:, 0], y * rows, rows, 1),
-        ],
-        axis=2,
-    )
-    own = lax.dynamic_slice_in_dim(own, c * half, half, 2)
-
     to_row = [((i % CORES) * ys + i // CORES, i) for i in range(head_devices)]
-    my_index_query = lax.ppermute(index_query, "head", to_row)
-    my_index_weight = lax.ppermute(index_weight, "head", to_row)
-    heads_first = jnp.pad(
-        jnp.transpose(queries, (1, 0, 2)), [(0, 0), (0, 0), (0, pad_width - entry_width)]
-    )
-
-    my_picks = lax.dynamic_index_in_dim(blocks, c, 0, keepdims=False)
-    my_position = lax.dynamic_index_in_dim(block_position, c, 0, keepdims=False)
-    key_place = (my_picks[:, None] * block_len + jnp.arange(block_len)[None, :]).reshape(key_count)
-    query_place = my_position * block_len + jnp.arange(block_len)
-    allowed = key_place[None, :] <= query_place[:, None]
-    chunks = 4
-    chunk_place = key_place.reshape(chunks, 1, key_count // chunks)
-    bias = jnp.where(chunk_place <= query_place[None, :, None], 0.0, -jnp.inf).astype(jnp.float32)
-    scale = queries.shape[2] ** (-0.5) * 1.4426950408889634
-    target, index_keys, tables = attend(
-        table, own, heads_first, up_weight, bias,
-        zs, ys, picks, block_len, local_heads * head_devices, scale,
-    )
     index_keys = index_keys.reshape(key_count, index_width)
-    my_allowed = lax.dynamic_slice_in_dim(allowed, y * rows, rows, 0)
+    my_allowed = mask == 0.0
     index_scale = index_width ** (-0.5)
     raw = jnp.einsum("ijd,sd->ijs", my_index_query, index_keys, preferred_element_type=jnp.float32)
     act = jnp.maximum(raw, 0.0) * index_scale

time: 163 us -> 146 us (0.90)
  starting transfers between devices: 11.4 us -> 3.91 us
  Pallas kernels: 134 us -> 130 us
  local copies, waits for them, and re-layouts: 6.51 us -> 3.98 us
  other arithmetic: 5.62 us -> 3.2 us
    ppermute x2 -> x0, starting transfers between devices: 8.21 us -> none  [the longest x1 4.73 us: local(): my_index_weight = lax.ppermute(index_weight, 'head', to_row)]
    pallas_call x1, Pallas kernels: 45.7 us -> 43.3 us  [give_back(): pl.pallas_call(functools.partial(return_kernel, zs, ys), out_shape=jax.Sh...]
    dynamic_slice x5 -> x0, local copies, waits for them, and re-layouts: 2.18 us -> none  [the longest x1 1.24 us: local(): my_position = lax.dynamic_index_in_dim(block_position, c, 0, keepdims=False)]
    unnamed x9 -> x13, local copies, waits for them, and re-layouts: 2.76 us -> 3.98 us
  transfers between devices with their start and end apart: 3 -> 1, of which waited for: 0 -> 0; matrix products, arithmetic and copies ran while one was open for 7% -> 2% of each run, Pallas kernels for 82% -> 30%
where the time goes in v4:
time: 146 us
  Pallas kernels  130 us (89%)
  matrix products  4.3 us (3%)
  local copies, waits for them, and re-layouts  3.98 us (3%)
  starting transfers between devices  3.91 us (3%)
  other arithmetic  3.2 us (2%)
    pallas_call x1, Pallas kernels, attend(): pl.pallas_call(functools.partial(attend_kernel, zs, ys, scale, heads_tota...  86.6 us
    pallas_call x1, Pallas kernels, give_back(): pl.pallas_call(functools.partial(return_kernel, zs, ys), out_shape=jax.Sh...  43.3 us
    unnamed x13, local copies, waits for them, and re-layouts  3.98 us
    ppermute x1, starting transfers between devices, local(): weight_grad = lax.ppermute(weight_part, 'head', [(b, a) for a, b in to_row])  3.91 us
  transfers between devices with their start and end apart: 1, of which 0 were waited for; matrix products, arithmetic and copies ran while one was open for 2% of the time, Pallas kernels for 30%

profile of v4, /device:TPU:1, one launch (start us, length us, event | category | flops | bytes accessed | tf_op | source)
XLA Modules:
  0.0 146.1 jit_solution(1820897468901358653)
XLA Ops:
  0.6 2.7 %copy.10.raw_ref = bf16[128,16,192]{2,1,0:T(8,128)(2,1)} copy(bf16[128,16,192]{0,2,1:T(8,128)(2,1)} %param.8) | data formatting | bytes 1572864 | tf_op args[0]
  3.3 86.6 %attend.1 = (f32[16,2048]{1,0:T(8,128)}, bf16[32,64,128]{2,1,0:T(8,128)(2,1)}, s32[4,8,128]{2,1,0:T(8,128)}, f32[16,2048]{1,0:T(8,128)}, bf16[16,64,128]{2,1,0:T(8,128)(2,1)}, /*index=5*/f32[16,64]{1,0:T(8,128)}) custom-call(s32[2,32]{1,0:T(2,128)} %picked_ref.1, s32[2]{0:T(128)} %position_ref.1, bf16[8,64,576]{2,1,0:T(8,128)(2,1)} %bitcast.16, ...), custom_call_target="tpu_custom_call" | custom-call | tf_op jit(solution)/shard_map/attend/pallas_call | solution.py:443
  89.9 0.0 copy-start.3
  89.9 0.0 copy-start.2
  89.9 0.7 broadcast_multiply_fusion.1
  90.7 2.4 %multiply_reduce_fusion.1 = (f32[16,2048]{1,0:T(8,128)S(1)}, f32[16,64,2048]{2,1,0:T(8,128)S(1)}) fusion(f32[16,64]{1,0:T(8,128)S(1)} %broadcast_multiply_fusion.1, bf16[16,64,128]{2,1,0:T(8,128)(2,1)} %get-tuple-element.9, bf16[2048,128,1]{1,0,2:T(8,128)(2,1)} %bitcast.17), kind=kOutput, calls=%fused_computation.4 | convolution fusion | flops 543129600 | bytes 9310208 | tf_op jit(solution)/shard_map/ijd,sd->ijs/dot_general | solution.py:670
  93.1 0.0 copy-done.3
  93.1 0.1 fusion.4
  93.2 0.2 fusion.3
  93.4 0.0 copy-done.2
  93.5 0.1 broadcast_multiply_fusion
  93.6 0.0 copy-start.1
  93.6 0.0 copy-start.4
  93.6 0.9 multiply_reduce_fusion
  94.5 3.9 %collective-permute-start = (f32[16,64]{1,0:T(8,128)S(1)}, f32[16,64]{1,0:T(8,128)S(1)}, u32[]{:S(2)}, u32[]{:S(2)}) collective-permute-start(f32[16,64]{1,0:T(8,128)S(1)} %multiply_reduce_fusion), channel_id=1, source_target_pairs={{0,0},{1,4},{2,1},{3,5},{4,2},{5,6},{6,3},{7,7},{8,8},{9,12},{10,9... | collective-permute-start | bytes 12296 | tf_op jit(solution)/shard_map/ppermute | solution.py:682
  98.4 1.1 fusion
  99.5 0.0 copy-done.1
  99.5 0.0 copy-done.4
  99.5 0.0 copy-start
  99.5 1.9 %fusion.1 = f32[2048,128,1]{1,0,2:T(8,128)S(1)} fusion(bf16[16,64,128]{2,1,0:T(8,128)(2,1)S(1)} %copy-done.1, f32[16,64]{1,0:T(8,128)S(1)} %copy-done.4, f32[16,2048]{1,0:T(8,128)S(1)} %get-tuple-element.17, u16[64,2048]{1,0:T(8,128)(2,1)S(1)} %fusion), kind=kOutput, calls=%fused_computation.6 | convolution fusion | flops 553648128 | bytes 1708032 | tf_op jit(solution)/shard_map/ijs,ijd->sd/dot_general | solution.py:679
  101.5 43.3 %give_back.1 = f32[8,64,128]{2,1,0:T(8,128)S(1)} custom-call(s32[4,8,128]{2,1,0:T(8,128)S(1)} %copy-done, f32[32,64,128]{2,1,0:T(8,128)S(1)} %bitcast.14), custom_call_target="tpu_custom_call" | custom-call | tf_op jit(solution)/shard_map/give_back/pallas_call | solution.py:608
  144.7 0.0 collective-permute-done
  144.8 0.7 copy.14
  145.5 0.6 copy.15
  (1 shorter events, 0.0 us)
Async XLA Ops:
  89.9 3.2 %copy-start.3 = (f32[16,2048]{1,0:T(8,128)S(1)}, f32[16,2048]{1,0:T(8,128)}, u32[]{:S(2)}) copy-start(f32[16,2048]{1,0:T(8,128)} %get-tuple-element.11) | copy-start | bytes 393220
  89.9 3.5 %copy-start.2 = (f32[16,2048]{1,0:T(8,128)S(1)}, f32[16,2048]{1,0:T(8,128)}, u32[]{:S(2)}) copy-start(f32[16,2048]{1,0:T(8,128)} %get-tuple-element.13) | copy-start | bytes 393220
  93.6 5.9 %copy-start.1 = (bf16[16,64,128]{2,1,0:T(8,128)(2,1)S(1)}, bf16[16,64,128]{2,1,0:T(8,128)(2,1)}, u32[]{:S(2)}) copy-start(bf16[16,64,128]{2,1,0:T(8,128)(2,1)} %get-tuple-element.9) | copy-start | bytes 786436
  93.6 5.9 %copy-start.4 = (f32[16,64]{1,0:T(8,128)S(1)}, f32[16,64]{1,0:T(8,128)}, u32[]{:S(2)}) copy-start(f32[16,64]{1,0:T(8,128)} %get-tuple-element.12) | copy-start | bytes 12292
  94.5 50.2 %collective-permute-start = (f32[16,64]{1,0:T(8,128)S(1)}, f32[16,64]{1,0:T(8,128)S(1)}, u32[]{:S(2)}, u32[]{:S(2)}) collective-permute-start(f32[16,64]{1,0:T(8,128)S(1)} %multiply_reduce_fusion), channel_id=1, source_target_pairs={{0,0},{1,4},{2,1},{3,5},{4,2},{5,6},{6,3},{7,7},{8,8},{9,12},{10,9... | collective-permute-start | bytes 12296 | tf_op jit(solution)/shard_map/ppermute | solution.py:682
  99.5 1.9 %copy-start = (s32[4,8,128]{2,1,0:T(8,128)S(1)}, s32[4,8,128]{2,1,0:T(8,128)}, u32[]{:S(2)}) copy-start(s32[4,8,128]{2,1,0:T(8,128)} %get-tuple-element.8.tabs_ref) | copy-start | bytes 49156

commit v5 on v4

--- a/solution.py
+++ b/solution.py
@@ -173,23 +173,6 @@
     for dx in range(1, X):
         tx = lax.rem(x + dx, X)
         start(remote(tabs_v.at[x], tabs_v.at[x], ts_sem.at[dx - 1], tr_sem.at[dx - 1], (z * X + tx, head)))
-    for dx in range(1, X):
-        fx = lax.rem(x + X - dx, X)
-        remote(tabs_v.at[fx], tabs_v.at[fx], ts_sem.at[dx - 1], tr_sem.at[dx - 1], to_a).wait_recv()
-    my_place = jnp.where(c == 0, places[0], places[1])
-    lane_slot = lane_behind * X + lax.rem(lane_shard, X)
-    for i in range(picks // 8):
-        hit = my_place == line_id + (i * 8 + 1)
-        slot = jnp.sum(jnp.where(hit, lane_slot, 0), axis=1, keepdims=True)
-        slots_v[i * 8 : (i + 1) * 8, :] = jnp.broadcast_to(slot, (8, LANES))
-    slots_copy = pltpu.make_async_copy(slots_v, slots_s, local_sem)
-    slots_copy.start()
-    slots_copy.wait()
-    to_scalar = pltpu.make_async_copy(tabs_v, tabs_s, local_sem)
-    to_scalar.start()
-    to_scalar.wait()
-    tabs_ref[...] = tabs_v[...]
-
     def sources(hop):
         if hop == 0:
             return [(own_ref, 0)]
@@ -241,12 +224,15 @@
         lax.fori_loop(j * chunk, (j + 1) * chunk, place, 0)
         start(y_copy(0, y, j, to_a))
         start(y_copy(1, y, j, to_b))
+        if j == chunks - 1:
+            start(y_copy(2, y, j, to_far))
 
     def y_forward(j):
         y_copy(0, y_b, j, to_a).wait_recv()
         start(y_copy(2, y_b, j, to_a))
 
     def make_query(h):
+        q_ref[h] = raw_ref[h].T
         for mine, ref in ((True, query), (False, query_out)):
             at = pl.ds(pl.multiple_of((c if mine else 1 - c) * block_len, block_len), block_len)
             ref[h, :, :latent] = jnp.dot(
@@ -256,6 +242,25 @@
             ref[h, :, latent:entry_end] = q_ref[h, at, nope:]
             ref[h, :, entry_end:] = jnp.zeros((block_len, width - entry_end), query.dtype)
 
+    my_place = jnp.where(c == 0, places[0], places[1])
+
+    def tables_wait():
+        for dx in range(1, X):
+            fx = lax.rem(x + X - dx, X)
+            remote(tabs_v.at[fx], tabs_v.at[fx], ts_sem.at[dx - 1], tr_sem.at[dx - 1], to_a).wait_recv()
+        lane_slot = lane_behind * X + lax.rem(lane_shard, X)
+        for i in range(picks // 8):
+            hit = my_place == line_id + (i * 8 + 1)
+            slot = jnp.sum(jnp.where(hit, lane_slot, 0), axis=1, keepdims=True)
+            slots_v[i * 8 : (i + 1) * 8, :] = jnp.broadcast_to(slot, (8, LANES))
+        slots_copy = pltpu.make_async_copy(slots_v, slots_s, local_sem)
+        slots_copy.start()
+        slots_copy.wait()
+        to_scalar = pltpu.make_async_copy(tabs_v, tabs_s, local_sem)
+        to_scalar.start()
+        to_scalar.wait()
+        tabs_ref[...] = tabs_v[...]
+
     def prepare():
         @pl.when(moves)
         def move():
@@ -267,7 +272,6 @@
             my_iq_ref[...] = iq_ref[...]
             my_iw_ref[...] = iw_ref[...]
 
-        q_ref[...] = jnp.swapaxes(raw_ref[...], 0, 1)
         own_shard = lax.rem(position_ref[c], shards)
         own_place = jnp.sum(jnp.where(lane_id == own_shard, my_place, 0), axis=1, keepdims=True) - 1
         parts, unused, part_keys = bias_ref.shape
@@ -285,8 +289,6 @@
     hops = len(plan)
     arrived = X
     started = forwarded = 0
-    x_step(0)
-    prepare()
     made = 0
     for hop in range(1, hops + 1):
         while made * hops < local_heads * hop:
@@ -300,7 +302,12 @@
                 for lane in z_lanes(hop):
                     if lane[0] == direction and lane[2] == d and lane[3] == i:
                         start(z_copy(*lane))
+        if hop == 1:
+            tables_wait()
+            x_step(0)
         x_step(hop)
+        if hop == 1:
+            prepare()
         x_finish(hop - 1)
         before = started
         ready = max(0, picks - (shards - arrived)) // chunk
@@ -316,11 +323,12 @@
     while started < chunks:
         y_start(started)
         started += 1
-    start(index_copy(0, y, to_a))
-    start(index_copy(1, y, to_b))
     while forwarded < before:
         y_forward(forwarded)
         forwarded += 1
+    start(index_copy(0, y, to_a))
+    start(index_copy(1, y, to_b))
+    start(index_copy(2, y, to_far))
     swap.wait_recv()
 
     group = logits_a.shape[0] // block_len
@@ -352,6 +360,10 @@
                 total[j, at, :] = functools.reduce(jnp.add, raised)
 
     def attend_chunk(j, carry):
+        @pl.when(j == parts - 1)
+        def last_chunk():
+            y_copy(0, y_b, chunks - 1, to_a).wait_recv()
+
         for i in range(chunks // parts):
             y_copy(1, y_a, j * (chunks // parts) + i, to_a).wait_recv()
             y_copy(2, y_far, j * (chunks // parts) + i, to_a).wait_recv()
@@ -365,13 +377,7 @@
             soften(j, 2 * p + 1, logits_b)
         return carry
 
-    lax.fori_loop(0, 1, attend_chunk, 0)
-    while forwarded < chunks:
-        y_forward(forwarded)
-        forwarded += 1
-    lax.fori_loop(1, parts, attend_chunk, 0)
-    index_copy(0, y_b, to_a).wait_recv()
-    start(index_copy(2, y_b, to_a))
+    lax.fori_loop(0, parts, attend_chunk, 0)
     def sum_heads(at):
         def one(h, sums):
             here = pl.ds(pl.multiple_of(h * block_len + at, 8), 8)
@@ -402,6 +408,7 @@
         quarter(owner, part.at[n])
         start(remote(part.at[n], t_in.at[n], ps_sem.at[n], pr_sem.at[n], device))
     quarter(y, target_ref)
+    index_copy(0, y_b, to_a).wait_recv()
     index_copy(1, y_a, to_a).wait_recv()
     index_copy(2, y_far, to_a).wait_recv()
     index_keys_ref[...] = keys[:, :, width:]
@@ -415,6 +422,7 @@
             copy.wait_send()
             copy.wait_recv()
 
+    my_iw_ref[...] = my_iw_ref[...] * index_ref.shape[2] ** (-0.5)
     for copy in pending:
         copy.wait_send()
 
@@ -423,7 +431,7 @@
     own_blocks, block_len, entry = cache.shape
     query_rows, picks = picked.shape
     rows = block_len // ys
-    tokens, local_heads, q_width = queries.shape
+    local_heads, q_width, tokens = queries.shape
     scale = q_width ** (-0.5) * 1.4426950408889634
     nope, latent = up_weight.shape[1:]
     width = -(-entry // LANES) * LANES
@@ -489,9 +497,9 @@
 
 
 def return_kernel(
-    zs, ys, tabs_ref, part_ref, out_ref,
-    y_out, y_in, quarter, x_out, x_in, z_out, z_in, mine, theirs,
-    ys_sem, yr_sem, xs_sem, xr_sem, zs_sem, zr_sem, cs_sem, cr_sem, os_sem, or_sem,
+    zs, ys, tabs_ref, ids_ref, part_ref, out_ref,
+    y_out, y_in, quarter, x_out, x_in, z_out, z_in, id_out, id_in, mine, theirs,
+    is_sem, ir_sem, ys_sem, yr_sem, xs_sem, xr_sem, zs_sem, zr_sem, cs_sem, cr_sem, os_sem, or_sem,
 ):
     ctx = lax.axis_index("ctx")
     z, x = ctx // X, ctx % X
@@ -500,7 +508,6 @@
     picks, block_len, width = part_ref.shape
     own_blocks = out_ref.shape[0]
     rows = block_len // ys
-    slots = X * rows
     to_a, to_b, to_far = (ctx, y_a * CORES + c), (ctx, y_b * CORES + c), (ctx, y_far * CORES + c)
     to_core = (ctx, y * CORES + 1 - c)
     x_peers = [(lax.rem(x + d, X), (z * X + lax.rem(x + d, X), head)) for d in range(1, X)]
@@ -511,9 +518,24 @@
         return pl.ds(pl.multiple_of(k * rows, rows), rows)
 
     y_copies = []
+    order = sorted(range(1, zs), key=lambda d: -min(d, zs - d))
+    line = lax.broadcasted_iota(jnp.int32, id_out.shape, 0)
+    lane = lax.broadcasted_iota(jnp.int32, id_out.shape, 1)
+    asked = jnp.zeros(id_out.shape, jnp.int32)
+    for fx in range(X):
+        row = jnp.where(
+            c == 0, ids_ref[fx, 2 * CORES : 2 * CORES + 1, :], ids_ref[fx, 2 * CORES + 1 : 2 * CORES + 2, :]
+        )
+        asked = jnp.where(line == fx, jnp.broadcast_to(row, id_out.shape), asked)
+    id_out[...] = asked
+    id_in[z] = asked
     for n, (owner, device) in enumerate(((y_far, to_far), (y_a, to_a), (y_b, to_b))):
         y_out[n] = part_ref[:, span(owner), :].astype(y_out.dtype)
         copy = remote(y_out.at[n], y_in.at[n], ys_sem.at[n], yr_sem.at[n], device)
+        copy.start()
+        y_copies.append(copy)
+    for d in order:
+        copy = remote(id_out, id_in.at[z], is_sem.at[d - 1], ir_sem.at[d - 1], z_peers[d - 1][1])
         copy.start()
         y_copies.append(copy)
     for n in range(ys - 1):
@@ -545,18 +567,11 @@
         fx = lax.rem(x + X - n - 1, X)
         remote(x_out.at[n], x_in.at[fx], xs_sem.at[n], xr_sem.at[n], to_a).wait_recv()
 
-    line = lax.broadcasted_iota(jnp.int32, (rows, width), 0)
-
     def gather(owner, dst):
-        ids = jnp.zeros((rows, width), jnp.float32)
         for fx in range(X):
             dst[fx * rows : (fx + 1) * rows] = x_in[fx, owner]
-            block = tabs_ref[fx, 2 * CORES + c, owner * X + x]
-            ids = jnp.where(line == fx, block.astype(jnp.float32), ids)
-        dst[slots : slots + rows] = ids.astype(dst.dtype)
 
     z_copies = []
-    order = sorted(range(1, zs), key=lambda d: -min(d, zs - d))
     for d in order:
         tz, device = z_peers[d - 1]
         gather(tz, z_out.at[d - 1])
@@ -566,16 +581,17 @@
     gather(z, z_in.at[z])
     for d in order:
         fz = lax.rem(z + zs - d, zs)
+        remote(id_out, id_in.at[fz], is_sem.at[d - 1], ir_sem.at[d - 1], to_a).wait_recv()
         remote(z_out.at[d - 1], z_in.at[fz], zs_sem.at[d - 1], zr_sem.at[d - 1], to_a).wait_recv()
 
     def add(fz, totals):
-        ids = z_in[fz, slots : slots + rows].astype(jnp.float32)
+        ids = jnp.sum(jnp.where(lane == ctx, id_in[fz], 0), axis=1, keepdims=True)
         totals = list(totals)
         for fx in range(X):
             value = z_in[fz, fx * rows : (fx + 1) * rows].astype(jnp.float32)
             block = jnp.broadcast_to(ids[fx : fx + 1], value.shape)
             for r in range(own_blocks):
-                totals[r] = totals[r] + jnp.where(block == r + 1.0, value, 0.0)
+                totals[r] = totals[r] + jnp.where(block == r + 1, value, 0.0)
         return tuple(totals)
 
     totals = lax.fori_loop(
@@ -611,6 +627,7 @@
         in_specs=[
             pl.BlockSpec(memory_space=pltpu.SMEM),
             pl.BlockSpec(memory_space=pltpu.VMEM),
+            pl.BlockSpec(memory_space=pltpu.VMEM),
         ],
         out_specs=pl.BlockSpec(memory_space=pltpu.VMEM),
         scratch_shapes=[
@@ -619,10 +636,13 @@
             pltpu.VMEM((picks, rows, width), jnp.float32),
             pltpu.VMEM((X - 1, zs, rows, width), half),
             pltpu.VMEM((X, zs, rows, width), half),
-            pltpu.VMEM((zs - 1, (X + 1) * rows, width), half),
-            pltpu.VMEM((zs, (X + 1) * rows, width), half),
+            pltpu.VMEM((zs - 1, X * rows, width), half),
+            pltpu.VMEM((zs, X * rows, width), half),
+            pltpu.VMEM((8, LANES), jnp.int32),
+            pltpu.VMEM((zs, 8, LANES), jnp.int32),
             pltpu.VMEM((own_blocks, rows, width), jnp.float32),
             pltpu.VMEM((own_blocks, rows, width), jnp.float32),
+            dma((zs - 1,)), dma((zs - 1,)),
             dma((3,)), dma((3,)), dma((X - 1,)), dma((X - 1,)), dma((zs - 1,)), dma((zs - 1,)),
             dma, dma, dma((3,)), dma((3,)),
         ],
@@ -630,7 +650,7 @@
             collective_id=2, has_side_effects=True, vmem_limit_bytes=40 * 2**20
         ),
         name="give_back",
-    )(tables, key_part)
+    )(tables, tables, key_part)
 
 
 def masked_softmax(values, allowed):
@@ -660,21 +680,20 @@
     rows = block_len // ys
     local_heads = queries.shape[1]
     target, index_keys, tables, mask, my_index_query, my_index_weight = attend(
-        picked_blocks, block_position, cache_entry[:, 0], index_key[:, 0], queries, up_weight,
+        picked_blocks, block_position, cache_entry[:, 0], index_key[:, 0], jnp.transpose(queries, (1, 2, 0)), up_weight,
         index_query, index_weight, zs, ys, local_heads * head_devices,
     )
     to_row = [((i % CORES) * ys + i // CORES, i) for i in range(head_devices)]
     index_keys = index_keys.reshape(key_count, index_width)
     my_allowed = mask == 0.0
-    index_scale = index_width ** (-0.5)
     raw = jnp.einsum("ijd,sd->ijs", my_index_query, index_keys, preferred_element_type=jnp.float32)
-    act = jnp.maximum(raw, 0.0) * index_scale
-    score = jnp.sum(my_index_weight[:, :, None] * act, axis=1)
+    positive = jnp.maximum(raw, 0.0)
+    score = jnp.sum(my_index_weight[:, :, None] * positive, axis=1)
     soft = masked_softmax(score, my_allowed)
     score_grad = jnp.where(my_allowed, soft - target, 0.0)
-    weight_part = jnp.sum(score_grad[:, None, :] * act, axis=2)
+    weight_part = jnp.sum(score_grad[:, None, :] * positive, axis=2) * index_width ** (-0.5)
     coefficient = jnp.where(
-        raw > 0, score_grad[:, None, :] * my_index_weight[:, :, None] * index_scale, 0.0
+        raw > 0, score_grad[:, None, :] * my_index_weight[:, :, None], 0.0
     ).astype(jnp.bfloat16)
     key_part = jnp.einsum(
         "ijs,ijd->sd", coefficient, my_index_query, preferred_element_type=jnp.float32

time: 146 us -> 144 us (0.986)
  local copies, waits for them, and re-layouts: 3.98 us -> 1.32 us
    unnamed x13 -> x12, local copies, waits for them, and re-layouts: 3.98 us -> 1.32 us
where the time goes in v5:
time: 144 us; the launch traced here: 143 us
  Pallas kernels  129 us (90%)
  starting transfers between devices  5.31 us (4%)
  matrix products  4.13 us (3%)
  other arithmetic  2.46 us (2%)
    pallas_call x1, Pallas kernels, attend(): pl.pallas_call(functools.partial(attend_kernel, zs, ys, scale, heads_tota...  87 us
    pallas_call x1, Pallas kernels, give_back(): pl.pallas_call(functools.partial(return_kernel, zs, ys), out_shape=jax.Sh...  42.4 us
    ppermute x1, starting transfers between devices, local(): weight_grad = lax.ppermute(weight_part, 'head', [(b, a) for a, b in to_row])  5.31 us
  transfers between devices with their start and end apart: 1, of which 0 were waited for; matrix products, arithmetic and copies ran while one was open for 2% of the time, Pallas kernels for 30%

profile of v5, /device:TPU:1, one launch (start us, length us, event | category | flops | bytes accessed | tf_op | source)
XLA Modules:
  0.0 143.4 jit_solution(8847828460723116432)
XLA Ops:
  0.6 87.0 %attend.1 = (f32[16,2048]{1,0:T(8,128)}, bf16[32,64,128]{2,1,0:T(8,128)(2,1)}, s32[4,8,128]{2,1,0:T(8,128)}, f32[16,2048]{1,0:T(8,128)}, bf16[16,64,128]{2,1,0:T(8,128)(2,1)}, /*index=5*/f32[16,64]{1,0:T(8,128)}) custom-call(s32[2,32]{1,0:T(2,128)} %picked_ref.1, s32[2]{0:T(128)} %position_ref.1, bf16[8,64,576]{2,1,0:T(8,128)(2,1)} %bitcast.18, ...), custom_call_target="tpu_custom_call" | custom-call | tf_op jit(solution)/shard_map/attend/pallas_call | solution.py:451
  87.7 0.0 copy-start.3
  87.7 0.0 copy-start.2
  87.7 2.4 %multiply_reduce_fusion.1 = (f32[16,2048]{1,0:T(8,128)S(1)}, f32[16,64,2048]{2,1,0:T(8,128)S(1)}) fusion(f32[16,64]{1,0:T(8,128)} %get-tuple-element.12, bf16[16,64,128]{2,1,0:T(8,128)(2,1)} %get-tuple-element.9, bf16[2048,128,1]{1,0,2:T(8,128)(2,1)} %bitcast.19), kind=kOutput, calls=%fused_computation.4 | convolution fusion | flops 543129600 | bytes 9310208 | tf_op jit(solution)/shard_map/ijd,sd->ijs/dot_general | solution.py:689
  90.1 0.0 copy-done.3
  90.1 0.1 fusion.4
  90.3 0.2 fusion.3
  90.5 0.0 copy-done.2
  90.5 0.1 subtract_select_fusion
  90.6 0.0 copy-start.1
  90.6 0.0 copy-start.4
  90.6 0.9 multiply_reduce_fusion
  91.5 5.3 %collective-permute-start = (f32[16,64]{1,0:T(8,128)S(1)}, f32[16,64]{1,0:T(8,128)S(1)}, u32[]{:S(2)}, u32[]{:S(2)}) collective-permute-start(f32[16,64]{1,0:T(8,128)S(1)} %broadcast_multiply_fusion), channel_id=1, source_target_pairs={{0,0},{1,4},{2,1},{3,5},{4,2},{5,6},{6,3},{7,7},{8,8},{9,12},{10,9... | collective-permute-start | bytes 12296 | tf_op jit(solution)/shard_map/ppermute | solution.py:701
  96.9 1.1 fusion
  98.0 0.0 copy-done.1
  98.0 0.0 copy-done.4
  98.0 0.0 copy-start
  98.0 1.7 %fusion.1 = f32[2048,128,1]{1,0,2:T(8,128)S(1)} fusion(bf16[16,64,128]{2,1,0:T(8,128)(2,1)S(1)} %copy-done.1, f32[16,2048]{1,0:T(8,128)S(1)} %subtract_select_fusion, f32[16,64]{1,0:T(8,128)S(1)} %copy-done.4, u16[64,2048]{1,0:T(8,128)(2,1)S(1)} %fusion), kind=kOutput, calls=%fused_computation.6 | convolution fusion | flops 551550976 | bytes 1708032 | tf_op jit(solution)/shard_map/ijs,ijd->sd/dot_general | solution.py:698
  99.7 0.0 copy-done
  99.7 42.4 %give_back.1 = f32[8,64,128]{2,1,0:T(8,128)S(1)} custom-call(s32[4,8,128]{2,1,0:T(8,128)S(1)} %copy-done, s32[4,8,128]{2,1,0:T(8,128)S(1)} %copy-done, f32[32,64,128]{2,1,0:T(8,128)S(1)} %bitcast.15), custom_call_target="tpu_custom_call" | custom-call | tf_op jit(solution)/shard_map/give_back/pallas_call | solution.py:624
  142.1 0.0 collective-permute-done
  142.1 0.7 copy.13
  142.8 0.6 copy.14
  (1 shorter events, 0.0 us)
Async XLA Ops:
  87.7 2.5 %copy-start.3 = (f32[16,2048]{1,0:T(8,128)S(1)}, f32[16,2048]{1,0:T(8,128)}, u32[]{:S(2)}) copy-start(f32[16,2048]{1,0:T(8,128)} %get-tuple-element.11) | copy-start | bytes 393220
  87.7 2.8 %copy-start.2 = (f32[16,2048]{1,0:T(8,128)S(1)}, f32[16,2048]{1,0:T(8,128)}, u32[]{:S(2)}) copy-start(f32[16,2048]{1,0:T(8,128)} %get-tuple-element.13) | copy-start | bytes 393220
  90.6 7.3 %copy-start.1 = (bf16[16,64,128]{2,1,0:T(8,128)(2,1)S(1)}, bf16[16,64,128]{2,1,0:T(8,128)(2,1)}, u32[]{:S(2)}) copy-start(bf16[16,64,128]{2,1,0:T(8,128)(2,1)} %get-tuple-element.9) | copy-start | bytes 786436
  90.6 7.3 %copy-start.4 = (f32[16,64]{1,0:T(8,128)S(1)}, f32[16,64]{1,0:T(8,128)}, u32[]{:S(2)}) copy-start(f32[16,64]{1,0:T(8,128)} %get-tuple-element.12) | copy-start | bytes 12292
  91.5 50.6 %collective-permute-start = (f32[16,64]{1,0:T(8,128)S(1)}, f32[16,64]{1,0:T(8,128)S(1)}, u32[]{:S(2)}, u32[]{:S(2)}) collective-permute-start(f32[16,64]{1,0:T(8,128)S(1)} %broadcast_multiply_fusion), channel_id=1, source_target_pairs={{0,0},{1,4},{2,1},{3,5},{4,2},{5,6},{6,3},{7,7},{8,8},{9,12},{10,9... | collective-permute-start | bytes 12296 | tf_op jit(solution)/shard_map/ppermute | solution.py:701
  98.0 1.7 %copy-start = (s32[4,8,128]{2,1,0:T(8,128)S(1)}, s32[4,8,128]{2,1,0:T(8,128)}, u32[]{:S(2)}) copy-start(s32[4,8,128]{2,1,0:T(8,128)} %get-tuple-element.8.tabs_ref.ids_ref) | copy-start | bytes 49156

commit v6 on v5

--- a/solution.py
+++ b/solution.py
@@ -47,9 +47,9 @@
 
 def attend_kernel(
     zs, ys, scale, heads_total,
-    picked_ref, position_ref, cache_ref, index_ref, raw_ref, up_ref, iq_ref, iw_ref,
+    picked_ref, position_ref, cache_ref, index_ref, raw_hbm, up_hbm, iq_ref, iw_ref,
     target_ref, index_keys_ref, tabs_ref, mask_ref, my_iq_ref, my_iw_ref,
-    tabs_v, tabs_s, slots_v, slots_s, own_ref, q_ref, bias_ref, z_low, z_high, x_out, x_in, x_all, keys, query, query_out,
+    raw_ref, up_ref, load_sem, tabs_v, tabs_s, slots_v, slots_s, own_ref, q_ref, bias_ref, z_low, z_high, x_out, x_in, x_all, keys, query, query_out,
     logits_a, logits_b, expo, top, total, part, t_in,
     zs_sem, zr_sem, xs_sem, xr_sem, ts_sem, tr_sem, ys_sem, yr_sem, is_sem, ir_sem, qs_sem, qr_sem, ps_sem, pr_sem, ms_sem, mr_sem, local_sem,
 ):
@@ -79,6 +79,13 @@
             if dx or dc:
                 tx, tc = lax.rem(x + dx, X), lax.rem(c + dc, CORES)
                 x_peers.append((dx, dc, tx, tc, (z * X + tx, y * CORES + tc)))
+    loads = [
+        pltpu.make_async_copy(raw_hbm, raw_ref, load_sem.at[0]),
+        pltpu.make_async_copy(up_hbm, up_ref, load_sem.at[1]),
+    ]
+    for load in loads:
+        load.start()
+
     row_to = lax.rem(head, ys) * CORES + head // ys
     row_from = c * ys + y
     moves = row_to != head
@@ -291,6 +298,9 @@
     started = forwarded = 0
     made = 0
     for hop in range(1, hops + 1):
+        if hop == 1:
+            for load in loads:
+                load.wait()
         while made * hops < local_heads * hop:
             make_query(made)
             made += 1
@@ -458,9 +468,15 @@
             jax.ShapeDtypeStruct(index_query.shape, index_query.dtype),
             jax.ShapeDtypeStruct(index_weight.shape, index_weight.dtype),
         ),
-        in_specs=[pl.BlockSpec(memory_space=pltpu.SMEM)] * 2 + [pl.BlockSpec(memory_space=pltpu.VMEM)] * 6,
+        in_specs=[pl.BlockSpec(memory_space=pltpu.SMEM)] * 2
+        + [pl.BlockSpec(memory_space=pltpu.VMEM)] * 2
+        + [pl.BlockSpec(memory_space=pl.ANY)] * 2
+        + [pl.BlockSpec(memory_space=pltpu.VMEM)] * 2,
         out_specs=[pl.BlockSpec(memory_space=pltpu.VMEM)] * 6,
         scratch_shapes=[
+            pltpu.VMEM(queries.shape, keep),
+            pltpu.VMEM(up_weight.shape, keep),
+            dma((2,)),
             pltpu.VMEM((X, 8, LANES), jnp.int32),
             pltpu.SMEM((X, 8, LANES), jnp.int32),
             pltpu.VMEM((picks, LANES), jnp.int32),
@@ -497,9 +513,9 @@
 
 
 def return_kernel(
-    zs, ys, tabs_ref, ids_ref, part_ref, out_ref,
+    zs, ys, tabs_ref, ids_ref, part_ref, weight_ref, out_ref, home_ref,
     y_out, y_in, quarter, x_out, x_in, z_out, z_in, id_out, id_in, mine, theirs,
-    is_sem, ir_sem, ys_sem, yr_sem, xs_sem, xr_sem, zs_sem, zr_sem, cs_sem, cr_sem, os_sem, or_sem,
+    ws_sem, wr_sem, is_sem, ir_sem, ys_sem, yr_sem, xs_sem, xr_sem, zs_sem, zr_sem, cs_sem, cr_sem, os_sem, or_sem,
 ):
     ctx = lax.axis_index("ctx")
     z, x = ctx // X, ctx % X
@@ -512,7 +528,20 @@
     to_core = (ctx, y * CORES + 1 - c)
     x_peers = [(lax.rem(x + d, X), (z * X + lax.rem(x + d, X), head)) for d in range(1, X)]
     z_peers = [(lax.rem(z + d, zs), (lax.rem(z + d, zs) * X + x, head)) for d in range(1, zs)]
-    enter([to_a, to_b, to_far, to_core] + [p[1] for p in x_peers] + [p[1] for p in z_peers])
+    home = c * ys + y
+    comes_from = lax.rem(head, ys) * CORES + head // ys
+    moves = home != head
+    barrier = pltpu.get_barrier_semaphore()
+
+    @pl.when(moves)
+    def greet_movers():
+        for other in (home, comes_from):
+            pl.semaphore_signal(barrier, inc=1, device_id=(ctx, other), device_id_type=MESH)
+
+    enter(
+        [to_a, to_b, to_far, to_core] + [p[1] for p in x_peers] + [p[1] for p in z_peers],
+        2 * moves.astype(jnp.int32),
+    )
 
     def span(k):
         return pl.ds(pl.multiple_of(k * rows, rows), rows)
@@ -534,6 +563,16 @@
         copy = remote(y_out.at[n], y_in.at[n], ys_sem.at[n], yr_sem.at[n], device)
         copy.start()
         y_copies.append(copy)
+    weight_copy = remote(weight_ref, home_ref, ws_sem, wr_sem, (ctx, home))
+
+    @pl.when(moves)
+    def move():
+        weight_copy.start()
+
+    @pl.when(jnp.logical_not(moves))
+    def stay():
+        home_ref[...] = weight_ref[...]
+
     for d in order:
         copy = remote(id_out, id_in.at[z], is_sem.at[d - 1], ir_sem.at[d - 1], z_peers[d - 1][1])
         copy.start()
@@ -612,24 +651,33 @@
     for n, fy in enumerate((y_b, y_a, y_far)):
         ref = out_ref.at[:, span(fy), :]
         remote(ref, ref, os_sem.at[n], or_sem.at[n], to_a).wait_recv()
+    @pl.when(moves)
+    def moved():
+        weight_copy.wait_send()
+        weight_copy.wait_recv()
+
     for copy in y_copies + [core] + x_copies + z_copies + o_copies:
         copy.wait_send()
 
 
-def give_back(tables, key_part, zs, ys, own_blocks):
+def give_back(tables, key_part, weight_part, zs, ys, own_blocks):
     picks, block_len, width = key_part.shape
     rows = block_len // ys
     half = jnp.bfloat16
     dma = pltpu.SemaphoreType.DMA
     return pl.pallas_call(
         functools.partial(return_kernel, zs, ys),
-        out_shape=jax.ShapeDtypeStruct((own_blocks, block_len, width), jnp.float32),
+        out_shape=(
+            jax.ShapeDtypeStruct((own_blocks, block_len, width), jnp.float32),
+            jax.ShapeDtypeStruct(weight_part.shape, jnp.float32),
+        ),
         in_specs=[
             pl.BlockSpec(memory_space=pltpu.SMEM),
             pl.BlockSpec(memory_space=pltpu.VMEM),
             pl.BlockSpec(memory_space=pltpu.VMEM),
+            pl.BlockSpec(memory_space=pltpu.VMEM),
         ],
-        out_specs=pl.BlockSpec(memory_space=pltpu.VMEM),
+        out_specs=[pl.BlockSpec(memory_space=pltpu.VMEM)] * 2,
         scratch_shapes=[
             pltpu.VMEM((3, picks, rows, width), half),
             pltpu.VMEM((3, picks, rows, width), half),
@@ -642,7 +690,7 @@
             pltpu.VMEM((zs, 8, LANES), jnp.int32),
             pltpu.VMEM((own_blocks, rows, width), jnp.float32),
             pltpu.VMEM((own_blocks, rows, width), jnp.float32),
-            dma((zs - 1,)), dma((zs - 1,)),
+            dma, dma, dma((zs - 1,)), dma((zs - 1,)),
             dma((3,)), dma((3,)), dma((X - 1,)), dma((X - 1,)), dma((zs - 1,)), dma((zs - 1,)),
             dma, dma, dma((3,)), dma((3,)),
         ],
@@ -650,7 +698,7 @@
             collective_id=2, has_side_effects=True, vmem_limit_bytes=40 * 2**20
         ),
         name="give_back",
-    )(tables, tables, key_part)
+    )(tables, tables, key_part, weight_part)
 
 
 def masked_softmax(values, allowed):
@@ -683,7 +731,6 @@
         picked_blocks, block_position, cache_entry[:, 0], index_key[:, 0], jnp.transpose(queries, (1, 2, 0)), up_weight,
         index_query, index_weight, zs, ys, local_heads * head_devices,
     )
-    to_row = [((i % CORES) * ys + i // CORES, i) for i in range(head_devices)]
     index_keys = index_keys.reshape(key_count, index_width)
     my_allowed = mask == 0.0
     raw = jnp.einsum("ijd,sd->ijs", my_index_query, index_keys, preferred_element_type=jnp.float32)
@@ -698,11 +745,10 @@
     key_part = jnp.einsum(
         "ijs,ijd->sd", coefficient, my_index_query, preferred_element_type=jnp.float32
     )
-    weight_grad = lax.ppermute(weight_part, "head", [(b, a) for a, b in to_row])
-
-    key_grad = give_back(
-        tables, key_part.reshape(picks, block_len, index_width), zs, ys, own_blocks
-    ).reshape(own_blocks, 1, block_len, index_width)
+    key_grad, weight_grad = give_back(
+        tables, key_part.reshape(picks, block_len, index_width), weight_part, zs, ys, own_blocks
+    )
+    key_grad = key_grad.reshape(own_blocks, 1, block_len, index_width)
     return (key_grad, weight_grad)
 
 

time: 144 us -> 138 us (0.958)
  starting transfers between devices: 5.31 us -> 0 us
    ppermute x1 -> x0, starting transfers between devices: 5.31 us -> none  [local(): weight_grad = lax.ppermute(weight_part, 'head', [(b, a) for a, b in to_row])]
  transfers between devices with their start and end apart: 1 -> 0, of which waited for: 0 -> 0; matrix products, arithmetic and copies ran while one was open for 2% -> 0% of each run, Pallas kernels for 30% -> 0%
where the time goes in v6:
time: 138 us; the launch traced here: 137 us
  Pallas kernels  129 us (93%)
  matrix products  4.13 us (3%)
  other arithmetic  2.46 us (2%)
    pallas_call x1, Pallas kernels, attend(): pl.pallas_call(functools.partial(attend_kernel, zs, ys, scale, heads_tota...  86 us
    pallas_call x1, Pallas kernels, give_back(): pl.pallas_call(functools.partial(return_kernel, zs, ys), out_shape=(jax.S...  42.7 us

profile of v6, /device:TPU:1, one launch (start us, length us, event | category | flops | bytes accessed | tf_op | source)
XLA Modules:
  0.0 137.4 jit_solution(9160059459326743436)
XLA Ops:
  0.6 86.0 %attend.1 = (f32[16,2048]{1,0:T(8,128)}, bf16[32,64,128]{2,1,0:T(8,128)(2,1)}, s32[4,8,128]{2,1,0:T(8,128)}, f32[16,2048]{1,0:T(8,128)}, bf16[16,64,128]{2,1,0:T(8,128)(2,1)}, /*index=5*/f32[16,64]{1,0:T(8,128)}) custom-call(s32[2,32]{1,0:T(2,128)} %picked_ref.1, s32[2]{0:T(128)} %position_ref.1, bf16[8,64,576]{2,1,0:T(8,128)(2,1)} %bitcast.18, ...), custom_call_target="tpu_custom_call" | custom-call | tf_op jit(solution)/shard_map/attend/pallas_call | solution.py:461
  86.7 0.0 copy-start.3
  86.7 0.0 copy-start.2
  86.7 2.4 %multiply_reduce_fusion.1 = (f32[16,2048]{1,0:T(8,128)S(1)}, f32[16,64,2048]{2,1,0:T(8,128)S(1)}) fusion(f32[16,64]{1,0:T(8,128)} %get-tuple-element.14, bf16[16,64,128]{2,1,0:T(8,128)(2,1)} %get-tuple-element.11, bf16[2048,128,1]{1,0,2:T(8,128)(2,1)} %bitcast.19), kind=kOutput, calls=%fused_computation.4 | convolution fusion | flops 543129600 | bytes 9310208 | tf_op jit(solution)/shard_map/ijd,sd->ijs/dot_general | solution.py:736
  89.1 0.0 copy-done.3
  89.1 0.1 fusion.4
  89.3 0.2 fusion.3
  89.5 0.0 copy-done.2
  89.5 0.1 subtract_select_fusion
  89.6 0.0 copy-start.1
  89.6 0.0 copy-start.4
  89.6 0.9 multiply_reduce_fusion
  90.5 1.1 fusion
  91.6 0.0 copy-done.1
  91.7 0.0 copy-done.4
  91.7 0.0 copy-start
  91.7 1.7 %fusion.1 = f32[2048,128,1]{1,0,2:T(8,128)S(1)} fusion(bf16[16,64,128]{2,1,0:T(8,128)(2,1)S(1)} %copy-done.1, f32[16,2048]{1,0:T(8,128)S(1)} %subtract_select_fusion, f32[16,64]{1,0:T(8,128)S(1)} %copy-done.4, u16[64,2048]{1,0:T(8,128)(2,1)S(1)} %fusion), kind=kOutput, calls=%fused_computation.6 | convolution fusion | flops 551550976 | bytes 1708032 | tf_op jit(solution)/shard_map/ijs,ijd->sd/dot_general | solution.py:745
  93.4 0.0 copy-done
  93.4 42.7 %give_back.1 = (f32[8,64,128]{2,1,0:T(8,128)S(1)}, f32[16,64]{1,0:T(8,128)S(1)}) custom-call(s32[4,8,128]{2,1,0:T(8,128)S(1)} %copy-done, s32[4,8,128]{2,1,0:T(8,128)S(1)} %copy-done, f32[32,64,128]{2,1,0:T(8,128)S(1)} %bitcast.15, f32[16,64]{1,0:T(8,128)S(1)} %broadcast_multiply_fusion.weight_ref), custom_call_target="tpu_custom_call" | custom-call | tf_op jit(solution)/shard_map/give_back/pallas_call | solution.py:668
  136.1 0.7 copy.13
  136.8 0.6 copy.14
  (1 shorter events, 0.0 us)
Async XLA Ops:
  86.7 2.5 %copy-start.3 = (f32[16,2048]{1,0:T(8,128)S(1)}, f32[16,2048]{1,0:T(8,128)}, u32[]{:S(2)}) copy-start(f32[16,2048]{1,0:T(8,128)} %get-tuple-element.13) | copy-start | bytes 393220
  86.7 2.8 %copy-start.2 = (f32[16,2048]{1,0:T(8,128)S(1)}, f32[16,2048]{1,0:T(8,128)}, u32[]{:S(2)}) copy-start(f32[16,2048]{1,0:T(8,128)} %get-tuple-element.15) | copy-start | bytes 393220
  89.6 2.0 %copy-start.1 = (bf16[16,64,128]{2,1,0:T(8,128)(2,1)S(1)}, bf16[16,64,128]{2,1,0:T(8,128)(2,1)}, u32[]{:S(2)}) copy-start(bf16[16,64,128]{2,1,0:T(8,128)(2,1)} %get-tuple-element.11) | copy-start | bytes 786436
  89.6 2.0 %copy-start.4 = (f32[16,64]{1,0:T(8,128)S(1)}, f32[16,64]{1,0:T(8,128)}, u32[]{:S(2)}) copy-start(f32[16,64]{1,0:T(8,128)} %get-tuple-element.14) | copy-start | bytes 12292
  91.7 1.7 %copy-start = (s32[4,8,128]{2,1,0:T(8,128)S(1)}, s32[4,8,128]{2,1,0:T(8,128)}, u32[]{:S(2)}) copy-start(s32[4,8,128]{2,1,0:T(8,128)} %get-tuple-element.10.tabs_ref.ids_ref) | copy-start | bytes 49156

commit v7 on v6

--- a/solution.py
+++ b/solution.py
@@ -11,6 +11,7 @@
 X = 4
 CORES = 2
 LANES = 128
+DIRECT = 3
 JUMP = 1
 
 
@@ -210,6 +211,7 @@
 
     chunks = ys_sem.shape[1]
     chunk = picks // chunks
+    straight = chunks - DIRECT
 
     def y_copy(kind, owner, j, device):
         here = pl.ds(pl.multiple_of(owner * rows, rows), rows)
@@ -231,7 +233,7 @@
         lax.fori_loop(j * chunk, (j + 1) * chunk, place, 0)
         start(y_copy(0, y, j, to_a))
         start(y_copy(1, y, j, to_b))
-        if j == chunks - 1:
+        if j >= straight:
             start(y_copy(2, y, j, to_far))
 
     def y_forward(j):
@@ -325,7 +327,7 @@
         while started < ready:
             y_start(started)
             started += 1
-        while forwarded < before:
+        while forwarded < min(before, straight):
             y_forward(forwarded)
             forwarded += 1
     x_finish(hops)
@@ -333,7 +335,7 @@
     while started < chunks:
         y_start(started)
         started += 1
-    while forwarded < before:
+    while forwarded < min(before, straight):
         y_forward(forwarded)
         forwarded += 1
     start(index_copy(0, y, to_a))
@@ -370,13 +372,15 @@
                 total[j, at, :] = functools.reduce(jnp.add, raised)
 
     def attend_chunk(j, carry):
-        @pl.when(j == parts - 1)
-        def last_chunk():
-            y_copy(0, y_b, chunks - 1, to_a).wait_recv()
-
         for i in range(chunks // parts):
-            y_copy(1, y_a, j * (chunks // parts) + i, to_a).wait_recv()
-            y_copy(2, y_far, j * (chunks // parts) + i, to_a).wait_recv()
+            here = j * (chunks // parts) + i
+
+            @pl.when(here >= straight)
+            def not_forwarded():
+                y_copy(0, y_b, here, to_a).wait_recv()
+
+            y_copy(1, y_a, here, to_a).wait_recv()
+            y_copy(2, y_far, here, to_a).wait_recv()
         dot(j, 0, logits_a)
 
         for p in range(groups // 2):

time: 138 us -> 140 us (1.014)
  Pallas kernels: 129 us -> 132 us
    pallas_call x1, Pallas kernels: 86 us -> 87.5 us  [attend(): pl.pallas_call(functools.partial(attend_kernel, zs, ys, scale, heads_tota...]
where the time goes in v7:
time: 140 us
  Pallas kernels  132 us (94%)
  matrix products  4.13 us (3%)
  other arithmetic  2.46 us (2%)
    pallas_call x1, Pallas kernels, attend(): pl.pallas_call(functools.partial(attend_kernel, zs, ys, scale, heads_tota...  87.5 us
    pallas_call x1, Pallas kernels, give_back(): pl.pallas_call(functools.partial(return_kernel, zs, ys), out_shape=(jax.S...  44.1 us

profile of v7, /device:TPU:1, one launch (start us, length us, event | category | flops | bytes accessed | tf_op | source)
XLA Modules:
  0.0 140.2 jit_solution(5687138540919380930)
XLA Ops:
  0.6 87.5 %attend.1 = (f32[16,2048]{1,0:T(8,128)}, bf16[32,64,128]{2,1,0:T(8,128)(2,1)}, s32[4,8,128]{2,1,0:T(8,128)}, f32[16,2048]{1,0:T(8,128)}, bf16[16,64,128]{2,1,0:T(8,128)(2,1)}, /*index=5*/f32[16,64]{1,0:T(8,128)}) custom-call(s32[2,32]{1,0:T(2,128)} %picked_ref.1, s32[2]{0:T(128)} %position_ref.1, bf16[8,64,576]{2,1,0:T(8,128)(2,1)} %bitcast.18, ...), custom_call_target="tpu_custom_call" | custom-call | tf_op jit(solution)/shard_map/attend/pallas_call | solution.py:465
  88.1 0.0 copy-start.3
  88.1 0.0 copy-start.2
  88.1 2.4 %multiply_reduce_fusion.1 = (f32[16,2048]{1,0:T(8,128)S(1)}, f32[16,64,2048]{2,1,0:T(8,128)S(1)}) fusion(f32[16,64]{1,0:T(8,128)} %get-tuple-element.14, bf16[16,64,128]{2,1,0:T(8,128)(2,1)} %get-tuple-element.11, bf16[2048,128,1]{1,0,2:T(8,128)(2,1)} %bitcast.19), kind=kOutput, calls=%fused_computation.4 | convolution fusion | flops 543129600 | bytes 9310208 | tf_op jit(solution)/shard_map/ijd,sd->ijs/dot_general | solution.py:740
  90.6 0.0 copy-done.3
  90.6 0.1 fusion.4
  90.7 0.2 fusion.3
  90.9 0.0 copy-done.2
  90.9 0.1 subtract_select_fusion
  91.0 0.0 copy-start.1
  91.1 0.0 copy-start.4
  91.1 0.9 multiply_reduce_fusion
  92.0 1.1 fusion
  93.1 0.0 copy-done.1
  93.1 0.0 copy-done.4
  93.1 0.0 copy-start
  93.1 1.7 %fusion.1 = f32[2048,128,1]{1,0,2:T(8,128)S(1)} fusion(bf16[16,64,128]{2,1,0:T(8,128)(2,1)S(1)} %copy-done.1, f32[16,2048]{1,0:T(8,128)S(1)} %subtract_select_fusion, f32[16,64]{1,0:T(8,128)S(1)} %copy-done.4, u16[64,2048]{1,0:T(8,128)(2,1)S(1)} %fusion), kind=kOutput, calls=%fused_computation.6 | convolution fusion | flops 551550976 | bytes 1708032 | tf_op jit(solution)/shard_map/ijs,ijd->sd/dot_general | solution.py:749
  94.8 0.0 copy-done
  94.8 44.1 %give_back.1 = (f32[8,64,128]{2,1,0:T(8,128)S(1)}, f32[16,64]{1,0:T(8,128)S(1)}) custom-call(s32[4,8,128]{2,1,0:T(8,128)S(1)} %copy-done, s32[4,8,128]{2,1,0:T(8,128)S(1)} %copy-done, f32[32,64,128]{2,1,0:T(8,128)S(1)} %bitcast.15, f32[16,64]{1,0:T(8,128)S(1)} %broadcast_multiply_fusion.weight_ref), custom_call_target="tpu_custom_call" | custom-call | tf_op jit(solution)/shard_map/give_back/pallas_call | solution.py:672
  138.9 0.7 copy.13
  139.6 0.6 copy.14
  (1 shorter events, 0.0 us)
Async XLA Ops:
  88.1 2.5 %copy-start.3 = (f32[16,2048]{1,0:T(8,128)S(1)}, f32[16,2048]{1,0:T(8,128)}, u32[]{:S(2)}) copy-start(f32[16,2048]{1,0:T(8,128)} %get-tuple-element.13) | copy-start | bytes 393220
  88.1 2.8 %copy-start.2 = (f32[16,2048]{1,0:T(8,128)S(1)}, f32[16,2048]{1,0:T(8,128)}, u32[]{:S(2)}) copy-start(f32[16,2048]{1,0:T(8,128)} %get-tuple-element.15) | copy-start | bytes 393220
  91.0 2.0 %copy-start.1 = (bf16[16,64,128]{2,1,0:T(8,128)(2,1)S(1)}, bf16[16,64,128]{2,1,0:T(8,128)(2,1)}, u32[]{:S(2)}) copy-start(bf16[16,64,128]{2,1,0:T(8,128)(2,1)} %get-tuple-element.11) | copy-start | bytes 786436
  91.1 2.0 %copy-start.4 = (f32[16,64]{1,0:T(8,128)S(1)}, f32[16,64]{1,0:T(8,128)}, u32[]{:S(2)}) copy-start(f32[16,64]{1,0:T(8,128)} %get-tuple-element.14) | copy-start | bytes 12292
  93.1 1.7 %copy-start = (s32[4,8,128]{2,1,0:T(8,128)S(1)}, s32[4,8,128]{2,1,0:T(8,128)}, u32[]{:S(2)}) copy-start(s32[4,8,128]{2,1,0:T(8,128)} %get-tuple-element.10.tabs_ref.ids_ref) | copy-start | bytes 49156

commit v8 on v6

--- a/solution.py
+++ b/solution.py
@@ -295,7 +295,7 @@
     swap = remote(query_out, query.at[pl.ds(local_heads, local_heads)], qs_sem, qr_sem, to_core)
     hops = len(plan)
     arrived = X
-    started = forwarded = 0
+    started = forwarded = before = 0
     made = 0
     for hop in range(1, hops + 1):
         if hop == 1:
@@ -319,17 +319,16 @@
         if hop == 1:
             prepare()
         x_finish(hop - 1)
-        before = started
+        settled, before = before, started
         ready = max(0, picks - (shards - arrived)) // chunk
         arrived += X * len(sources(hop))
         while started < ready:
             y_start(started)
             started += 1
-        while forwarded < before:
+        while forwarded < settled:
             y_forward(forwarded)
             forwarded += 1
     x_finish(hops)
-    before = started
     while started < chunks:
         y_start(started)
         started += 1
@@ -370,6 +369,12 @@
                 total[j, at, :] = functools.reduce(jnp.add, raised)
 
     def attend_chunk(j, carry):
+        @pl.when(j == 1)
+        def forward_rest():
+            for late in range(forwarded, chunks - 1):
+                y_copy(0, y_b, late, to_a).wait_recv()
+                y_copy(2, y_b, late, to_a).start()
+
         @pl.when(j == parts - 1)
         def last_chunk():
             y_copy(0, y_b, chunks - 1, to_a).wait_recv()
@@ -433,6 +438,8 @@
             copy.wait_recv()
 
     my_iw_ref[...] = my_iw_ref[...] * index_ref.shape[2] ** (-0.5)
+    for late in range(forwarded, chunks - 1):
+        y_copy(2, y_b, late, to_a).wait_send()
     for copy in pending:
         copy.wait_send()
 

time: 138 us -> 142 us (1.029)
  Pallas kernels: 129 us -> 133 us
    pallas_call x1, Pallas kernels: 86 us -> 90.1 us  [attend(): pl.pallas_call(functools.partial(attend_kernel, zs, ys, scale, heads_tota...]
where the time goes in v8:
time: 142 us
  Pallas kernels  133 us (94%)
  matrix products  4.13 us (3%)
  other arithmetic  2.46 us (2%)
    pallas_call x1, Pallas kernels, attend(): pl.pallas_call(functools.partial(attend_kernel, zs, ys, scale, heads_tota...  90.1 us
    pallas_call x1, Pallas kernels, give_back(): pl.pallas_call(functools.partial(return_kernel, zs, ys), out_shape=(jax.S...  43.3 us

profile of v8, /device:TPU:1, one launch (start us, length us, event | category | flops | bytes accessed | tf_op | source)
XLA Modules:
  0.0 142.0 jit_solution(14555802995389159679)
XLA Ops:
  0.6 90.1 %attend.1 = (f32[16,2048]{1,0:T(8,128)}, bf16[32,64,128]{2,1,0:T(8,128)(2,1)}, s32[4,8,128]{2,1,0:T(8,128)}, f32[16,2048]{1,0:T(8,128)}, bf16[16,64,128]{2,1,0:T(8,128)(2,1)}, /*index=5*/f32[16,64]{1,0:T(8,128)}) custom-call(s32[2,32]{1,0:T(2,128)} %picked_ref.1, s32[2]{0:T(128)} %position_ref.1, bf16[8,64,576]{2,1,0:T(8,128)(2,1)} %bitcast.18, ...), custom_call_target="tpu_custom_call" | custom-call | tf_op jit(solution)/shard_map/attend/pallas_call | solution.py:468
  90.7 0.0 copy-start.3
  90.7 0.0 copy-start.2
  90.7 2.4 %multiply_reduce_fusion.1 = (f32[16,2048]{1,0:T(8,128)S(1)}, f32[16,64,2048]{2,1,0:T(8,128)S(1)}) fusion(f32[16,64]{1,0:T(8,128)} %get-tuple-element.14, bf16[16,64,128]{2,1,0:T(8,128)(2,1)} %get-tuple-element.11, bf16[2048,128,1]{1,0,2:T(8,128)(2,1)} %bitcast.19), kind=kOutput, calls=%fused_computation.4 | convolution fusion | flops 543129600 | bytes 9310208 | tf_op jit(solution)/shard_map/ijd,sd->ijs/dot_general | solution.py:743
  93.2 0.0 copy-done.3
  93.2 0.1 fusion.4
  93.3 0.2 fusion.3
  93.5 0.0 copy-done.2
  93.5 0.1 subtract_select_fusion
  93.6 0.0 copy-start.1
  93.6 0.0 copy-start.4
  93.7 0.9 multiply_reduce_fusion
  94.6 1.1 fusion
  95.7 0.0 copy-done.1
  95.7 0.0 copy-done.4
  95.7 0.0 copy-start
  95.7 1.7 %fusion.1 = f32[2048,128,1]{1,0,2:T(8,128)S(1)} fusion(bf16[16,64,128]{2,1,0:T(8,128)(2,1)S(1)} %copy-done.1, f32[16,2048]{1,0:T(8,128)S(1)} %subtract_select_fusion, f32[16,64]{1,0:T(8,128)S(1)} %copy-done.4, u16[64,2048]{1,0:T(8,128)(2,1)S(1)} %fusion), kind=kOutput, calls=%fused_computation.6 | convolution fusion | flops 551550976 | bytes 1708032 | tf_op jit(solution)/shard_map/ijs,ijd->sd/dot_general | solution.py:752
  97.4 0.0 copy-done
  97.4 43.3 %give_back.1 = (f32[8,64,128]{2,1,0:T(8,128)S(1)}, f32[16,64]{1,0:T(8,128)S(1)}) custom-call(s32[4,8,128]{2,1,0:T(8,128)S(1)} %copy-done, s32[4,8,128]{2,1,0:T(8,128)S(1)} %copy-done, f32[32,64,128]{2,1,0:T(8,128)S(1)} %bitcast.15, f32[16,64]{1,0:T(8,128)S(1)} %broadcast_multiply_fusion.weight_ref), custom_call_target="tpu_custom_call" | custom-call | tf_op jit(solution)/shard_map/give_back/pallas_call | solution.py:675
  140.7 0.7 copy.13
  141.4 0.6 copy.14
  (1 shorter events, 0.0 us)
Async XLA Ops:
  90.7 2.5 %copy-start.3 = (f32[16,2048]{1,0:T(8,128)S(1)}, f32[16,2048]{1,0:T(8,128)}, u32[]{:S(2)}) copy-start(f32[16,2048]{1,0:T(8,128)} %get-tuple-element.13) | copy-start | bytes 393220
  90.7 2.8 %copy-start.2 = (f32[16,2048]{1,0:T(8,128)S(1)}, f32[16,2048]{1,0:T(8,128)}, u32[]{:S(2)}) copy-start(f32[16,2048]{1,0:T(8,128)} %get-tuple-element.15) | copy-start | bytes 393220
  93.6 2.0 %copy-start.1 = (bf16[16,64,128]{2,1,0:T(8,128)(2,1)S(1)}, bf16[16,64,128]{2,1,0:T(8,128)(2,1)}, u32[]{:S(2)}) copy-start(bf16[16,64,128]{2,1,0:T(8,128)(2,1)} %get-tuple-element.11) | copy-start | bytes 786436
  93.6 2.0 %copy-start.4 = (f32[16,64]{1,0:T(8,128)S(1)}, f32[16,64]{1,0:T(8,128)}, u32[]{:S(2)}) copy-start(f32[16,64]{1,0:T(8,128)} %get-tuple-element.14) | copy-start | bytes 12292
  95.7 1.7 %copy-start = (s32[4,8,128]{2,1,0:T(8,128)S(1)}, s32[4,8,128]{2,1,0:T(8,128)}, u32[]{:S(2)}) copy-start(s32[4,8,128]{2,1,0:T(8,128)} %get-tuple-element.10.tabs_ref.ids_ref) | copy-start | bytes 49156
